TPU v7x, 32 devices: a whole 2x2x4 slice. The times are simulated.
32 devices in a mesh: dp: 8 (over z, x), tensor: 4 (over y, core).
Axes of the slice: x: 2, y: 2, z: 4, core: 2. Of those that a mesh axis runs over, the one named last changes fastest.
Arguments:
- tokens: bfloat16 [32768, 1024], P(('dp', 'tensor')), may hold values from -6 to 6
- doc_starts: int32 [16, 4], P('dp'), may hold values from 0 to 2047, as said below
- norm_gains: bfloat16 [2, 2, 1024], replicated, may hold values from 0.5 to 1.5
- norm_shifts: bfloat16 [2, 2, 1024], replicated, may hold values from -1.1953125 to 1.1953125
- qkv_weight: bfloat16 [2, 1024, 3072], P(None, None, 'tensor'), may hold values from -0.1875 to 0.1875
- qkv_bias: bfloat16 [2, 3072], P(None, 'tensor'), may hold values from -1.796875 to 1.796875
- dense_weight: bfloat16 [2, 1024, 1024], P(None, 'tensor'), may hold values from -1.5 to 1.5
- dense_bias: bfloat16 [2, 1024], replicated, may hold values from -1.796875 to 1.796875
- up_weight: bfloat16 [2, 1024, 4096], P(None, None, 'tensor'), may hold values from -0.1875 to 0.1875
- up_bias: bfloat16 [2, 4096], P(None, 'tensor'), may hold values from -3 to 3
- down_weight: bfloat16 [2, 4096, 1024], P(None, 'tensor'), may hold values from -0.09375 to 0.09375
- down_bias: bfloat16 [2, 1024], replicated, may hold values from -1.796875 to 1.796875
- out_grad: bfloat16 [32768, 1024], P(('dp', 'tensor')), may hold values from -6 to 6
Outputs:
- out: bfloat16 [32768, 1024], P(('dp', 'tensor'))
- tokens_grad: float32 [32768, 1024], P(('dp', 'tensor'))
- norm_gains_grad: float32 [2, 2, 1024], replicated
- norm_shifts_grad: float32 [2, 2, 1024], replicated
- qkv_weight_grad: float32 [2, 1024, 3072], P(None, None, 'tensor')
- qkv_bias_grad: float32 [2, 3072], P(None, 'tensor')
- dense_weight_grad: float32 [2, 1024, 1024], P(None, 'tensor')
- dense_bias_grad: float32 [2, 1024], replicated
- up_weight_grad: float32 [2, 1024, 4096], P(None, None, 'tensor')
- up_bias_grad: float32 [2, 4096], P(None, 'tensor')
- down_weight_grad: float32 [2, 4096, 1024], P(None, 'tensor')
- down_bias_grad: float32 [2, 1024], replicated
Inputs may be any that keep to these rules, and one draw needn't show every extreme that they name: `doc_starts`: each row holds the document starts of one packed sequence: the first is 0 and they never fall (equal starts leave empty documents). In each aligned block of 2 rows one row has its second start below 128, its last start at 2047 and the others from 1920 on; the other row's last start is 2047.
All inputs are finite; a program needn't handle non-finite values.
Results may differ from a plain program's by a relative error of at most 0.019.
Values may be sent and summed in bfloat16 or wider, within the bound.
No kernel may reach another device: no remote copies, remote signals or barrier semaphores. Data moves between devices by JAX's collectives and lax.ppermute only.
A program may use at most 448 MiB of HBM per device.

v0:
```python
from functools import partial
import math

import jax
import jax.numpy as jnp
from jax import lax
from jax.sharding import PartitionSpec as P

HS = 64
FEATS = 64
ROT = 16
BLOCK = 64


norm_eps = 1e-05
feature_scale = 0.75
rotary_base = 10000.0
highest = lax.Precision.HIGHEST


def rounded(operand):
    return operand + lax.stop_gradient(operand.astype(jnp.bfloat16).astype(jnp.float32) - operand)


def both_ways(operand):
    return operand.astype(jnp.bfloat16).astype(jnp.float32)


def grad_only(operand):
    coarse = both_ways(operand)
    return coarse + lax.stop_gradient(operand - coarse)


def normalize(matrix, scaling, offset):
    center = jnp.mean(matrix, axis=-1, keepdims=True)
    shifted = matrix - center
    spread = jnp.mean(shifted * shifted, axis=-1, keepdims=True)
    return shifted * lax.rsqrt(spread + norm_eps) * scaling + offset


def two_norms(matrix, gain_pair, shift_pair):
    return (
        normalize(matrix, gain_pair[0], shift_pair[0]),
        normalize(matrix, gain_pair[1], shift_pair[1]),
    )


def exact_gelu(hidden):
    return jax.nn.gelu(hidden, approximate=False)


def dct_rows(feature_count, head_width):
    row_index = jnp.arange(feature_count, dtype=jnp.float32)[:, None]
    col_index = jnp.arange(head_width, dtype=jnp.float32)[None, :]
    table = jnp.cos(math.pi * (col_index + 0.5) * row_index / head_width) * math.sqrt(
        2.0 / head_width
    )
    return table * jnp.where(row_index == 0, math.sqrt(0.5), 1.0)


def doc_layout(starts, length):
    places = jnp.arange(length, dtype=jnp.int32)
    started = starts[:, None, :] <= places[None, :, None]
    doc_ids = jnp.sum(started.astype(jnp.int32), axis=-1)
    latest = jnp.max(jnp.where(started, starts[:, None, :], 0), axis=-1)
    return (doc_ids, places[None, :] - latest)


def rotary_tables(offsets, rotary_dims):
    halfway = rotary_dims // 2
    inverse = rotary_base ** (-(jnp.arange(halfway, dtype=jnp.float32) * 2.0 / rotary_dims))
    angles = offsets.astype(jnp.float32)[..., None] * inverse
    return (jnp.cos(angles), jnp.sin(angles))


def rotate(vectors, cosine, sine_table, rotary_dims):
    halfway = rotary_dims // 2
    leading = vectors[..., :halfway]
    trailing = vectors[..., halfway:rotary_dims]
    return jnp.concatenate(
        [
            leading * cosine - trailing * sine_table,
            trailing * cosine + leading * sine_table,
            vectors[..., rotary_dims:],
        ],
        axis=-1,
    )


def attend_head(
    queries, keys_in, values_in, cosine, sine_table, doc_ids, dct_table, block_size, rotary_dims
):
    length = queries.shape[0]
    blocks = length // block_size
    turned_q = rotate(queries, cosine, sine_table, rotary_dims)
    turned_k = rotate(keys_in, cosine, sine_table, rotary_dims)
    query_feat = rounded(jnp.exp(feature_scale * jnp.dot(turned_q, dct_table.T, precision=highest)))
    key_feat = rounded(jnp.exp(feature_scale * jnp.dot(turned_k, dct_table.T, precision=highest)))
    value_low = rounded(values_in)
    query_blocks = query_feat.reshape(blocks, block_size, -1)
    key_blocks = key_feat.reshape(blocks, block_size, -1)
    value_blocks = value_low.reshape(blocks, block_size, -1)
    doc_blocks = doc_ids.reshape(blocks, block_size)
    lead_doc = doc_blocks[:, 0]
    next_doc = jnp.concatenate([lead_doc[1:], jnp.full((1,), -1, jnp.int32)])
    carried = (doc_blocks == lead_doc[:, None]).astype(jnp.float32)
    feeding = (doc_blocks == next_doc[:, None]).astype(jnp.float32)
    places = jnp.arange(block_size)
    causal = places[:, None] >= places[None, :]
    allowed = (causal[None] & (doc_blocks[:, :, None] == doc_blocks[:, None, :])).astype(
        jnp.float32
    )
    scores = jnp.einsum("bcm,bdm->bcd", query_blocks, key_blocks, precision=highest) * allowed
    inner_den = jnp.sum(scores, axis=-1)
    inner_num = jnp.einsum("bcd,bde->bce", both_ways(scores), value_blocks, precision=highest)
    fed_keys = key_blocks * feeding[..., None]
    state_add = jnp.einsum("bcm,bce->bme", fed_keys, value_blocks, precision=highest)
    total_add = jnp.sum(fed_keys, axis=1)
    block_index = jnp.arange(blocks)
    earlier = block_index[None, :] < block_index[:, None]
    linked = (earlier & (next_doc[None, :] == lead_doc[:, None])).astype(jnp.float32)
    states = jnp.einsum("cd,dme->cme", linked, state_add, precision=highest)
    totals = jnp.einsum("cd,dm->cm", linked, total_add, precision=highest)
    outer_num = (
        jnp.einsum("bcm,bme->bce", query_blocks, both_ways(states), precision=highest)
        * carried[..., None]
    )
    outer_den = jnp.einsum("bcm,bm->bc", query_blocks, totals, precision=highest) * carried
    numerator = (inner_num + outer_num).reshape(length, -1)
    denominator = (inner_den + outer_den).reshape(length, 1)
    return grad_only(numerator) / denominator


def attend_all(
    mixed, cosine, sine_table, doc_ids, dct_table, seq_count, head_size, block_size, rotary_dims
):
    length = mixed.shape[0] // seq_count
    packed = mixed.reshape(seq_count, length, -1, 3, head_size)
    per_head = partial(
        attend_head, dct_table=dct_table, block_size=block_size, rotary_dims=rotary_dims
    )
    over_heads = jax.vmap(per_head, in_axes=(1, 1, 1, None, None, None), out_axes=1)
    over_seqs = jax.vmap(over_heads)
    context = over_seqs(
        packed[:, :, :, 0], packed[:, :, :, 1], packed[:, :, :, 2], cosine, sine_table, doc_ids
    )
    return context.reshape(seq_count * length, -1)


def contract_rows(left, right):
    return lax.dot_general(
        left, right, (((0,), (0,)), ((), ())), preferred_element_type=jnp.float32
    )


def contract_cols(left, right):
    return lax.dot_general(
        left, right, (((1,), (1,)), ((), ())), preferred_element_type=jnp.float32
    )


def on_device(
    tokens,
    doc_starts,
    norm_gains,
    norm_shifts,
    qkv_weight,
    qkv_bias,
    dense_weight,
    dense_bias,
    up_weight,
    up_bias,
    down_weight,
    down_bias,
    out_grad,
):
    layer_count = qkv_weight.shape[0]
    row_count = tokens.shape[0]
    seq_count = doc_starts.shape[0]
    group_rows = row_count * lax.axis_size("tensor")
    length = group_rows // seq_count
    doc_ids, offsets = doc_layout(doc_starts, length)
    cosine, sine_table = rotary_tables(offsets, ROT)
    dct_table = dct_rows(FEATS, HS)
    gains = norm_gains.astype(jnp.float32)
    shifts = norm_shifts.astype(jnp.float32)
    attend_local = partial(
        attend_all,
        cosine=cosine,
        sine_table=sine_table,
        doc_ids=doc_ids,
        dct_table=dct_table,
        seq_count=seq_count,
        head_size=HS,
        block_size=BLOCK,
        rotary_dims=ROT,
    )
    residual = tokens.astype(jnp.float32)
    stored = []
    for layer_index in range(layer_count):
        whole_rows = None
        local_one = normalize(residual, gains[layer_index, 0], shifts[layer_index, 0]).astype(
            jnp.bfloat16
        )
        local_two = normalize(residual, gains[layer_index, 1], shifts[layer_index, 1]).astype(
            jnp.bfloat16
        )
        normed_one, normed_two = (
            lax.all_gather(local_one, "tensor", axis=0, tiled=True),
            lax.all_gather(local_two, "tensor", axis=0, tiled=True),
        )
        mixed = jnp.dot(
            normed_one, qkv_weight[layer_index], preferred_element_type=jnp.float32
        ) + qkv_bias[layer_index].astype(jnp.float32)
        context_full, attend_back = jax.vjp(attend_local, mixed)
        context = context_full.astype(jnp.bfloat16)
        hidden = jnp.dot(
            normed_two, up_weight[layer_index], preferred_element_type=jnp.float32
        ) + up_bias[layer_index].astype(jnp.float32)
        active_full, gelu_back = jax.vjp(exact_gelu, hidden)
        active = active_full.astype(jnp.bfloat16)
        dense_part = dense_weight[layer_index]
        down_part = down_weight[layer_index]
        summed = lax.psum_scatter(
            (
                jnp.dot(context, dense_part, preferred_element_type=jnp.float32)
                + jnp.dot(active, down_part, preferred_element_type=jnp.float32)
            ).astype(jnp.bfloat16),
            "tensor",
            scatter_dimension=0,
            tiled=True,
        ).astype(jnp.float32)
        branch = (
            summed
            + dense_bias[layer_index].astype(jnp.float32)
            + down_bias[layer_index].astype(jnp.float32)
        )
        stored.append(
            (residual, normed_one, normed_two, context, active, attend_back, gelu_back, whole_rows)
        )
        residual = residual + branch
        if layer_index + 1 < layer_count:
            residual = residual.astype(jnp.bfloat16).astype(jnp.float32)
    result = residual.astype(jnp.bfloat16)
    incoming = out_grad.astype(jnp.float32)
    layer_grads = [None] * layer_count
    gain_grads = [None] * layer_count
    shift_grads = [None] * layer_count
    bias_grads = [None] * layer_count
    for layer_index in reversed(range(layer_count)):
        layer_input, normed_one, normed_two, context, active, attend_back, gelu_back, whole_rows = (
            stored[layer_index]
        )
        branch_grad = incoming.astype(jnp.bfloat16)
        bias_grads[layer_index] = jnp.sum(branch_grad.astype(jnp.float32), axis=0)
        gathered_grad = lax.all_gather(branch_grad, "tensor", axis=0, tiled=True)
        context_grad = contract_cols(gathered_grad, dense_weight[layer_index])
        dense_grad = contract_rows(context, gathered_grad)
        active_grad = contract_cols(gathered_grad, down_weight[layer_index])
        down_grad = contract_rows(active, gathered_grad)
        hidden_grad = gelu_back(active_grad)[0].astype(jnp.bfloat16)
        up_grad = contract_rows(normed_two, hidden_grad)
        part_two = contract_cols(hidden_grad, up_weight[layer_index])
        mixed_grad = attend_back(context_grad)[0].astype(jnp.bfloat16)
        qkv_grad = contract_rows(normed_one, mixed_grad)
        part_one = contract_cols(mixed_grad, qkv_weight[layer_index])
        share_one, share_two = (
            lax.psum_scatter(
                part_one.astype(jnp.bfloat16), "tensor", scatter_dimension=0, tiled=True
            ).astype(jnp.float32),
            lax.psum_scatter(
                part_two.astype(jnp.bfloat16), "tensor", scatter_dimension=0, tiled=True
            ).astype(jnp.float32),
        )
        _, norm_back = jax.vjp(two_norms, layer_input, gains[layer_index], shifts[layer_index])
        input_grad, gain_grad, shift_grad = norm_back((share_one, share_two))
        gain_grads[layer_index] = gain_grad
        shift_grads[layer_index] = shift_grad
        incoming = incoming + input_grad
        qkv_bias_part = jnp.sum(mixed_grad.astype(jnp.float32), axis=0)
        up_bias_part = jnp.sum(hidden_grad.astype(jnp.float32), axis=0)
        layer_grads[layer_index] = (
            qkv_grad,
            qkv_bias_part,
            dense_grad,
            up_grad,
            up_bias_part,
            down_grad,
        )
    stacked = []
    for member in range(6):
        pieces = []
        for layer_index in range(layer_count):
            pieces.append(layer_grads[layer_index][member])
        stacked.append(jnp.stack(pieces))
    qkv_total, qkv_bias_total, dense_total, up_total, up_bias_total, down_total = stacked
    qkv_total, qkv_bias_total, dense_total, up_total, up_bias_total, down_total = (
        lax.psum(qkv_total.astype(jnp.bfloat16), "dp").astype(jnp.float32),
        lax.psum(qkv_bias_total.astype(jnp.bfloat16), "dp").astype(jnp.float32),
        lax.psum(dense_total.astype(jnp.bfloat16), "dp").astype(jnp.float32),
        lax.psum(up_total.astype(jnp.bfloat16), "dp").astype(jnp.float32),
        lax.psum(up_bias_total.astype(jnp.bfloat16), "dp").astype(jnp.float32),
        lax.psum(down_total.astype(jnp.bfloat16), "dp").astype(jnp.float32),
    )
    gains_total, shifts_total, bias_total = lax.psum(
        (jnp.stack(gain_grads), jnp.stack(shift_grads), jnp.stack(bias_grads)), ("dp", "tensor")
    )
    return (
        result,
        incoming,
        gains_total,
        shifts_total,
        qkv_total,
        qkv_bias_total,
        dense_total,
        bias_total,
        up_total,
        up_bias_total,
        down_total,
        bias_total,
    )


def solution(mesh):
    return jax.shard_map(
        on_device,
        mesh=mesh,
        in_specs=(
            P(("dp", "tensor"), None),
            P("dp", None),
            P(),
            P(),
            P(None, None, "tensor"),
            P(None, "tensor"),
            P(None, "tensor", None),
            P(),
            P(None, None, "tensor"),
            P(None, "tensor"),
            P(None, "tensor", None),
            P(),
            P(("dp", "tensor"), None),
        ),
        out_specs=(
            P(("dp", "tensor"), None),
            P(("dp", "tensor"), None),
            P(),
            P(),
            P(None, None, "tensor"),
            P(None, "tensor"),
            P(None, "tensor", None),
            P(),
            P(None, None, "tensor"),
            P(None, "tensor"),
            P(None, "tensor", None),
            P(),
        ),
        check_vma=False,
    )
```

profile of v0, /device:TPU:0, one launch (start us, length us, event | category | flops | bytes accessed | tf_op | source)
XLA Modules:
  0.0 2223.2 jit_solution(3805071325727976082)
XLA Ops:
  20.2 57.2 %all-gather.7.cloned.1.call-done = bf16[4096,1024]{1,0:T(8,128)(2,1)} async-done(((bf16[1024,1024]{1,0:T(8,128)(2,1)}), bf16[4096,1024]{1,0:T(8,128)(2,1)}) %all-gather.7.cloned.1.call-update) | async-done | bytes 8388624 | tf_op jit(solution)/shard_map/all_gather | solution.py:209
  103.4 16.9 reshape.354
  218.6 17.1 multiply_reduce_fusion.1
  235.9 17.7 fusion.42
  263.5 14.6 fusion.244
  278.2 16.7 multiply_add_fusion.3
  309.4 49.6 %multiply_convert_fusion.1 = (bf16[4096,1024]{1,0:T(8,128)(2,1)S(1)}, f32[4096,1024]{1,0:T(8,128)}, f32[4096,1024]{1,0:T(8,128)}) fusion(f32[1024]{0:T(1024)S(1)} %bitcast.533, bf16[4096,1024]{1,0:T(8,128)(2,1)} %all-gather.9.cloned.1.call-done, bf16[2,1024,1024]{2,1,0:T(8,128)(2,1)} %param.21), kind=kOutput, calls=%fused_computation.21 | convolution fusion | flops 8866758656 | bytes 52432896 | tf_op jit(solution)/shard_map/dot_general | solution.py:217
  384.5 69.9 %reduce-scatter.7.cloned.1.call-done = bf16[1024,1024]{1,0:T(8,128)(2,1)} async-done(((bf16[4096,1024]{1,0:T(8,128)(2,1)}), bf16[1024,1024]{1,0:T(8,128)(2,1)}) %reduce-scatter.7.cloned.1.call-update) | async-done | bytes 2097168 | tf_op jit(solution)/shard_map/reduce_scatter | solution.py:224
  462.4 56.6 %all-gather.11.cloned.1.call-done = bf16[4096,1024]{1,0:T(8,128)(2,1)} async-done(((bf16[1024,1024]{1,0:T(8,128)(2,1)}), bf16[4096,1024]{1,0:T(8,128)(2,1)}) %all-gather.11.cloned.1.call-update) | async-done | bytes 8388624 | tf_op jit(solution)/shard_map/all_gather | solution.py:209
  545.1 17.0 reshape.359
  647.8 15.9 fusion.354
  663.7 19.4 multiply_reduce_fusion
  683.2 18.6 fusion.39
  701.8 14.3 fusion.197
  716.3 14.7 fusion.245
  730.9 16.7 multiply_add_fusion.2
  783.0 18.8 fusion.22
  801.8 14.2 add_add_fusion.1
  822.8 18.7 fusion.184
  847.5 15.8 fusion.33
  882.0 22.0 fusion.35
  917.0 24.4 %multiply_add_fusion.1 = f32[2,4,32,64,64]{4,3,2,1,0:T(8,128)} fusion(f32[2,4,32,64,64]{4,3,2,1,0:T(8,128)} %fusion.23, f32[2,4,32,64]{3,2,1,0:T(8,128)S(1)} %convolution_bitcast_fusion.1, f32[2,32,64]{2,1,0:T(8,128)S(1)} %copy-done.51, f32[2,4,32,64,64]{4,3,2,1,0:T(8,128)S(1)} %bitcast.454, f32[2,4,32,64,64]{4,2,3,1,0:T(8,128)} %copy-done.8), kind=kOutput, calls=%fused_computation.56 | convolution fusion | flops 808452096 | bytes 16859136 | tf_op jit(solution)/shard_map/transpose(jvp(vmap(vmap(bcm,bce->bme))))/dot_general | solution.py:117
  967.5 14.4 copy.350
  998.7 49.7 %multiply_convert_fusion = (bf16[4096,1024]{1,0:T(8,128)(2,1)}, f32[4096,1024]{1,0:T(8,128)}, f32[4096,1024]{1,0:T(8,128)}) fusion(f32[1024]{0:T(1024)S(1)} %bitcast.535, bf16[4096,1024]{1,0:T(8,128)(2,1)} %all-gather.13.cloned.1.call-done, bf16[2,1024,1024]{2,1,0:T(8,128)(2,1)} %param.21), kind=kOutput, calls=%fused_computation.7 | convolution fusion | flops 8866758656 | bytes 52432896 | tf_op jit(solution)/shard_map/dot_general | solution.py:217
  1048.5 23.4 %fusion.351 = (bf16[1024]{0:T(1024)(128)(2,1)}, bf16[4096,1024]{1,0:T(8,128)(2,1)}) fusion(f32[4096,1024]{1,0:T(8,128)} %get-tuple-element.53, bf16[4096,1024]{1,0:T(8,128)(2,1)} %all-gather.15.cloned.1.call-done, bf16[2,1024,1024]{2,1,0:T(8,128)(2,1)S(1)} %copy-done.128, f32[4096,1024]{1,0:T(8,128)} %get-tuple-element.128, f32[1024]{0:T(1024)S(1)} %bitcast.536), kind=kOutput, calls=%fused_computation.506 | convolution fusion | flops 8657042432 | bytes 52434944 | tf_op jit(solution)/shard_map/dot_general | solution.py:157
  1071.8 15.2 convolution_convert_fusion.3
  1091.7 15.9 fusion.202
  1120.0 39.0 %reduce-scatter.11.cloned.1.call-done = bf16[1024,1024]{1,0:T(8,128)(2,1)} async-done(((bf16[4096,1024]{1,0:T(8,128)(2,1)}), bf16[1024,1024]{1,0:T(8,128)(2,1)}) %reduce-scatter.11.cloned.1.call-update) | async-done | bytes 2097168 | tf_op jit(solution)/shard_map/reduce_scatter | solution.py:271
  1169.3 64.1 %reduce-scatter.9.cloned.1.call-done = bf16[1024,1024]{1,0:T(8,128)(2,1)} async-done(((bf16[4096,1024]{1,0:T(8,128)(2,1)}), bf16[1024,1024]{1,0:T(8,128)(2,1)}) %reduce-scatter.9.cloned.1.call-update) | async-done | bytes 2097168 | tf_op jit(solution)/shard_map/reduce_scatter | solution.py:224
  1251.3 14.3 fusion.237
  1314.7 19.8 fusion.189
  1334.5 13.5 convolution_convert_fusion.4
  1348.1 14.6 fusion.21
  1362.7 18.7 fusion.20
  1381.5 19.7 fusion.28
  1404.1 15.1 fusion.26
  1419.2 13.9 add_add_fusion
  1439.9 25.8 %multiply_add_fusion = f32[2,4,32,64,64]{4,3,2,1,0:T(8,128)} fusion(f32[2,4,32,64,64]{4,3,2,1,0:T(8,128)} %fusion.21, f32[2,4,32,64]{3,2,1,0:T(8,128)S(1)} %convolution_bitcast_fusion, f32[2,32,64]{2,1,0:T(8,128)S(1)} %copy-done.52, f32[2,4,32,64,64]{4,3,2,1,0:T(8,128)} %bitcast.448, f32[2,4,32,64,64]{4,2,3,1,0:T(8,128)} %copy-done.9), kind=kOutput, calls=%fused_computation.50 | convolution fusion | flops 808452096 | bytes 16859136 | tf_op jit(solution)/shard_map/transpose(jvp(vmap(vmap(bcm,bce->bme))))/dot_general | solution.py:117
  1517.5 14.6 copy.367
  1536.2 25.7 %fusion.352 = (bf16[1024]{0:T(1024)(128)(2,1)S(1)}, bf16[4096,1024]{1,0:T(8,128)(2,1)}) fusion(f32[4096,1024]{1,0:T(8,128)} %get-tuple-element.57, bf16[4096,1024]{1,0:T(8,128)(2,1)} %all-gather.17.cloned.1.call-done, bf16[2,1024,1024]{2,1,0:T(8,128)(2,1)} %param.23, f32[4096,1024]{1,0:T(8,128)} %get-tuple-element.121, f32[1024]{0:T(1024)S(1)} %bitcast.534), kind=kOutput, calls=%fused_computation.507 | convolution fusion | flops 8657042432 | bytes 52434944 | tf_op jit(solution)/shard_map/dot_general | solution.py:157
  1561.8 14.3 convert_bitcast_fusion.3
  1585.6 14.0 convert_bitcast_fusion.1
  1624.7 15.2 convolution_convert_fusion.1
  1640.9 23.4 %all-reduce.28 = (bf16[2,768]{1,0:T(2,128)(2,1)S(1)}, bf16[2,1024]{1,0:T(2,128)(2,1)S(1)}) all-reduce(bf16[2,768]{1,0:T(2,128)(2,1)S(1)} %pad_maximum_fusion.8, bf16[2,1024]{1,0:T(2,128)(2,1)S(1)} %pad_maximum_fusion.7), channel_id=1, replica_groups=mesh['dp'=8,'tensor'=4] {'dp'}, use_global_device_ids=true, to_apply=%region_39.40 | all-reduce | flops 3584 | bytes 14336 | tf_op jit(solution)/shard_map/psum | solution.py:299
  1665.5 346.7 %all-reduce.32.cloned.1.call-done = (bf16[2,1024,768]{2,1,0:T(8,128)(2,1)}, bf16[2,256,1024]{2,1,0:T(8,128)(2,1)}, bf16[2,1024,1024]{2,1,0:T(8,128)(2,1)}, bf16[2,1024,1024]{2,1,0:T(8,128)(2,1)}) async-done(((bf16[2,1024,768]{2,1,0:T(8,128)(2,1)}, bf16[2,256,1024]{2,1,0:T(8,128)(2,1)}, bf16[2,1024,1024]{2,1,0:T(8,128)(2,1)}, bf16[2,1024,1024]{2,1,0:T(8,128)(2,1)}), (bf16[2,1024,768]{2,1,0:T(8,128)(2,1)}, ...) | async-done | bytes 12582928 | tf_op jit(solution)/shard_map/psum | solution.py:298
  2030.0 55.4 %reduce-scatter.17.cloned.1.call-done = bf16[1024,1024]{1,0:T(8,128)(2,1)} async-done(((bf16[4096,1024]{1,0:T(8,128)(2,1)}), bf16[1024,1024]{1,0:T(8,128)(2,1)}) %reduce-scatter.17.cloned.1.call-update) | async-done | bytes 2097168 | tf_op jit(solution)/shard_map/reduce_scatter | solution.py:268
  2085.5 74.4 %reduce-scatter.15.cloned.1.call-done = bf16[1024,1024]{1,0:T(8,128)(2,1)} async-done(((bf16[4096,1024]{1,0:T(8,128)(2,1)}), bf16[1024,1024]{1,0:T(8,128)(2,1)}) %reduce-scatter.15.cloned.1.call-update) | async-done | bytes 2097168 | tf_op jit(solution)/shard_map/reduce_scatter | solution.py:271
  2169.0 40.4 %all-reduce.27 = (f32[2,2,1024]{2,1,0:T(2,128)}, f32[2,2,1024]{2,1,0:T(2,128)}, f32[2,1024]{1,0:T(2,128)S(1)}) all-reduce(f32[2,2,1024]{2,1,0:T(2,128)S(1)} %pad_maximum_fusion.4, f32[2,2,1024]{2,1,0:T(2,128)S(1)} %pad_maximum_fusion.5, f32[2,1024]{1,0:T(2,128)S(1)} %pad_maximum_fusion.6), channel_id=1, replica_groups=mesh['dp'=8,'tensor'=4] {'dp','tensor'}, use_global_device_ids=true, to_apply=%region_30.31 | all-reduce | flops 10240 | bytes 81920 | tf_op jit(solution)/shard_map/psum | solution.py:305
  (507 shorter events, 658.9 us)
Async XLA Ops:
  7.2 70.2 %all-gather.7.cloned.1.call-start = ((), (), s32[]{:S(2)}) async-start(), calls=%async_computation.6 | async-start | bytes 10485760 | tf_op jit(solution)/shard_map/all_gather | solution.py:209
  16.3 293.1 %all-gather.9.cloned.1.call-start = ((), (), s32[]{:S(2)}) async-start(), calls=%async_computation.7 | async-start | bytes 10485760 | tf_op jit(solution)/shard_map/all_gather | solution.py:210
  17.1 437.3 %reduce-scatter.7.cloned.1.call-start = ((), (), s32[]{:S(2)}) async-start(), calls=%async_computation.8 | async-start | bytes 10485760 | tf_op jit(solution)/shard_map/reduce_scatter | solution.py:224
  17.1 156.6 %copy-start.97 = (f32[64]{0:T(128)}, f32[64]{0:T(128)S(1)}, u32[]{:S(2)}) copy-start(f32[64]{0:T(128)S(1)} %get-tuple-element.141) | copy-start | bytes 772
  17.1 156.6 %copy-start.100 = (f32[64]{0:T(128)}, f32[64]{0:T(128)S(1)}, u32[]{:S(2)}) copy-start(f32[64]{0:T(128)S(1)} %get-tuple-element.142) | copy-start | bytes 772
  17.2 236.4 %copy-start.63 = (pred[32,32]{0,1:T(8,128)(4,1)}, pred[32,32]{0,1:T(8,128)(4,1)S(1)}, u32[]{:S(2)}) copy-start(pred[32,32]{0,1:T(8,128)(4,1)S(1)} %iota_compare_fusion.2) | copy-start | bytes 3076
  18.4 291.0 %copy-start.122 = (f32[1,1024]{1,0:T(1,128)}, f32[1,1024]{1,0:T(1,128)S(1)}, u32[]{:S(2)}) copy-start(f32[1,1024]{1,0:T(1,128)S(1)} %get-tuple-element.120) | copy-start | bytes 12292
  18.8 234.8 %copy-start.71 = (s32[2,32]{1,0:T(2,128)}, s32[2,32]{1,0:T(2,128)S(1)}, u32[]{:S(2)}) copy-start(s32[2,32]{1,0:T(2,128)S(1)} %slice_reduce_fusion) | copy-start | bytes 772
  18.9 234.7 %copy-start.74 = (s32[2,32]{1,0:T(2,128)}, s32[2,32]{1,0:T(2,128)S(1)}, u32[]{:S(2)}) copy-start(s32[2,32]{1,0:T(2,128)S(1)} %concatenate.18) | copy-start | bytes 772
  19.0 216.9 %copy-start.50 = (f32[2,32,64]{2,1,0:T(8,128)}, f32[2,32,64]{2,1,0:T(8,128)S(1)}, u32[]{:S(2)}) copy-start(f32[2,32,64]{2,1,0:T(8,128)S(1)} %get-tuple-element.100) | copy-start | bytes 49156
  19.0 259.2 %copy-start.34 = (f32[2,32,64]{2,1,0:T(8,128)}, f32[2,32,64]{2,1,0:T(8,128)S(1)}, u32[]{:S(2)}) copy-start(f32[2,32,64]{2,1,0:T(8,128)S(1)} %get-tuple-element.99) | copy-start | bytes 49156
  19.6 243.9 %copy-start = (f32[2,32,64,64]{2,3,1,0:T(8,128)}, f32[2,32,64,64]{2,3,1,0:T(8,128)S(1)}, u32[]{:S(2)}) copy-start(f32[2,32,64,64]{2,3,1,0:T(8,128)S(1)} %and_convert_fusion) | copy-start | bytes 3145732
  20.2 134.9 %copy-start.41 = (f32[2,2048,8]{1,2,0:T(8,128)}, f32[2,2048,8]{1,2,0:T(8,128)S(1)}, u32[]{:S(2)}) copy-start(f32[2,2048,8]{1,2,0:T(8,128)S(1)} %get-tuple-element.101) | copy-start | bytes 393220
  20.2 134.9 %copy-start.45 = (f32[2,2048,8]{1,2,0:T(8,128)}, f32[2,2048,8]{1,2,0:T(8,128)S(1)}, u32[]{:S(2)}) copy-start(f32[2,2048,8]{1,2,0:T(8,128)S(1)} %get-tuple-element.102) | copy-start | bytes 393220
  235.9 65.8 %copy-start.66 = (f32[2,4,2048]{2,1,0:T(4,128)}, f32[2,4,2048]{2,1,0:T(4,128)S(1)}, u32[]{:S(2)}) copy-start(f32[2,4,2048]{2,1,0:T(4,128)S(1)} %div.145) | copy-start | bytes 196612
  309.3 61.8 %copy-start.19 = (bf16[32,8,2,2048]{3,1,2,0:T(8,128)(2,1)}, bf16[32,8,2,2048]{3,1,2,0:T(8,128)(2,1)S(1)}, u32[]{:S(2)}) copy-start(bf16[32,8,2,2048]{3,1,2,0:T(8,128)(2,1)S(1)} %copy.424) | copy-start | bytes 6291460
  309.4 49.7 %copy-start.127 = (bf16[2,1024,1024]{2,1,0:T(8,128)(2,1)S(1)}, bf16[2,1024,1024]{2,1,0:T(8,128)(2,1)}, u32[]{:S(2)}) copy-start(bf16[2,1024,1024]{2,1,0:T(8,128)(2,1)} %param.23) | copy-start | bytes 12582916
  382.6 71.8 %copy-start.6 = (bf16[1024,1024]{1,0:T(8,128)(2,1)S(1)}, bf16[1024,1024]{1,0:T(8,128)(2,1)}, u32[]{:S(2)}) copy-start(bf16[1024,1024]{1,0:T(8,128)(2,1)} %param.13) | copy-start | bytes 6291460
  382.6 136.4 %all-gather.11.cloned.1.call-start = ((), (), s32[]{:S(2)}) async-start(), calls=%async_computation.9 | async-start | bytes 10485760 | tf_op jit(solution)/shard_map/all_gather | solution.py:209
  460.6 58.5 %copy-start.121 = (f32[768]{0:T(1024)S(1)}, f32[768]{0:T(1024)}, u32[]{:S(2)}) copy-start(f32[768]{0:T(1024)} %get-tuple-element.32) | copy-start | bytes 9220
  460.6 293.9 %all-gather.15.cloned.1.call-start = ((), (), s32[]{:S(2)}) async-start(), calls=%async_computation.12 | async-start | bytes 10485760 | tf_op jit(solution)/shard_map/all_gather | solution.py:256
  461.2 536.9 %all-gather.13.cloned.1.call-start = ((), (), s32[]{:S(2)}) async-start(), calls=%async_computation.10 | async-start | bytes 10485760 | tf_op jit(solution)/shard_map/all_gather | solution.py:210
  462.4 657.6 %reduce-scatter.13.cloned.1.call-start = ((), (), s32[]{:S(2)}) async-start(), calls=%async_computation.14 | async-start | bytes 10485760 | tf_op jit(solution)/shard_map/reduce_scatter | solution.py:268
  647.8 35.4 %slice-start.4 = ((s8[8388608]{0:T(1024)(128)(4,1)}), s8[4194304]{0:T(1024)(128)(4,1)S(1)}, s32[]{:S(2)}) async-start(s8[8388608]{0:T(1024)(128)(4,1)} %bitcast.442), calls=%async_computation.23 | async-start | bytes 8388608
  882.0 35.0 %slice-start.6 = ((s8[8388608]{0:T(1024)(128)(4,1)}), s8[4194304]{0:T(1024)(128)(4,1)S(1)}, s32[]{:S(2)}) async-start(s8[8388608]{0:T(1024)(128)(4,1)} %bitcast.452), calls=%async_computation.25 | async-start | bytes 8388608
  998.1 160.9 %reduce-scatter.11.cloned.1.call-start = ((), (), s32[]{:S(2)}) async-start(), calls=%async_computation.13 | async-start | bytes 10485760 | tf_op jit(solution)/shard_map/reduce_scatter | solution.py:271
  998.7 49.7 %copy-start.128 = (bf16[2,1024,1024]{2,1,0:T(8,128)(2,1)S(1)}, bf16[2,1024,1024]{2,1,0:T(8,128)(2,1)}, u32[]{:S(2)}) copy-start(bf16[2,1024,1024]{2,1,0:T(8,128)(2,1)} %param.23) | copy-start | bytes 12582916
  1087.0 146.4 %reduce-scatter.9.cloned.1.call-start = ((), (), s32[]{:S(2)}) async-start(), calls=%async_computation.11 | async-start | bytes 10485760 | tf_op jit(solution)/shard_map/reduce_scatter | solution.py:224
  1119.9 39.1 %copy-start.11 = (bf16[1024,1024]{1,0:T(8,128)(2,1)S(1)}, bf16[1024,1024]{1,0:T(8,128)(2,1)}, u32[]{:S(2)}) copy-start(bf16[1024,1024]{1,0:T(8,128)(2,1)} %copy-done.10) | copy-start | bytes 6291460
  1119.9 39.1 %copy-start.80 = (f32[1024]{0:T(1024)S(1)}, f32[1024]{0:T(1024)}, u32[]{:S(2)}) copy-start(f32[1024]{0:T(1024)} %copy-done.79) | copy-start | bytes 12292
  1119.9 39.1 %copy-start.86 = (f32[1,1,1024]{2,1,0:T(1,128)S(1)}, f32[1,1,1024]{2,1,0:T(1,128)}, u32[]{:S(2)}) copy-start(f32[1,1,1024]{2,1,0:T(1,128)} %get-tuple-element.103) | copy-start | bytes 12292
  1119.9 39.1 %copy-start.88 = (f32[1,1,1024]{2,1,0:T(1,128)S(1)}, f32[1,1,1024]{2,1,0:T(1,128)}, u32[]{:S(2)}) copy-start(f32[1,1,1024]{2,1,0:T(1,128)} %get-tuple-element.104) | copy-start | bytes 12292
  1119.9 44.4 %copy-start.96 = (f32[1024]{0:T(1024)S(1)}, f32[1024]{0:T(1024)}, u32[]{:S(2)}) copy-start(f32[1024]{0:T(1024)} %copy-done.95) | copy-start | bytes 12292
  1119.9 44.4 %copy-start.92 = (f32[1024]{0:T(1024)S(1)}, f32[1024]{0:T(1024)}, u32[]{:S(2)}) copy-start(f32[1024]{0:T(1024)} %copy-done.91) | copy-start | bytes 12292
  1119.9 182.4 %all-gather.17.cloned.1.call-start = ((), (), s32[]{:S(2)}) async-start(), calls=%async_computation.15 | async-start | bytes 10485760 | tf_op jit(solution)/shard_map/all_gather | solution.py:256
  1164.3 69.2 %copy-start.114 = (f32[1,1024]{1,0:T(1,128)S(1)}, f32[1,1024]{1,0:T(1,128)}, u32[]{:S(2)}) copy-start(f32[1,1024]{1,0:T(1,128)} %get-tuple-element.115) | copy-start | bytes 12292
  1164.3 69.2 %copy-start.115 = (f32[1,1024]{1,0:T(1,128)S(1)}, f32[1,1024]{1,0:T(1,128)}, u32[]{:S(2)}) copy-start(f32[1,1024]{1,0:T(1,128)} %get-tuple-element.117) | copy-start | bytes 12292
  1243.9 768.3 %all-reduce.32.cloned.1.call-start = ((), (), s32[]{:S(2)}) async-start(), calls=%async_computation.18 | async-start | bytes 25165824 | tf_op jit(solution)/shard_map/psum | solution.py:298
  1244.0 33.7 %slice-start.14 = ((s8[8388608]{0:T(1024)(128)(4,1)}), s8[4194304]{0:T(1024)(128)(4,1)S(1)}, s32[]{:S(2)}) async-start(s8[8388608]{0:T(1024)(128)(4,1)} %bitcast.542), calls=%async_computation.33 | async-start | bytes 8388608
  1536.1 65.9 %copy-start.33 = (bf16[96,8,2,2048]{3,1,2,0:T(8,128)(2,1)}, bf16[96,8,2,2048]{3,1,2,0:T(8,128)(2,1)S(1)}, u32[]{:S(2)}) copy-start(bf16[96,8,2,2048]{3,1,2,0:T(8,128)(2,1)S(1)} %copy.427) | copy-start | bytes 18874372
  1610.8 474.6 %reduce-scatter.17.cloned.1.call-start = ((), (), s32[]{:S(2)}) async-start(), calls=%async_computation.17 | async-start | bytes 10485760 | tf_op jit(solution)/shard_map/reduce_scatter | solution.py:268
  1624.7 535.2 %reduce-scatter.15.cloned.1.call-start = ((), (), s32[]{:S(2)}) async-start(), calls=%async_computation.16 | async-start | bytes 10485760 | tf_op jit(solution)/shard_map/reduce_scatter | solution.py:271
  2025.3 134.6 %copy-start.7 = (bf16[1024,1024]{1,0:T(8,128)(2,1)S(1)}, bf16[1024,1024]{1,0:T(8,128)(2,1)}, u32[]{:S(2)}) copy-start(bf16[1024,1024]{1,0:T(8,128)(2,1)} %param.13) | copy-start | bytes 6291460
  2025.3 134.6 %copy-start.78 = (f32[1024]{0:T(1024)S(1)}, f32[1024]{0:T(1024)}, u32[]{:S(2)}) copy-start(f32[1024]{0:T(1024)} %copy-done.77) | copy-start | bytes 12292
  2025.3 134.6 %copy-start.82 = (f32[1,1,1024]{2,1,0:T(1,128)S(1)}, f32[1,1,1024]{2,1,0:T(1,128)}, u32[]{:S(2)}) copy-start(f32[1,1,1024]{2,1,0:T(1,128)} %copy-done.81) | copy-start | bytes 12292
  2025.3 134.6 %copy-start.84 = (f32[1,1,1024]{2,1,0:T(1,128)S(1)}, f32[1,1,1024]{2,1,0:T(1,128)}, u32[]{:S(2)}) copy-start(f32[1,1,1024]{2,1,0:T(1,128)} %copy-done.83) | copy-start | bytes 12292
  2030.0 134.4 %copy-start.94 = (f32[1024]{0:T(1024)S(1)}, f32[1024]{0:T(1024)}, u32[]{:S(2)}) copy-start(f32[1024]{0:T(1024)} %copy-done.93) | copy-start | bytes 12292
  2030.0 134.4 %copy-start.90 = (f32[1024]{0:T(1024)S(1)}, f32[1024]{0:T(1024)}, u32[]{:S(2)}) copy-start(f32[1024]{0:T(1024)} %copy-done.89) | copy-start | bytes 12292
  (114 other events, 952.2 us)
Sparse Core Ops, SparseCore 0:
  16.4 60.9 all-gather.6
  79.6 58.2 all-gather.8
  382.7 71.5 reduce-scatter.6
  460.7 58.2 all-gather.10
  520.5 58.2 all-gather.14
  580.9 58.2 all-gather.12
  998.2 71.7 reduce-scatter.12
  1087.2 71.7 reduce-scatter.10
  1161.7 71.6 reduce-scatter.8
  1244.0 58.2 all-gather.16
  1611.0 401.1 all-reduce.31
  2014.8 70.6 reduce-scatter.16
  2088.1 71.7 reduce-scatter.14
where the time goes:
time: 2230 us; the launch traced here: 2220 us
  matrix products  946 us (42%)
  waiting for transfers between devices  777 us (35%)
  local copies, waits for them, and re-layouts  304 us (14%)
  other arithmetic  116 us (5%)
  blocking collectives  63.7 us (3%)
    psum x1, waiting for transfers between devices, on_device(): lax.psum(qkv_total.astype(jnp.bfloat16), 'dp').astype(jnp.float32)  347 us
    reduce_scatter x2, waiting for transfers between devices, on_device(): lax.psum_scatter((jnp.dot(context, dense_part, preferred_element_type=jnp...  134 us
    dot_general x8, matrix products, contract_cols(): lax.dot_general(left, right, (((1,), (1,)), ((), ())), preferred_element_...  122 us
    dot_general x6, matrix products, attend_head(): jnp.einsum('bcm,bce->bme', fed_keys, value_blocks, precision=highest)  117 us
    all_gather x2, waiting for transfers between devices, on_device(): lax.all_gather(local_one, 'tensor', axis=0, tiled=True)  114 us
    reduce_scatter x2, waiting for transfers between devices, on_device(): lax.psum_scatter(part_two.astype(jnp.bfloat16), 'tensor', scatter_dimensi...  113 us
    dot_general x6, matrix products, attend_head(): jnp.einsum('bcm,bdm->bcd', query_blocks, key_blocks, precision=highest)  101 us
    dot_general x6, matrix products, attend_head(): jnp.einsum('bcm,bme->bce', query_blocks, both_ways(states), precision=hig...  100 us
  transfers between devices with their start and end apart: 13, of which 9 were waited for; matrix products, arithmetic and copies ran while one was open for 42% of the time, Pallas kernels for 0%

commit v1 on v0

v1 whole, which is shorter than its diff:
```python
from functools import partial
import math

import numpy as np
import jax
import jax.numpy as jnp
from jax import lax
from jax.experimental import pallas as pl
from jax.experimental.pallas import tpu as pltpu
from jax.sharding import PartitionSpec as P

HS = 64
FEATS = 64
ROT = 16
PAIR = 2 * HS
SUB = 128

norm_eps = 1e-05
feature_scale = 0.75
rotary_base = 10000.0

f32 = jnp.float32
bf16 = jnp.bfloat16
NT = (((1,), (1,)), ((), ()))
TN = (((0,), (0,)), ((), ()))


def pair_order():
    half = ROT // 2
    rest = (HS - ROT) // 2
    order = []
    for side in range(2):
        for head in range(2):
            order += [(head, side * half + i) for i in range(half)]
        for head in range(2):
            order += [(head, ROT + side * rest + i) for i in range(rest)]
    return order


def column_order(heads):
    padded = heads + heads % 2
    width = padded * HS
    matrix = np.zeros((heads * 3 * HS, 3 * width), np.float32)
    order = pair_order()
    for pair in range(padded // 2):
        for lane, (side, entry) in enumerate(order):
            head = 2 * pair + side
            if head < heads:
                for part in range(2):
                    matrix[head * 3 * HS + part * HS + entry, part * width + pair * PAIR + lane] = 1
    for head in range(heads):
        for entry in range(HS):
            matrix[head * 3 * HS + 2 * HS + entry, 2 * width + head * HS + entry] = 1
    return matrix


def feature_matrix(group):
    rows = np.arange(FEATS)[:, None]
    cols = np.arange(HS)[None, :]
    table = np.cos(np.pi * (cols + 0.5) * rows / HS) * np.sqrt(2.0 / HS)
    table = table * np.where(rows == 0, np.sqrt(0.5), 1.0) * feature_scale
    matrix = np.zeros((group, group), np.float32)
    for pair in range(group // PAIR):
        for lane, (side, entry) in enumerate(pair_order()):
            start = pair * PAIR + side * FEATS
            matrix[pair * PAIR + lane, start : start + FEATS] = table[:, entry]
    return matrix


def lane_rates():
    half = ROT // 2
    rates = np.zeros((1, PAIR), np.float32)
    signs = np.zeros((1, PAIR), np.float32)
    for lane, (_, entry) in enumerate(pair_order()):
        if entry < ROT:
            rates[0, lane] = 1.0
            signs[0, lane] = -1.0 if entry < half else 1.0
    return rates, signs


def rotary_tables(starts, length):
    places = jnp.arange(length, dtype=jnp.int32)
    started = starts[:, None, :] <= places[None, :, None]
    latest = jnp.max(jnp.where(started, starts[:, None, :], 0), axis=-1)
    offsets = (places[None, :] - latest).reshape(-1, 1).astype(f32)
    half = ROT // 2
    rates, signs = lane_rates()
    powers = np.array([entry % half if entry < ROT else 0 for _, entry in pair_order()], np.float32)
    inverse = rotary_base ** (-(jnp.asarray(powers) * 2.0 / ROT)) * jnp.asarray(rates)
    angles = offsets * inverse.reshape(1, PAIR)
    return jnp.cos(angles), jnp.sin(angles) * jnp.asarray(signs)


def dot(a, b):
    return jnp.dot(a, b, preferred_element_type=f32)


def dot_nt(a, b):
    return lax.dot_general(a, b, NT, preferred_element_type=f32)


def latest_start(starts_ref, seq, count, places):
    latest = jnp.zeros_like(places)
    for j in range(count):
        start = starts_ref[seq, j]
        latest = jnp.maximum(latest, jnp.where(start <= places, start, 0))
    return latest


def latest_scalar(starts_ref, seq, count, place):
    latest = jnp.int32(0)
    for j in range(count):
        start = starts_ref[seq, j]
        latest = jnp.maximum(latest, jnp.where(start <= place, start, 0))
    return latest


def block_masks(starts_ref, seq, count, place):
    rows = place + lax.broadcasted_iota(jnp.int32, (SUB, SUB), 0)
    cols = place + lax.broadcasted_iota(jnp.int32, (SUB, SUB), 1)
    latest_rows = latest_start(starts_ref, seq, count, rows)
    allowed = (cols <= rows) & (cols >= latest_rows)
    carried = (latest_rows <= place).astype(f32)
    following = latest_scalar(starts_ref, seq, count, place + SUB)
    feeding = (rows >= following).astype(f32)
    keeping = jnp.where(following <= place, 1.0, 0.0).astype(f32)
    return rows, cols, allowed, carried, feeding, keeping


def halves(tile, low_lanes):
    zero = jnp.zeros_like(tile)
    return jnp.where(low_lanes, tile, zero), jnp.where(low_lanes, zero, tile)


def gelu_parts(hidden):
    size = jnp.abs(hidden)
    bell = jnp.exp(hidden * hidden * -0.5)
    t = 1.0 / (1.0 + (0.3275911 * math.sqrt(0.5)) * size)
    series = t * (
        0.5 * 0.254829592
        + t
        * (
            0.5 * -0.284496736
            + t * (0.5 * 1.421413741 + t * (0.5 * -1.453152027 + t * (0.5 * 1.061405429)))
        )
    )
    tail = series * bell
    share = jnp.where(hidden >= 0, 1.0 - tail, tail)
    return hidden * share, share + hidden * bell * (1.0 / math.sqrt(2.0 * math.pi))


def forward_kernel(
    width,
    count,
    blocks_per_seq,
    first_place,
    starts_ref,
    x_ref,
    wf_ref,
    bf_ref,
    wo_ref,
    dct_ref,
    cos_ref,
    sin_ref,
    state_in_ref,
    xh_ref,
    qkv_ref,
    ca_ref,
    rden_ref,
    gp_ref,
    states_ref,
    out_ref,
    state_ref,
):
    step = pl.program_id(0)
    seq = step // blocks_per_seq
    within = lax.rem(step, blocks_per_seq)
    rows = x_ref.shape[0]
    pairs = width // PAIR
    group = dct_ref.shape[0]

    @pl.when(within == 0)
    def _():
        state_ref[...] = state_in_ref[0]

    x = x_ref[...].astype(f32)
    center = jnp.mean(x, axis=-1, keepdims=True)
    shifted = x - center
    spread = jnp.mean(shifted * shifted, axis=-1, keepdims=True)
    xh = (shifted * lax.rsqrt(spread + norm_eps)).astype(bf16)
    xh_ref[...] = xh

    mixed = dot(xh, wf_ref[:, : 3 * width]) + bf_ref[:, : 3 * width]
    cosine = cos_ref[...]
    sine = sin_ref[...]
    dct = dct_ref[...]
    for part in range(2):
        for start in range(0, width, group):
            turned = []
            for lane in range(start, start + group, PAIR):
                tile = mixed[:, part * width + lane : part * width + lane + PAIR]
                turned.append(tile * cosine + pltpu.roll(tile, HS, 1) * sine)
            turned = turned[0] if len(turned) == 1 else jnp.concatenate(turned, axis=1)
            feats = jnp.exp(dot(turned.astype(bf16), dct)).astype(bf16)
            qkv_ref[:, part * width + start : part * width + start + group] = feats
    qkv_ref[:, 2 * width :] = mixed[:, 2 * width :].astype(bf16)

    hidden = dot(xh, wf_ref[:, 3 * width :]) + bf_ref[:, 3 * width :]
    active, slope = gelu_parts(hidden)
    ca_ref[:, width:] = active.astype(bf16)
    gp_ref[...] = slope.astype(bf16)

    low_lanes = lax.broadcasted_iota(jnp.int32, (SUB, PAIR), 1) < HS
    ones = jnp.ones((SUB, PAIR), bf16)
    for sub in range(rows // SUB):
        place = first_place + within * rows + sub * SUB
        _, _, allowed, carried, feeding, keeping = block_masks(starts_ref, seq, count, place)
        allowed2 = jnp.concatenate([allowed, allowed], axis=0)
        carried = carried.astype(bf16)
        feeding = feeding.astype(bf16)
        at = slice(sub * SUB, (sub + 1) * SUB)
        for pair in range(pairs):
            lanes = slice(pair * PAIR, (pair + 1) * PAIR)
            q = qkv_ref[at, pair * PAIR : (pair + 1) * PAIR]
            k = qkv_ref[at, width + pair * PAIR : width + (pair + 1) * PAIR]
            v = qkv_ref[at, 2 * width + pair * PAIR : 2 * width + (pair + 1) * PAIR]
            q0, q1 = halves(q, low_lanes)
            qs = jnp.concatenate([q0, q1], axis=0)
            weights = jnp.where(allowed2, dot_nt(qs, k), 0.0).astype(bf16)
            state = state_ref[pair * PAIR : (pair + 1) * PAIR, :]
            state_low = state.astype(bf16)
            first = (sub * pairs + pair) * PAIR
            states_ref[first : first + PAIR, :] = state_low
            qc = jnp.concatenate([q0 * carried, q1 * carried], axis=0)
            left = jnp.concatenate([weights, qc], axis=1)
            valued = jnp.concatenate([v, ones], axis=1)
            right = jnp.concatenate([valued, state_low], axis=0)
            both = dot(left, right)
            numerator = jnp.where(low_lanes, both[:SUB, :PAIR], both[SUB:, :PAIR])
            denominator = jnp.where(low_lanes, both[:SUB, PAIR:], both[SUB:, PAIR:])
            inverse = 1.0 / denominator
            ca_ref[at, lanes] = (numerator * inverse).astype(bf16)
            rden_ref[at, lanes] = inverse.astype(bf16)
            added = lax.dot_general(k * feeding, valued, TN, preferred_element_type=f32)
            state_ref[pair * PAIR : (pair + 1) * PAIR, :] = keeping * state + added

    out_ref[...] = dot(ca_ref[...], wo_ref[...]).astype(bf16)


def backward_kernel(
    width,
    count,
    blocks_per_seq,
    first_place,
    starts_ref,
    bg_ref,
    wot_ref,
    wft_ref,
    dctt_ref,
    cos_ref,
    sin_ref,
    state_in_ref,
    qkv_ref,
    ca_ref,
    rden_ref,
    gp_ref,
    states_ref,
    dz_ref,
    dx_ref,
    db_ref,
    state_ref,
    dqk_ref,
):
    step = pl.program_id(0)
    blocks = pl.num_programs(0)
    seq = (blocks - 1 - step) // blocks_per_seq
    within = lax.rem(blocks - 1 - step, blocks_per_seq)
    rows = bg_ref.shape[0]
    pairs = width // PAIR
    group = dctt_ref.shape[0]

    @pl.when(within == blocks_per_seq - 1)
    def _():
        state_ref[...] = state_in_ref[0]

    @pl.when(step == 0)
    def _():
        db_ref[...] = jnp.zeros_like(db_ref)

    bg = bg_ref[...]
    active_grad = dot(bg, wot_ref[:, width:])
    dz_ref[:, 3 * width :] = (active_grad * gp_ref[...].astype(f32)).astype(bf16)
    context_grad = dot(bg, wot_ref[:, :width])

    low_lanes = lax.broadcasted_iota(jnp.int32, (SUB, PAIR), 1) < HS
    ones = jnp.ones((SUB, PAIR), bf16)
    zeros = jnp.zeros((SUB, PAIR), bf16)
    scale = 1.0 / HS
    sum_rows = lax.broadcasted_iota(jnp.int32, (2 * PAIR, 2 * PAIR), 0)
    sum_cols = lax.broadcasted_iota(jnp.int32, (2 * PAIR, 2 * PAIR), 1)
    same_head = (lax.rem(sum_rows, PAIR) // HS) == (sum_cols // PAIR)
    summing = jnp.where(same_head, -scale, 0.0).astype(bf16)
    for sub in reversed(range(rows // SUB)):
        place = first_place + within * rows + sub * SUB
        rows_at, cols_at, allowed, carried, feeding, keeping = block_masks(
            starts_ref, seq, count, place
        )
        latest_cols = latest_start(starts_ref, seq, count, cols_at)
        flipped = (rows_at <= cols_at) & (rows_at >= latest_cols)
        allowed2 = jnp.concatenate([allowed, allowed], axis=0)
        flipped2 = jnp.concatenate([flipped, flipped], axis=0)
        carried2 = jnp.concatenate([carried, carried], axis=0)
        feeding2 = jnp.concatenate([feeding, feeding], axis=0)
        carried_low = carried.astype(bf16)
        at = slice(sub * SUB, (sub + 1) * SUB)
        for pair in range(pairs):
            lanes = slice(pair * PAIR, (pair + 1) * PAIR)
            q = qkv_ref[at, pair * PAIR : (pair + 1) * PAIR]
            k = qkv_ref[at, width + pair * PAIR : width + (pair + 1) * PAIR]
            v = qkv_ref[at, 2 * width + pair * PAIR : 2 * width + (pair + 1) * PAIR]
            first = (sub * pairs + pair) * PAIR
            state = states_ref[first : first + PAIR, :]
            later = state_ref[pair * PAIR : (pair + 1) * PAIR, :]
            later_low = later.astype(bf16)
            scaled = context_grad[at, lanes] * rden_ref[at, lanes].astype(f32)
            dnum = scaled.astype(bf16)
            product = scaled * ca_ref[at, lanes].astype(f32)
            product_high = product.astype(bf16)
            product_low = (product - product_high.astype(f32)).astype(bf16)
            dden = dot(jnp.concatenate([product_high, product_low], axis=1), summing)
            dden0, dden1 = dden[:, :PAIR], dden[:, PAIR:]
            high0, high1 = dden0.astype(bf16), dden1.astype(bf16)
            split0 = jnp.where(low_lanes, dden0, dden0 - high0.astype(f32)).astype(bf16)
            split1 = jnp.where(low_lanes, dden1, dden1 - high1.astype(f32)).astype(bf16)
            dnum0, dnum1 = halves(dnum, low_lanes)
            xs = jnp.concatenate(
                [
                    jnp.concatenate([dnum0, split0], axis=1),
                    jnp.concatenate([dnum1, split1], axis=1),
                ],
                axis=0,
            )
            valued = jnp.concatenate([v, ones], axis=1)
            first_two = dot_nt(xs, jnp.concatenate([valued, state], axis=0))
            dscores = jnp.where(allowed2, first_two[:, :SUB], 0.0).astype(bf16)
            dq = dot(dscores, k) + first_two[:, SUB:] * carried2
            dq = jnp.where(low_lanes, dq[:SUB], dq[SUB:])
            v0, v1 = halves(v, low_lanes)
            k0, k1 = halves(k, low_lanes)
            q0, q1 = halves(q, low_lanes)
            back0 = dot_nt(
                jnp.concatenate([v0, ones], axis=1),
                jnp.concatenate([jnp.concatenate([dnum, split0], axis=1), later_low], axis=0),
            )
            back1 = dot_nt(
                jnp.concatenate([v1, ones], axis=1),
                jnp.concatenate([jnp.concatenate([dnum, split1], axis=1), later_low], axis=0),
            )
            back = jnp.concatenate([back0, back1], axis=0)
            ks = jnp.concatenate([k0, k1], axis=0)
            q_turned = jnp.transpose(q)
            over = dot(ks, jnp.concatenate([q_turned, later_low[:, :PAIR]], axis=1))
            left = jnp.concatenate(
                [
                    jnp.where(flipped2, back[:, :SUB], 0.0).astype(bf16),
                    jnp.where(flipped2, over[:, :SUB], 0.0).astype(bf16),
                ],
                axis=1,
            )
            right = jnp.concatenate(
                [
                    jnp.concatenate([q, zeros], axis=1),
                    jnp.concatenate([zeros, dnum], axis=1),
                ],
                axis=0,
            )
            both = dot(left, right)
            dk = both[:, :PAIR] + back[:, SUB:] * feeding2
            dv = both[:, PAIR:] + over[:, SUB:] * feeding2
            dk = jnp.where(low_lanes, dk[:SUB], dk[SUB:])
            dv = jnp.where(low_lanes, dv[:SUB], dv[SUB:])
            dqk_ref[at, lanes] = (dq * q.astype(f32)).astype(bf16)
            dqk_ref[at, width + pair * PAIR : width + (pair + 1) * PAIR] = (
                dk * k.astype(f32)
            ).astype(bf16)
            dz_ref[at, 2 * width + pair * PAIR : 2 * width + (pair + 1) * PAIR] = dv.astype(bf16)
            qs = jnp.concatenate([q0 * carried_low, q1 * carried_low], axis=0)
            added = lax.dot_general(qs, xs, TN, preferred_element_type=f32)
            state_ref[pair * PAIR : (pair + 1) * PAIR, :] = keeping * later + added

    cosine = cos_ref[...]
    sine = sin_ref[...]
    dctt = dctt_ref[...]
    for part in range(2):
        for start in range(0, width, group):
            begin = part * width + start
            turned = dot(dqk_ref[:, begin : begin + group], dctt)
            for lane in range(0, group, PAIR):
                tile = turned[:, lane : lane + PAIR]
                back = tile * cosine - pltpu.roll(tile, HS, 1) * sine
                dz_ref[:, begin + lane : begin + lane + PAIR] = back.astype(bf16)

    dz = dz_ref[...]
    dx_ref[...] = dot(dz, wft_ref[...]).astype(bf16)
    db_ref[...] += jnp.sum(dz.astype(f32), axis=0, keepdims=True)


def whole_spec(array):
    return pl.BlockSpec(array.shape, lambda i, *_: (0,) * array.ndim)


def forward_layer(x, starts, wf, bf, wo, dct, cosine, sine, state_in, first_place, block):
    rows, model = x.shape
    seqs, count = starts.shape
    span = wf.shape[1]
    inner = wo.shape[0]
    width = (span - inner) // 2
    hidden = inner - width
    pairs = width // PAIR
    blocks = rows // block
    per_seq = blocks // seqs
    by_rows = lambda cols: pl.BlockSpec((block, cols), lambda i, *_: (i, 0))
    state_rows = block // SUB * pairs * PAIR
    return pl.pallas_call(
        partial(forward_kernel, width, count, per_seq, first_place),
        grid_spec=pltpu.PrefetchScalarGridSpec(
            num_scalar_prefetch=1,
            grid=(blocks,),
            in_specs=[
                by_rows(model),
                whole_spec(wf),
                whole_spec(bf),
                whole_spec(wo),
                whole_spec(dct),
                by_rows(PAIR),
                by_rows(PAIR),
                pl.BlockSpec((1, pairs * PAIR, 2 * PAIR), lambda i, *_: (i // per_seq, 0, 0)),
            ],
            out_specs=[
                by_rows(model),
                by_rows(3 * width),
                by_rows(inner),
                by_rows(width),
                by_rows(hidden),
                pl.BlockSpec((state_rows, 2 * PAIR), lambda i, *_: (i, 0)),
                by_rows(model),
            ],
            scratch_shapes=[pltpu.VMEM((pairs * PAIR, 2 * PAIR), f32)],
        ),
        out_shape=[
            jax.ShapeDtypeStruct((rows, model), bf16),
            jax.ShapeDtypeStruct((rows, 3 * width), bf16),
            jax.ShapeDtypeStruct((rows, inner), bf16),
            jax.ShapeDtypeStruct((rows, width), bf16),
            jax.ShapeDtypeStruct((rows, hidden), bf16),
            jax.ShapeDtypeStruct((blocks * state_rows, 2 * PAIR), bf16),
            jax.ShapeDtypeStruct((rows, model), bf16),
        ],
        compiler_params=pltpu.CompilerParams(vmem_limit_bytes=56 * 1024 * 1024),
        cost_estimate=pl.CostEstimate(
            flops=2 * rows * model * (span + inner),
            bytes_accessed=2 * rows * (3 * model + 3 * width + inner + width + hidden),
            transcendentals=0,
        ),
        name="layer_forward",
    )(starts, x, wf, bf, wo, dct, cosine, sine, state_in)


def backward_layer(bg, starts, wot, wft, dctt, cosine, sine, state_in, saved, first_place, block):
    qkv, ca, rden, gp, states = saved
    rows, model = bg.shape
    seqs, count = starts.shape
    span = wft.shape[0]
    inner = wot.shape[1]
    width = (span - inner) // 2
    hidden = inner - width
    pairs = width // PAIR
    blocks = rows // block
    per_seq = blocks // seqs
    by_rows = lambda cols: pl.BlockSpec((block, cols), lambda i, *_: (blocks - 1 - i, 0))
    state_rows = block // SUB * pairs * PAIR
    return pl.pallas_call(
        partial(backward_kernel, width, count, per_seq, first_place),
        grid_spec=pltpu.PrefetchScalarGridSpec(
            num_scalar_prefetch=1,
            grid=(blocks,),
            in_specs=[
                by_rows(model),
                whole_spec(wot),
                whole_spec(wft),
                whole_spec(dctt),
                by_rows(PAIR),
                by_rows(PAIR),
                pl.BlockSpec(
                    (1, pairs * PAIR, 2 * PAIR), lambda i, *_: ((blocks - 1 - i) // per_seq, 0, 0)
                ),
                by_rows(3 * width),
                by_rows(inner),
                by_rows(width),
                by_rows(hidden),
                pl.BlockSpec((state_rows, 2 * PAIR), lambda i, *_: (blocks - 1 - i, 0)),
            ],
            out_specs=[
                by_rows(span),
                by_rows(model),
                pl.BlockSpec((1, span), lambda i, *_: (0, 0)),
            ],
            scratch_shapes=[
                pltpu.VMEM((pairs * PAIR, 2 * PAIR), f32),
                pltpu.VMEM((block, 2 * width), bf16),
            ],
        ),
        out_shape=[
            jax.ShapeDtypeStruct((rows, span), bf16),
            jax.ShapeDtypeStruct((rows, model), bf16),
            jax.ShapeDtypeStruct((1, span), f32),
        ],
        compiler_params=pltpu.CompilerParams(vmem_limit_bytes=56 * 1024 * 1024),
        cost_estimate=pl.CostEstimate(
            flops=2 * rows * model * (span + inner),
            bytes_accessed=2 * rows * (2 * model + span + 3 * width + inner + width + hidden),
            transcendentals=0,
        ),
        name="layer_backward",
    )(starts, bg, wot, wft, dctt, cosine, sine, state_in, qkv, ca, rden, gp, states)


def swapped(array, axis, distance):
    size = lax.axis_size(axis)
    return lax.ppermute(array, axis, [(i, i ^ distance) for i in range(size)])


def bits_of(axis):
    return [1 << b for b in range(lax.axis_size(axis).bit_length() - 1)]


def gather_rows(block, axis):
    own = lax.axis_index(axis)
    held = {0: block}
    for distance in reversed(bits_of(axis)):
        held.update({m | distance: swapped(b, axis, distance) for m, b in list(held.items())})
    rows = block.shape[0]
    whole = jnp.zeros((rows * len(held),) + block.shape[1:], block.dtype)
    for m, b in held.items():
        whole = lax.dynamic_update_slice_in_dim(whole, b, (own ^ m) * rows, 0)
    return whole


def scatter_rows(partial_sum, axis):
    own = lax.axis_index(axis)
    size = lax.axis_size(axis)
    rows = partial_sum.shape[0] // size
    rest = partial_sum.shape[1:]
    now = partial_sum.reshape((size, rows) + rest)
    distances = bits_of(axis)
    for distance in distances:
        now = now.reshape((now.shape[0] // 2, 2, rows) + rest)
        bit = (own // distance) % 2
        keep = lax.dynamic_index_in_dim(now, bit, 1, keepdims=False)
        send = lax.dynamic_index_in_dim(now, 1 - bit, 1, keepdims=False)
        now = keep.astype(f32) + swapped(send, axis, distance).astype(f32)
        if distance != distances[-1]:
            now = now.astype(bf16)
    return now.reshape((rows,) + rest)


def on_device(
    tokens,
    doc_starts,
    norm_gains,
    norm_shifts,
    qkv_weight,
    qkv_bias,
    dense_weight,
    dense_bias,
    up_weight,
    up_bias,
    down_weight,
    down_bias,
    out_grad,
):
    layers = qkv_weight.shape[0]
    seqs = doc_starts.shape[0]
    model = tokens.shape[1]
    total_rows = tokens.shape[0] * lax.axis_size("tensor")
    length = total_rows // seqs
    heads = qkv_weight.shape[2] // (3 * HS)
    padded = heads + heads % 2
    width = padded * HS
    group = 2 * PAIR if padded % 4 == 0 else PAIR
    block = min(512, length)

    order = jnp.asarray(column_order(heads), bf16)
    feature = feature_matrix(group)
    dct = jnp.asarray(feature, bf16)
    dctt = jnp.asarray(feature.T, bf16)
    cosine, sine = rotary_tables(doc_starts, length)
    zero_state = jnp.zeros((seqs, padded // 2 * PAIR, 2 * PAIR), f32)
    gains = norm_gains.astype(f32)
    shifts = norm_shifts.astype(f32)

    folded = []
    for l in range(layers):
        ordered = dot(qkv_weight[l], order)
        wf = jnp.concatenate(
            [
                (gains[l, 0][:, None] * ordered).astype(bf16),
                (gains[l, 1][:, None] * up_weight[l].astype(f32)).astype(bf16),
            ],
            axis=1,
        )
        bias_one = dot(norm_shifts[l, 0:1], qkv_weight[l]) + qkv_bias[l].astype(f32)[None]
        bias_one = jnp.dot(bias_one, order.astype(f32), precision=lax.Precision.HIGHEST)
        bias_two = dot(norm_shifts[l, 1:2], up_weight[l]) + up_bias[l].astype(f32)[None]
        bf = jnp.concatenate([bias_one, bias_two], axis=1)
        dense = dense_weight[l]
        if padded != heads:
            dense = jnp.concatenate([dense, jnp.zeros((width - heads * HS, model), bf16)], axis=0)
        wo = jnp.concatenate([dense, down_weight[l]], axis=0)
        folded.append((wf, bf, wo, ordered.astype(bf16)))

    gathered_out_grad = gather_rows(out_grad, "tensor")
    own = tokens
    inputs = []
    saved = []
    for l in range(layers):
        wf, bf, wo, _ = folded[l]
        x = gather_rows(own, "tensor")
        xh, qkv, ca, rden, gp, states, out = forward_layer(
            x, doc_starts, wf, bf, wo, dct, cosine, sine, zero_state, 0, block
        )
        summed = scatter_rows(out, "tensor")
        inputs.append(own)
        saved.append((xh, qkv, ca, rden, gp, states))
        biases = dense_bias[l].astype(f32) + down_bias[l].astype(f32)
        own = (own.astype(f32) + (summed + biases)).astype(bf16)
    result = own

    incoming = out_grad.astype(f32)
    sums = [None] * layers
    weight_grads = [None] * layers
    for l in reversed(range(layers)):
        wf, bf, wo, ordered = folded[l]
        xh, qkv, ca, rden, gp, states = saved[l]
        own_grad = incoming.astype(bf16)
        bias_grad = jnp.sum(own_grad.astype(f32), axis=0)
        bg = gathered_out_grad if l == layers - 1 else gather_rows(own_grad, "tensor")
        dz, dx, db = backward_layer(
            bg,
            doc_starts,
            wo.T,
            wf.T,
            dctt,
            cosine,
            sine,
            zero_state,
            (qkv, ca, rden, gp, states),
            0,
            block,
        )
        out_weight_grad = lax.dot_general(ca, bg, TN, preferred_element_type=f32)
        in_weight_grad = lax.dot_general(xh, dz, TN, preferred_element_type=f32)
        db_one, db_two = db[:, : 3 * width], db[:, 3 * width :]
        grad_one = in_weight_grad[:, : 3 * width]
        grad_two = in_weight_grad[:, 3 * width :]
        weights_one = ordered.astype(f32)
        weights_two = up_weight[l].astype(f32)
        gain_grad = jnp.stack(
            [jnp.sum(weights_one * grad_one, axis=1), jnp.sum(weights_two * grad_two, axis=1)]
        )
        shift_grad = jnp.stack(
            [jnp.sum(weights_one * db_one, axis=1), jnp.sum(weights_two * db_two, axis=1)]
        )
        qkv_grad = (gains[l, 0][:, None] * grad_one + shifts[l, 0][:, None] * db_one).astype(bf16)
        up_grad = (gains[l, 1][:, None] * grad_two + shifts[l, 1][:, None] * db_two).astype(bf16)
        dense_grad = out_weight_grad[: heads * HS].astype(bf16)
        down_grad = out_weight_grad[width:].astype(bf16)
        qkv_bias_grad = jnp.dot(
            db_one, order.astype(f32).T, precision=lax.Precision.HIGHEST
        ).astype(bf16)[0]
        up_bias_grad = db_two.astype(bf16)[0]
        weight_grads[l] = lax.psum(
            (qkv_grad, dense_grad, up_grad, down_grad, qkv_bias_grad, up_bias_grad), "dp"
        )
        sums[l] = (gain_grad, shift_grad, bias_grad)

        normed_grad = scatter_rows(dx, "tensor")
        rows_in = inputs[l].astype(f32)
        center = jnp.mean(rows_in, axis=-1, keepdims=True)
        shifted = rows_in - center
        spread = jnp.mean(shifted * shifted, axis=-1, keepdims=True)
        inverse = lax.rsqrt(spread + norm_eps)
        normal = shifted * inverse
        along = jnp.mean(normed_grad * normal, axis=-1, keepdims=True)
        level = jnp.mean(normed_grad, axis=-1, keepdims=True)
        incoming = incoming + inverse * (normed_grad - level - normal * along)

    stack = lambda j: jnp.stack([weight_grads[l][j] for l in range(layers)])
    qkv_total = lax.dot_general(
        stack(0), order, (((2,), (1,)), ((), ())), preferred_element_type=f32
    )
    gains_total, shifts_total, bias_total = lax.psum(
        tuple(jnp.stack([sums[l][j] for l in range(layers)]) for j in range(3)), ("dp", "tensor")
    )
    return (
        result,
        incoming,
        gains_total,
        shifts_total,
        qkv_total,
        stack(4).astype(f32),
        stack(1).astype(f32),
        bias_total,
        stack(2).astype(f32),
        stack(5).astype(f32),
        stack(3).astype(f32),
        bias_total,
    )


def solution(mesh):
    return jax.shard_map(
        on_device,
        mesh=mesh,
        in_specs=(
            P(("dp", "tensor"), None),
            P("dp", None),
            P(),
            P(),
            P(None, None, "tensor"),
            P(None, "tensor"),
            P(None, "tensor", None),
            P(),
            P(None, None, "tensor"),
            P(None, "tensor"),
            P(None, "tensor", None),
            P(),
            P(("dp", "tensor"), None),
        ),
        out_specs=(
            P(("dp", "tensor"), None),
            P(("dp", "tensor"), None),
            P(),
            P(),
            P(None, None, "tensor"),
            P(None, "tensor"),
            P(None, "tensor", None),
            P(),
            P(None, None, "tensor"),
            P(None, "tensor"),
            P(None, "tensor", None),
            P(),
        ),
        check_vma=False,
    )
```

time: 2230 us -> 1230 us (0.55)
  matrix products: 946 us -> 98.9 us
  waiting for transfers between devices: 777 us -> 468 us
  Pallas kernels: 0 us -> 262 us
  local copies, waits for them, and re-layouts: 304 us -> 146 us
  blocking collectives: 63.7 us -> 124 us
    dot_general x68 -> x15, matrix products: 946 us -> 98.9 us  [the longest x2 46.5 us: on_device(): in_weight_grad = lax.dot_general(xh, dz, TN, preferred_element_type=f32)]
    reduce_scatter x6 -> x0, waiting for transfers between devices: 303 us -> none  [the longest x2 134 us: on_device(): lax.psum_scatter((jnp.dot(context, dense_part, preferred_element_type=jnp...]
    pallas_call x0 -> x4, Pallas kernels: none -> 262 us  [the longest x2 152 us: backward_layer(): pl.pallas_call(partial(backward_kernel, width, count, per_seq, first_plac...]
    ppermute x0 -> x20, waiting for transfers between devices: none -> 217 us  [swapped(): return lax.ppermute(array, axis, [(i, i ^ distance) for i in range(size)])]
    reshape x18 -> x0, local copies, waits for them, and re-layouts: 157 us -> none  [the longest x6 50.6 us: attend_head(): query_blocks = query_feat.reshape(blocks, block_size, -1)]
    all_gather x6 -> x0, waiting for transfers between devices: 126 us -> none  [the longest x2 114 us: on_device(): lax.all_gather(local_one, 'tensor', axis=0, tiled=True)]
    psum x1, waiting for transfers between devices: 347 us -> 251 us  [on_device(): lax.psum((qkv_grad, dense_grad, up_grad, down_grad, qkv_bias_grad, up_bia...]
    psum x2, blocking collectives: 63.7 us -> 124 us  [the longest x1 85.2 us: on_device(): lax.psum(tuple((jnp.stack([sums[l][j] for l in range(layers)]) for j in r...]
  transfers between devices with their start and end apart: 13 -> 21, of which waited for: 9 -> 8; matrix products, arithmetic and copies ran while one was open for 42% -> 18% of each run, Pallas kernels for 0% -> 6%
where the time goes in v1:
time: 1230 us
  waiting for transfers between devices  468 us (38%)
  Pallas kernels  262 us (21%)
  local copies, waits for them, and re-layouts  146 us (12%)
  blocking collectives  124 us (10%)
  other arithmetic  102 us (8%)
  matrix products  98.9 us (8%)
  between operations  15.5 us (1%)
    psum x1, waiting for transfers between devices, on_device(): lax.psum((qkv_grad, dense_grad, up_grad, down_grad, qkv_bias_grad, up_bia...  251 us
    ppermute x20, waiting for transfers between devices, swapped(): return lax.ppermute(array, axis, [(i, i ^ distance) for i in range(size)])  217 us
    pallas_call x2, Pallas kernels, backward_layer(): pl.pallas_call(partial(backward_kernel, width, count, per_seq, first_plac...  152 us
    pallas_call x2, Pallas kernels, forward_layer(): pl.pallas_call(partial(forward_kernel, width, count, per_seq, first_place...  110 us
    psum x1, blocking collectives, on_device(): lax.psum(tuple((jnp.stack([sums[l][j] for l in range(layers)]) for j in r...  85.2 us
    dot_general x2, matrix products, on_device(): in_weight_grad = lax.dot_general(xh, dz, TN, preferred_element_type=f32)  46.5 us
    psum x1, blocking collectives, on_device(): lax.psum((qkv_grad, dense_grad, up_grad, down_grad, qkv_bias_grad, up_bia...  38.5 us
    unnamed x123, local copies, waits for them, and re-layouts  37.8 us
  transfers between devices with their start and end apart: 21, of which 8 were waited for; matrix products, arithmetic and copies ran while one was open for 18% of the time, Pallas kernels for 6%

profile of v1, /device:TPU:0, one launch (start us, length us, event | category | flops | bytes accessed | tf_op | source)
XLA Modules:
  0.0 1225.5 jit_solution(11985312080711534358)
XLA Ops:
  11.1 4.7 fusion.89
  24.9 3.4 fusion.86
  28.3 5.9 copy.70.wf_ref
  34.4 4.7 fusion.88
  46.3 3.8 fusion.84
  50.0 4.5 copy.71.wo_ref
  58.9 4.5 broadcast.75.clone
  66.1 9.4 fusion.39
  84.0 54.7 %layer_forward.2 = (bf16[4096,1024]{1,0:T(8,128)(2,1)}, bf16[4096,768]{1,0:T(8,128)(2,1)}, bf16[4096,1280]{1,0:T(8,128)(2,1)}, bf16[4096,256]{1,0:T(8,128)(2,1)}...) custom-call(s32[2,4]{1,0:T(2,128)} %starts_ref.7, ...), custom_call_target="tpu_custom_call" | custom-call | flops 25769803776 | bytes 52428800 | tf_op jit(solution)/shard_map/layer_forward/pallas_call | solution.py:424
  138.7 4.7 dynamic-slice_bitcast_fusion.3
  143.4 7.5 collective-permute-done.3
  150.8 5.6 fusion.3
  162.4 46.4 %collective-permute-done.4 = bf16[1,1024,1024]{2,1,0:T(8,128)(2,1)} collective-permute-done((bf16[1,1024,1024]{2,1,0:T(8,128)(2,1)}, bf16[1,1024,1024]{2,1,0:T(8,128)(2,1)}, u32[]{:S(2)}, u32[]{:S(2)}) %collective-permute-start.4) | collective-permute-done | bytes 2097184 | tf_op jit(solution)/shard_map/ppermute | solution.py:530
  208.7 5.1 convert_reduce_fusion
  216.8 4.8 copy.96
  232.5 21.1 %collective-permute-done.10 = bf16[1024,1024]{1,0:T(8,128)(2,1)} collective-permute-done((bf16[1024,1024]{1,0:T(8,128)(2,1)}, bf16[1024,1024]{1,0:T(8,128)(2,1)}, u32[]{:S(2)}, u32[]{:S(2)}) %collective-permute-start.10) | collective-permute-done | bytes 2097184 | tf_op jit(solution)/shard_map/ppermute | solution.py:530
  254.2 43.6 %collective-permute-done.5 = bf16[1024,1024]{1,0:T(8,128)(2,1)} collective-permute-done((bf16[1024,1024]{1,0:T(8,128)(2,1)}, bf16[1024,1024]{1,0:T(8,128)(2,1)}, u32[]{:S(2)}, u32[]{:S(2)}) %collective-permute-start.5) | collective-permute-done | bytes 2097184 | tf_op jit(solution)/shard_map/ppermute | solution.py:530
  300.6 6.0 copy.76.wf_ref
  306.5 4.5 copy.77.wo_ref
  314.8 4.5 broadcast.75.clone.1
  329.7 4.3 broadcast.75.clone.2
  341.7 4.7 constant_dynamic-update-slice_fusion.4
  346.4 55.0 %layer_forward.3 = (bf16[4096,1024]{1,0:T(8,128)(2,1)}, bf16[4096,768]{1,0:T(8,128)(2,1)}, bf16[4096,1280]{1,0:T(8,128)(2,1)}, bf16[4096,256]{1,0:T(8,128)(2,1)}...) custom-call(s32[2,4]{1,0:T(2,128)} %starts_ref.7, ...), custom_call_target="tpu_custom_call" | custom-call | flops 25769803776 | bytes 52428800 | tf_op jit(solution)/shard_map/layer_forward/pallas_call | solution.py:424
  401.4 4.6 dynamic-slice_bitcast_fusion.2
  406.5 76.1 %layer_backward.2 = (bf16[4096,1792]{1,0:T(8,128)(2,1)}, bf16[4096,1024]{1,0:T(8,128)(2,1)}, f32[1,1792]{1,0:T(1,128)}) custom-call(s32[2,4]{1,0:T(2,128)} %starts_ref.7, bf16[4096,1024]{1,0:T(8,128)(2,1)} %get-tuple-element.153.bg_ref, bf16[1024,1280]{1,0:T(8,128)(2,1)} %get-tuple-element.132.wot_ref, bf16[1792,1024]{1,0:T(8,128)(2,1)} %get-tuple-element.128.wft_ref, ...), custom_call_target="tpu_custom_call" | custom-call | flops 25769803776 | bytes 58720256 | tf_op jit(solution)/shard_map/layer_backward/pallas_call | solution.py:482
  482.6 4.8 dynamic-slice_bitcast_fusion.1
  490.4 4.5 fusion.2
  495.5 5.2 fusion.1
  503.0 23.2 %fusion.96 = f32[1024,1792]{0,1:T(8,128)} fusion(bf16[4096,1024]{1,0:T(8,128)(2,1)} %get-tuple-element.48, bf16[4096,1792]{1,0:T(8,128)(2,1)} %get-tuple-element.49), kind=kOutput, calls=%fused_computation.199 | convolution fusion | flops 15032385536 | bytes 30408704 | tf_op jit(solution)/shard_map/dot_general | solution.py:662
  526.3 61.9 %collective-permute-done.14 = bf16[1,1024,1024]{2,1,0:T(8,128)(2,1)S(1)} collective-permute-done((bf16[1,1024,1024]{2,1,0:T(8,128)(2,1)}, bf16[1,1024,1024]{2,1,0:T(8,128)(2,1)S(1)}, u32[]{:S(2)}, u32[]{:S(2)}) %collective-permute-start.14) | collective-permute-done | bytes 2097184 | tf_op jit(solution)/shard_map/ppermute | solution.py:530
  591.8 6.7 convert_reduce_fusion.3
  598.9 17.1 %convolution_convert_fusion = bf16[1280,1024]{1,0:T(8,128)(2,1)S(1)} fusion(bf16[4096,1280]{1,0:T(8,128)(2,1)} %get-tuple-element.35.ca_ref, bf16[4096,1024]{1,0:T(8,128)(2,1)} %get-tuple-element.153.bg_ref), kind=kOutput, calls=%fused_computation.62 | convolution fusion | flops 10738728960 | bytes 21495808 | tf_op jit(solution)/shard_map/dot_general | solution.py:661
  616.0 29.8 %collective-permute-done.15 = bf16[1024,1024]{1,0:T(8,128)(2,1)S(1)} collective-permute-done((bf16[1024,1024]{1,0:T(8,128)(2,1)S(1)}, bf16[1024,1024]{1,0:T(8,128)(2,1)S(1)}, u32[]{:S(2)}, u32[]{:S(2)}) %collective-permute-start.15) | collective-permute-done | bytes 2097184 | tf_op jit(solution)/shard_map/ppermute | solution.py:530
  655.3 17.0 %convolution_convert_fusion.1 = bf16[1280,1024]{1,0:T(8,128)(2,1)S(1)} fusion(bf16[4096,1280]{1,0:T(8,128)(2,1)} %get-tuple-element.41.ca_ref, bf16[4096,1024]{1,0:T(8,128)(2,1)S(1)} %constant_dynamic-update-slice_fusion.bg_ref), kind=kOutput, calls=%fused_computation.63 | convolution fusion | flops 10738728960 | bytes 21495808 | tf_op jit(solution)/shard_map/dot_general | solution.py:661
  674.7 75.8 %layer_backward.3 = (bf16[4096,1792]{1,0:T(8,128)(2,1)}, bf16[4096,1024]{1,0:T(8,128)(2,1)}, f32[1,1792]{1,0:T(1,128)}) custom-call(s32[2,4]{1,0:T(2,128)} %starts_ref.7, bf16[4096,1024]{1,0:T(8,128)(2,1)} %copy-done.18, bf16[1024,1280]{1,0:T(8,128)(2,1)} %get-tuple-element.130.wot_ref, bf16[1792,1024]{1,0:T(8,128)(2,1)} %get-tuple-element.126.wft_ref, ...), custom_call_target="tpu_custom_call" | custom-call | flops 25769803776 | bytes 58720256 | tf_op jit(solution)/shard_map/layer_backward/pallas_call | solution.py:482
  751.9 23.3 %fusion.95 = f32[1024,1792]{0,1:T(8,128)} fusion(bf16[4096,1024]{1,0:T(8,128)(2,1)} %get-tuple-element.46, bf16[4096,1792]{1,0:T(8,128)(2,1)} %get-tuple-element.47), kind=kOutput, calls=%fused_computation.198 | convolution fusion | flops 15032385536 | bytes 30408704 | tf_op jit(solution)/shard_map/dot_general | solution.py:662
  775.3 4.1 fusion.38
  779.4 4.4 fusion.24
  787.0 6.8 collective-permute-done.18
  793.8 4.4 fusion
  804.4 85.2 %all-reduce = (f32[2,2,1024]{2,1,0:T(2,128)}, f32[2,2,1024]{2,1,0:T(2,128)}, f32[2,1024]{1,0:T(2,128)S(1)}) all-reduce(f32[2,2,1024]{2,1,0:T(2,128)S(1)} %pad_maximum_fusion.4, f32[2,2,1024]{2,1,0:T(2,128)S(1)} %pad_maximum_fusion.5, f32[2,1024]{1,0:T(2,128)S(1)} %pad_maximum_fusion.6), channel_id=1, replica_groups=mesh['dp'=8,'tensor'=4] {'dp','tensor'}, use_global_device_ids=true, to_apply=%region_13.14 | all-reduce | flops 10240 | bytes 81920 | tf_op jit(solution)/shard_map/psum | solution.py:702
  889.6 38.5 %all-reduce.1 = (bf16[1,768]{1,0:T(2,128)(2,1)S(1)}, bf16[1,768]{1,0:T(2,128)(2,1)S(1)}, bf16[1,1024]{1,0:T(2,128)(2,1)S(1)}, bf16[1,1024]{1,0:T(2,128)(2,1)S(1)}) all-reduce(bf16[1,768]{1,0:T(2,128)(2,1)S(1)} %stack.139, bf16[1,768]{1,0:T(2,128)(2,1)S(1)} %stack.138, ...), channel_id=1, replica_groups=mesh['dp'=8,'tensor'=4] {'dp'}, use_global_device_ids=true, to_apply=%region_22.23 | all-reduce | flops 3584 | bytes 14336 | tf_op jit(solution)/shard_map/psum | solution.py:682
  935.3 4.3 fusion.15
  939.6 251.3 %all-reduce.5.cloned.1.call-done = (bf16[1,1024,768]{1,2,0:T(8,128)(2,1)}, bf16[1,1024,768]{1,2,0:T(8,128)(2,1)}, bf16[1,256,1024]{2,1,0:T(8,128)(2,1)}, bf16[1,...) async-done(((bf16[1,1024,768]{1,2,0:T(8,128)(2,1)}, ...) | async-done | bytes 12582928 | tf_op jit(solution)/shard_map/psum | solution.py:682
  1190.8 6.2 maximum_convert_fusion
  1197.0 8.8 copy.86
  1205.8 5.7 maximum_convert_fusion.1
  1213.0 4.6 fusion.31
  (249 shorter events, 122.7 us)
Async XLA Ops:
  7.2 1183.6 %all-reduce.5.cloned.1.call-start = ((), (), s32[]{:S(2)}) async-start(), calls=%async_computation | async-start | bytes 25165824 | tf_op jit(solution)/shard_map/psum | solution.py:682
  7.2 51.1 %collective-permute-start = (bf16[1024,1024]{1,0:T(8,128)(2,1)}, bf16[1024,1024]{1,0:T(8,128)(2,1)}, u32[]{:S(2)}, u32[]{:S(2)}) collective-permute-start(bf16[1024,1024]{1,0:T(8,128)(2,1)} %param.19), channel_id=1, source_target_pairs={{0,2},{1,3},{2,0},{3,1},{4,6},{5,7},{6,4},{7,5},{8,10},{9,11},{10,... | collective-permute-start | bytes 6291464 | tf_op jit(solution)/shard_map/ppermute | solution.py:530
  10.3 68.3 %collective-permute-start.1 = (bf16[1024,1024]{1,0:T(8,128)(2,1)}, bf16[1024,1024]{1,0:T(8,128)(2,1)}, u32[]{:S(2)}, u32[]{:S(2)}) collective-permute-start(bf16[1024,1024]{1,0:T(8,128)(2,1)} %param.19), channel_id=1, source_target_pairs={{0,1},{1,0},{2,3},{3,2},{4,5},{5,4},{6,7},{7,6},{8,9},{9,8},{10,11... | collective-permute-start | bytes 6291464 | tf_op jit(solution)/shard_map/ppermute | solution.py:530
  11.0 7.7 copy-start.33
  11.1 11.8 copy-start.29
  11.1 212.6 %copy-start.35 = (f32[1,1,1024]{2,1,0:T(1,128)}, f32[1,1,1024]{2,1,0:T(1,128)S(1)}, u32[]{:S(2)}) copy-start(f32[1,1,1024]{2,1,0:T(1,128)S(1)} %get-tuple-element.148) | copy-start | bytes 12292
  11.1 215.9 %copy-start.31 = (f32[1,1,1024]{2,1,0:T(1,128)}, f32[1,1,1024]{2,1,0:T(1,128)S(1)}, u32[]{:S(2)}) copy-start(f32[1,1,1024]{2,1,0:T(1,128)S(1)} %get-tuple-element.147) | copy-start | bytes 12292
  50.0 8.2 copy-start.45
  50.0 8.9 copy-start.44
  58.3 23.3 %collective-permute-start.2 = (bf16[1024,1024]{1,0:T(8,128)(2,1)}, bf16[1024,1024]{1,0:T(8,128)(2,1)S(1)}, u32[]{:S(2)}, u32[]{:S(2)}) collective-permute-start(bf16[1024,1024]{1,0:T(8,128)(2,1)} %collective-permute-done), channel_id=1, source_target_pairs={{0,1},{1,0},{2,3},{3,2},{4,5},{5,4},{6,7},{7,6},{8,9},{9,8},{10,11... | collective-permute-start | bytes 6291464 | tf_op jit(solution)/shard_map/ppermute | solution.py:530
  143.3 7.5 collective-permute-start.3
  159.9 48.8 %collective-permute-start.4 = (bf16[1,1024,1024]{2,1,0:T(8,128)(2,1)}, bf16[1,1024,1024]{2,1,0:T(8,128)(2,1)}, u32[]{:S(2)}, u32[]{:S(2)}) collective-permute-start(bf16[1,1024,1024]{2,1,0:T(8,128)(2,1)} %constant_dynamic-slice_fusion.3), channel_id=1, source_target_pairs={{0,2},{1,3},{2,0},{3,1},{4,6},{5,7},{6,4},{7,5},{8,10},{9,11},{10,... | collective-permute-start | bytes 6291464 | tf_op jit(solution)/shard_map/ppermute | solution.py:530
  160.0 93.6 %collective-permute-start.10 = (bf16[1024,1024]{1,0:T(8,128)(2,1)}, bf16[1024,1024]{1,0:T(8,128)(2,1)}, u32[]{:S(2)}, u32[]{:S(2)}) collective-permute-start(bf16[1024,1024]{1,0:T(8,128)(2,1)} %param.31), channel_id=1, source_target_pairs={{0,2},{1,3},{2,0},{3,1},{4,6},{5,7},{6,4},{7,5},{8,10},{9,11},{10,... | collective-permute-start | bytes 6291464 | tf_op jit(solution)/shard_map/ppermute | solution.py:530
  162.3 51.5 %copy-start.27 = (f32[1024]{0:T(1024)}, f32[1024]{0:T(1024)S(1)}, u32[]{:S(2)}) copy-start(f32[1024]{0:T(1024)S(1)} %broadcast_multiply_fusion.2) | copy-start | bytes 12292
  213.9 83.9 %collective-permute-start.5 = (bf16[1024,1024]{1,0:T(8,128)(2,1)}, bf16[1024,1024]{1,0:T(8,128)(2,1)}, u32[]{:S(2)}, u32[]{:S(2)}) collective-permute-start(bf16[1024,1024]{1,0:T(8,128)(2,1)} %get-tuple-element.117), channel_id=1, source_target_pairs={{0,2},{1,3},{2,0},{3,1},{4,6},{5,7},{6,4},{7,5},{8,10},{9,11},{10,... | collective-permute-start | bytes 6291464 | tf_op jit(solution)/shard_map/ppermute | solution.py:530
  213.9 112.7 %collective-permute-start.11 = (bf16[1024,1024]{1,0:T(8,128)(2,1)}, bf16[1024,1024]{1,0:T(8,128)(2,1)}, u32[]{:S(2)}, u32[]{:S(2)}) collective-permute-start(bf16[1024,1024]{1,0:T(8,128)(2,1)} %param.31), channel_id=1, source_target_pairs={{0,1},{1,0},{2,3},{3,2},{4,5},{5,4},{6,7},{7,6},{8,9},{9,8},{10,11... | collective-permute-start | bytes 6291464 | tf_op jit(solution)/shard_map/ppermute | solution.py:530
  216.8 7.4 copy-start.8
  229.1 68.7 %copy-start.19 = (bf16[1,1024,1024]{1,2,0:T(8,128)(2,1)S(1)}, bf16[1,1024,1024]{1,2,0:T(8,128)(2,1)}, u32[]{:S(2)}) copy-start(bf16[1,1024,1024]{1,2,0:T(8,128)(2,1)} %copy.96) | copy-start | bytes 6291460
  229.1 68.7 %copy-start.23 = (bf16[1,256,1024]{1,2,0:T(8,128)(2,1)S(1)}, bf16[1,256,1024]{1,2,0:T(8,128)(2,1)}, u32[]{:S(2)}) copy-start(bf16[1,256,1024]{1,2,0:T(8,128)(2,1)} %copy.95) | copy-start | bytes 1572868
  253.7 88.0 %collective-permute-start.12 = (bf16[1024,1024]{1,0:T(8,128)(2,1)}, bf16[1024,1024]{1,0:T(8,128)(2,1)}, u32[]{:S(2)}, u32[]{:S(2)}) collective-permute-start(bf16[1024,1024]{1,0:T(8,128)(2,1)} %collective-permute-done.10), channel_id=1, source_target_pairs={{0,1},{1,0},{2,3},{3,2},{4,5},{5,4},{6,7},{7,6},{8,9},{9,8},{10,11... | collective-permute-start | bytes 6291464 | tf_op jit(solution)/shard_map/ppermute | solution.py:530
  253.7 86.5 %collective-permute-start.6 = (bf16[1024,1024]{1,0:T(8,128)(2,1)}, bf16[1024,1024]{1,0:T(8,128)(2,1)S(1)}, u32[]{:S(2)}, u32[]{:S(2)}) collective-permute-start(bf16[1024,1024]{1,0:T(8,128)(2,1)} %get-tuple-element.117), channel_id=1, source_target_pairs={{0,1},{1,0},{2,3},{3,2},{4,5},{5,4},{6,7},{7,6},{8,9},{9,8},{10,11... | collective-permute-start | bytes 6291464 | tf_op jit(solution)/shard_map/ppermute | solution.py:530
  297.8 43.9 %collective-permute-start.7 = (bf16[1024,1024]{1,0:T(8,128)(2,1)}, bf16[1024,1024]{1,0:T(8,128)(2,1)}, u32[]{:S(2)}, u32[]{:S(2)}) collective-permute-start(bf16[1024,1024]{1,0:T(8,128)(2,1)} %collective-permute-done.5), channel_id=1, source_target_pairs={{0,1},{1,0},{2,3},{3,2},{4,5},{5,4},{6,7},{7,6},{8,9},{9,8},{10,11... | collective-permute-start | bytes 6291464 | tf_op jit(solution)/shard_map/ppermute | solution.py:530
  406.0 84.5 %collective-permute-start.8 = (bf16[2,1024,1024]{2,1,0:T(8,128)(2,1)}, bf16[2,1024,1024]{2,1,0:T(8,128)(2,1)S(1)}, u32[]{:S(2)}, u32[]{:S(2)}) collective-permute-start(bf16[2,1024,1024]{2,1,0:T(8,128)(2,1)} %dynamic-slice_bitcast_fusion.2), channel_id=1, source_target_pairs={{0,1},{1,0},{2,3},{3,2},{4,5},{5,4},{6,7},{7,6},{8,9},{9,8},{10,11... | collective-permute-start | bytes 12582920 | tf_op jit(solution)/shard_map/ppermute | solution.py:530
  487.4 8.1 collective-permute-start.13
  488.0 7.5 slice-start
  495.1 96.7 %collective-permute-start.9 = (bf16[1,1024,1024]{2,1,0:T(8,128)(2,1)S(1)}, bf16[1,1024,1024]{2,1,0:T(8,128)(2,1)}, u32[]{:S(2)}, u32[]{:S(2)}) collective-permute-start(bf16[1,1024,1024]{2,1,0:T(8,128)(2,1)S(1)} %constant_dynamic-slice_fusion.2), channel_id=1, source_target_pairs={{0,2},{1,3},{2,0},{3,1},{4,6},{5,7},{6,4},{7,5},{8,10},{9,11},{10,... | collective-permute-start | bytes 6291464 | tf_op jit(solution)/shard_map/ppermute | solution.py:530
  502.2 85.9 %collective-permute-start.14 = (bf16[1,1024,1024]{2,1,0:T(8,128)(2,1)}, bf16[1,1024,1024]{2,1,0:T(8,128)(2,1)S(1)}, u32[]{:S(2)}, u32[]{:S(2)}) collective-permute-start(bf16[1,1024,1024]{2,1,0:T(8,128)(2,1)} %constant_dynamic-slice_fusion.1), channel_id=1, source_target_pairs={{0,2},{1,3},{2,0},{3,1},{4,6},{5,7},{6,4},{7,5},{8,10},{9,11},{10,... | collective-permute-start | bytes 6291464 | tf_op jit(solution)/shard_map/ppermute | solution.py:530
  598.5 49.7 %slice-start.2 = ((s8[7340032]{0:T(1024)(128)(4,1)}), s8[4194304]{0:T(1024)(128)(4,1)S(1)}, s32[]{:S(2)}) async-start(s8[7340032]{0:T(1024)(128)(4,1)} %bitcast.213), calls=%async_computation.3 | async-start | bytes 8388608
  598.5 17.5 %copy-start.37 = (f32[1,1792]{1,0:T(1,128)S(1)}, f32[1,1792]{1,0:T(1,128)}, u32[]{:S(2)}) copy-start(f32[1,1792]{1,0:T(1,128)} %get-tuple-element.51) | copy-start | bytes 21508
  598.5 49.7 %slice-start.3 = ((s8[7340032]{0:T(1024)(128)(4,1)}), s8[3145728]{0:T(1024)(128)(4,1)S(1)}, s32[]{:S(2)}) async-start(s8[7340032]{0:T(1024)(128)(4,1)} %bitcast.213), calls=%async_computation.4 | async-start | bytes 6291456
  598.5 47.3 %collective-permute-start.15 = (bf16[1024,1024]{1,0:T(8,128)(2,1)S(1)}, bf16[1024,1024]{1,0:T(8,128)(2,1)S(1)}, u32[]{:S(2)}, u32[]{:S(2)}) collective-permute-start(bf16[1024,1024]{1,0:T(8,128)(2,1)S(1)} %get-tuple-element.114), channel_id=1, source_target_pairs={{0,2},{1,3},{2,0},{3,1},{4,6},{5,7},{6,4},{7,5},{8,10},{9,11},{10,... | collective-permute-start | bytes 6291464 | tf_op jit(solution)/shard_map/ppermute | solution.py:530
  598.9 55.8 %collective-permute-start.16 = (bf16[1024,1024]{1,0:T(8,128)(2,1)S(1)}, bf16[1024,1024]{1,0:T(8,128)(2,1)S(1)}, u32[]{:S(2)}, u32[]{:S(2)}) collective-permute-start(bf16[1024,1024]{1,0:T(8,128)(2,1)S(1)} %get-tuple-element.114), channel_id=1, source_target_pairs={{0,1},{1,0},{2,3},{3,2},{4,5},{5,4},{6,7},{7,6},{8,9},{9,8},{10,11... | collective-permute-start | bytes 6291464 | tf_op jit(solution)/shard_map/ppermute | solution.py:530
  616.0 32.2 %copy-start.17 = (f32[768,1024]{1,0:T(8,128)S(1)}, f32[768,1024]{1,0:T(8,128)}, u32[]{:S(2)}) copy-start(f32[768,1024]{1,0:T(8,128)} %copy-done.16) | copy-start | bytes 9437188
  616.0 32.2 %copy-start.32 = (f32[1,1,1024]{2,1,0:T(1,128)S(1)}, f32[1,1,1024]{2,1,0:T(1,128)}, u32[]{:S(2)}) copy-start(f32[1,1,1024]{2,1,0:T(1,128)} %copy-done.31) | copy-start | bytes 12292
  645.9 9.2 collective-permute-start.17
  655.3 17.1 %copy-start.18 = (bf16[4096,1024]{1,0:T(8,128)(2,1)}, bf16[4096,1024]{1,0:T(8,128)(2,1)S(1)}, u32[]{:S(2)}) copy-start(bf16[4096,1024]{1,0:T(8,128)(2,1)S(1)} %constant_dynamic-update-slice_fusion.bg_ref) | copy-start | bytes 25165828
  751.9 23.3 %copy-start.15 = (f32[768,1024]{1,0:T(8,128)S(1)}, f32[768,1024]{1,0:T(8,128)}, u32[]{:S(2)}) copy-start(f32[768,1024]{1,0:T(8,128)} %copy-done.14) | copy-start | bytes 9437188
  751.9 23.3 %copy-start.30 = (f32[1,1,1024]{2,1,0:T(1,128)S(1)}, f32[1,1,1024]{2,1,0:T(1,128)}, u32[]{:S(2)}) copy-start(f32[1,1,1024]{2,1,0:T(1,128)} %copy-done.29) | copy-start | bytes 12292
  751.9 23.3 %copy-start.39 = (f32[1,1,1024]{2,1,0:T(1,128)S(1)}, f32[1,1,1024]{2,1,0:T(1,128)}, u32[]{:S(2)}) copy-start(f32[1,1,1024]{2,1,0:T(1,128)} %get-tuple-element.143) | copy-start | bytes 12292
  786.4 7.4 collective-permute-start.18
  801.7 130.6 %copy-start.1 = (bf16[1024,1024]{1,0:T(8,128)(2,1)S(1)}, bf16[1024,1024]{1,0:T(8,128)(2,1)}, u32[]{:S(2)}) copy-start(bf16[1024,1024]{1,0:T(8,128)(2,1)} %param.19) | copy-start | bytes 6291460
  801.7 130.6 %copy-start.28 = (f32[1024]{0:T(1024)S(1)}, f32[1024]{0:T(1024)}, u32[]{:S(2)}) copy-start(f32[1024]{0:T(1024)} %copy-done.27) | copy-start | bytes 12292
  801.7 127.6 %collective-permute-start.19 = (bf16[1,1024,1024]{2,1,0:T(8,128)(2,1)}, bf16[1,1024,1024]{2,1,0:T(8,128)(2,1)}, u32[]{:S(2)}, u32[]{:S(2)}) collective-permute-start(bf16[1,1024,1024]{2,1,0:T(8,128)(2,1)} %constant_dynamic-slice_fusion), channel_id=1, source_target_pairs={{0,2},{1,3},{2,0},{3,1},{4,6},{5,7},{6,4},{7,5},{8,10},{9,11},{10,... | collective-permute-start | bytes 6291464 | tf_op jit(solution)/shard_map/ppermute | solution.py:530
  889.6 328.1 %copy-start.46 = (f32[2,1024]{1,0:T(2,128)}, f32[2,1024]{1,0:T(2,128)S(1)}, u32[]{:S(2)}) copy-start(f32[2,1024]{1,0:T(2,128)S(1)} %get-tuple-element.178) | copy-start | bytes 24580
  1197.0 8.8 copy-start.22
  1205.8 7.2 copy-start.50
  1205.8 7.2 copy-start.51
  1205.8 7.2 copy-start.52
  (30 other events, 103.8 us)
Sparse Core Ops, SparseCore 0:
  783.9 406.8 all-reduce.4

commit v2 on v1

v2 whole, which is shorter than its diff:
```python
from functools import partial
import math

import numpy as np
import jax
import jax.numpy as jnp
from jax import lax
from jax.experimental import pallas as pl
from jax.experimental.pallas import tpu as pltpu
from jax.sharding import PartitionSpec as P

HS = 64
FEATS = 64
ROT = 16
PAIR = 2 * HS
SUB = 128
HIDDEN_CHUNK = 256
PARTS = 2

norm_eps = 1e-05
feature_scale = 0.75
rotary_base = 10000.0

f32 = jnp.float32
bf16 = jnp.bfloat16
NT = (((1,), (1,)), ((), ()))
TN = (((0,), (0,)), ((), ()))


def pair_order():
    half = ROT // 2
    rest = (HS - ROT) // 2
    order = []
    for side in range(2):
        for head in range(2):
            order += [(head, side * half + i) for i in range(half)]
        for head in range(2):
            order += [(head, ROT + side * rest + i) for i in range(rest)]
    return order


def column_order(heads):
    padded = heads + heads % 2
    width = padded * HS
    matrix = np.zeros((heads * 3 * HS, 3 * width), np.float32)
    order = pair_order()
    for pair in range(padded // 2):
        for lane, (side, entry) in enumerate(order):
            head = 2 * pair + side
            if head < heads:
                for part in range(2):
                    matrix[head * 3 * HS + part * HS + entry, part * width + pair * PAIR + lane] = 1
    for head in range(heads):
        for entry in range(HS):
            matrix[head * 3 * HS + 2 * HS + entry, 2 * width + head * HS + entry] = 1
    return matrix


def feature_matrix(group):
    rows = np.arange(FEATS)[:, None]
    cols = np.arange(HS)[None, :]
    table = np.cos(np.pi * (cols + 0.5) * rows / HS) * np.sqrt(2.0 / HS)
    table = table * np.where(rows == 0, np.sqrt(0.5), 1.0) * feature_scale
    matrix = np.zeros((group, group), np.float32)
    for pair in range(group // PAIR):
        for lane, (side, entry) in enumerate(pair_order()):
            start = pair * PAIR + side * FEATS
            matrix[pair * PAIR + lane, start : start + FEATS] = table[:, entry]
    return matrix


def rotary_tables(starts, length):
    places = jnp.arange(length, dtype=jnp.int32)
    started = starts[:, :, None] <= places[None, None, :]
    latest = jnp.max(jnp.where(started, starts[:, :, None], 0), axis=1)
    offsets = (places[None, :] - latest).reshape(1, -1).astype(f32)
    half = ROT // 2
    inverse = rotary_base ** (-(jnp.arange(half, dtype=f32) * 2.0 / ROT))
    angles = inverse[:, None] * offsets
    cos_lanes = np.zeros((half, PAIR), np.float32)
    sin_lanes = np.zeros((half, PAIR), np.float32)
    plain = np.zeros((1, PAIR), np.float32)
    for lane, (_, entry) in enumerate(pair_order()):
        if entry < ROT:
            cos_lanes[entry % half, lane] = 1.0
            sin_lanes[entry % half, lane] = -1.0 if entry < half else 1.0
        else:
            plain[0, lane] = 1.0

    def spread(table, lanes):
        return lax.dot_general(
            table, jnp.asarray(lanes), TN, precision=lax.Precision.HIGHEST
        )

    cosine = spread(jnp.cos(angles), cos_lanes) + jnp.asarray(plain)
    return cosine, spread(jnp.sin(angles), sin_lanes)


def dot(a, b):
    return jnp.dot(a, b, preferred_element_type=f32)


def dot_nt(a, b):
    return lax.dot_general(a, b, NT, preferred_element_type=f32)


def latest_start(starts_ref, seq, count, places):
    latest = jnp.zeros_like(places)
    for j in range(count):
        start = starts_ref[seq, j]
        latest = jnp.maximum(latest, jnp.where(start <= places, start, 0))
    return latest


def latest_scalar(starts_ref, seq, count, place):
    latest = jnp.int32(0)
    for j in range(count):
        start = starts_ref[seq, j]
        latest = jnp.maximum(latest, jnp.where(start <= place, start, 0))
    return latest


def block_masks(starts_ref, seq, count, place):
    rows = place + lax.broadcasted_iota(jnp.int32, (SUB, SUB), 0)
    cols = place + lax.broadcasted_iota(jnp.int32, (SUB, SUB), 1)
    latest_rows = latest_start(starts_ref, seq, count, rows)
    allowed = (cols <= rows) & (cols >= latest_rows)
    carried = (latest_rows <= place).astype(f32)
    following = latest_scalar(starts_ref, seq, count, place + SUB)
    feeding = (rows >= following).astype(f32)
    keeping = jnp.where(following <= place, 1.0, 0.0).astype(f32)
    return rows, cols, allowed, carried, feeding, keeping


def gelu_parts(hidden):
    share = 0.5 + 0.5 * lax.erf(hidden * math.sqrt(0.5))
    bell = jnp.exp(hidden * hidden * -0.5)
    return hidden * share, share + hidden * (bell * (1.0 / math.sqrt(2.0 * math.pi)))


def lane_halves():
    lane = lax.broadcasted_iota(jnp.int32, (SUB, PAIR), 1)
    low = (lane < HS).astype(f32).astype(bf16)
    return low, 1 - low


def pick_rows(seq, within, index, refs):
    values = []
    for one in refs:
        if len(one) == 1:
            values.append(one[0][...])
        else:
            values.append(jnp.where(within == index, one[0][...], one[1][...]))
    return jnp.where(seq == 0, values[0], values[1])


def place_rows(seq, within, index, rows, refs):
    if len(refs) == 1:
        refs[0][...] = rows
        return
    for side in range(2):
        for sent in range(2):

            @pl.when((seq == side) & ((within == index) == (sent == 0)))
            def _():
                refs[2 * side + sent][...] = rows


def forward_kernel(
    count,
    blocks_per_seq,
    first_place,
    shapes,
    starts_ref,
    index_ref,
    *refs,
):
    ways, rest = shapes
    sources = (refs[: ways[0]], refs[ways[0] : sum(ways)])
    outs = refs[sum(ways) + 16 : sum(ways) + 16 + rest]
    forward_body(
        count,
        blocks_per_seq,
        first_place,
        starts_ref,
        index_ref[0],
        sources,
        outs,
        *refs[sum(ways) : sum(ways) + 16],
        *refs[sum(ways) + 16 + rest :],
    )


def forward_body(
    count,
    blocks_per_seq,
    first_place,
    starts_ref,
    index,
    sources,
    outs,
    wq_ref,
    bq_ref,
    wu_ref,
    bu_ref,
    wo_ref,
    dct_ref,
    cos_ref,
    sin_ref,
    state_in_ref,
    xh_ref,
    qkv_ref,
    ca_ref,
    rden_ref,
    gp_ref,
    states_ref,
    state_out_ref,
    state_ref,
):
    step = pl.program_id(0)
    seq = step // blocks_per_seq
    within = lax.rem(step, blocks_per_seq)
    rows = sources[0][0].shape[0]
    inner = wu_ref.shape[1]
    width = wo_ref.shape[0] - inner
    pairs = width // PAIR
    group = dct_ref.shape[0]

    @pl.when(within == 0)
    def _():
        state_ref[...] = state_in_ref[0]

    x = pick_rows(seq, within, index, sources).astype(f32)
    center = jnp.mean(x, axis=-1, keepdims=True)
    shifted = x - center
    spread = jnp.mean(shifted * shifted, axis=-1, keepdims=True)
    xh = (shifted * lax.rsqrt(spread + norm_eps)).astype(bf16)
    xh_ref[...] = xh

    cosine = cos_ref[...]
    sine = sin_ref[...]
    dct = dct_ref[...]
    mixed = dot(xh, wq_ref[...]) + bq_ref[...]
    for start in range(0, 2 * width, group):
        turned = []
        for lane in range(start, start + group, PAIR):
            tile = mixed[:, lane : lane + PAIR]
            turned.append((tile * cosine + pltpu.roll(tile, HS, 1) * sine).astype(bf16))
        turned = turned[0] if len(turned) == 1 else jnp.concatenate(turned, axis=1)
        qkv_ref[:, start : start + group] = jnp.exp(dot(turned, dct)).astype(bf16)
    qkv_ref[:, 2 * width :] = mixed[:, 2 * width :].astype(bf16)

    low_lanes = lax.broadcasted_iota(jnp.int32, (SUB, PAIR), 1) < HS
    low, high = lane_halves()
    ones = jnp.ones((SUB, PAIR), bf16)
    active, slope = gelu_parts(dot(xh, wu_ref[...]) + bu_ref[...])
    ca_ref[:, width:] = active.astype(bf16)
    gp_ref[...] = slope.astype(bf16)

    for sub in range(rows // SUB):
        place = first_place + within * rows + sub * SUB
        _, _, allowed, carried, feeding, keeping = block_masks(starts_ref, seq, count, place)
        carried = carried.astype(bf16)
        feeding = feeding.astype(bf16)
        at = slice(sub * SUB, (sub + 1) * SUB)
        for pair in range(pairs):
            lanes = slice(pair * PAIR, (pair + 1) * PAIR)
            q = qkv_ref[at, pair * PAIR : (pair + 1) * PAIR]
            k = qkv_ref[at, width + pair * PAIR : width + (pair + 1) * PAIR]
            v = qkv_ref[at, 2 * width + pair * PAIR : 2 * width + (pair + 1) * PAIR]
            q0, q1 = q * low, q * high
            qs = jnp.concatenate([q0, q1], axis=0)
            scores = dot_nt(qs, k)
            weights = [
                jnp.where(allowed, scores[:SUB], 0.0).astype(bf16),
                jnp.where(allowed, scores[SUB:], 0.0).astype(bf16),
            ]
            state = state_ref[pair * PAIR : (pair + 1) * PAIR, :]
            state_low = state.astype(bf16)
            first = (sub * pairs + pair) * PAIR
            states_ref[first : first + PAIR, :] = state_low
            left = jnp.concatenate(
                [
                    jnp.concatenate([weights[0], q0 * carried], axis=1),
                    jnp.concatenate([weights[1], q1 * carried], axis=1),
                ],
                axis=0,
            )
            valued = jnp.concatenate([v, ones], axis=1)
            both = dot(left, jnp.concatenate([valued, state_low], axis=0))
            numerator = jnp.where(low_lanes, both[:SUB, :PAIR], both[SUB:, :PAIR])
            denominator = jnp.where(low_lanes, both[:SUB, PAIR:], both[SUB:, PAIR:])
            inverse = 1.0 / denominator
            ca_ref[at, lanes] = (numerator * inverse).astype(bf16)
            rden_ref[at, lanes] = inverse.astype(bf16)
            added = lax.dot_general(k * feeding, valued, TN, preferred_element_type=f32)
            state_ref[pair * PAIR : (pair + 1) * PAIR, :] = keeping * state + added

    out = dot(ca_ref[...], wo_ref[...]).astype(bf16)
    place_rows(seq, within, index, out, outs)

    @pl.when(within == blocks_per_seq - 1)
    def _():
        state_out_ref[0] = state_ref[...]


def backward_kernel(
    count,
    blocks_per_seq,
    first_place,
    shapes,
    starts_ref,
    index_ref,
    *refs,
):
    ways, rest = shapes
    sources = (refs[: ways[0]], refs[ways[0] : sum(ways)])
    outs = refs[sum(ways) + 15 : sum(ways) + 15 + rest]
    backward_body(
        count,
        blocks_per_seq,
        first_place,
        starts_ref,
        index_ref[0],
        sources,
        outs,
        *refs[sum(ways) : sum(ways) + 15],
        *refs[sum(ways) + 15 + rest :],
    )


def backward_body(
    count,
    blocks_per_seq,
    first_place,
    starts_ref,
    index,
    sources,
    outs,
    wq_ref,
    wu_ref,
    wo_ref,
    dctt_ref,
    cos_ref,
    sin_ref,
    state_in_ref,
    qkv_ref,
    ca_ref,
    rden_ref,
    gp_ref,
    states_ref,
    dz_ref,
    db_ref,
    state_out_ref,
    state_ref,
    dqk_ref,
    split_ref,
    dnum_ref,
):
    step = pl.program_id(0)
    blocks = pl.num_programs(0)
    seq = (blocks - 1 - step) // blocks_per_seq
    within = lax.rem(blocks - 1 - step, blocks_per_seq)
    rows = sources[0][0].shape[0]
    inner = wu_ref.shape[1]
    width = wo_ref.shape[0] - inner
    pairs = width // PAIR
    group = dctt_ref.shape[0]

    @pl.when(within == blocks_per_seq - 1)
    def _():
        state_ref[...] = state_in_ref[0]

    @pl.when(step == 0)
    def _():
        db_ref[...] = jnp.zeros_like(db_ref)

    bg = pick_rows(seq, within, index, sources)
    context_grad = dot_nt(bg, wo_ref[:width, :])

    low_rows = lax.broadcasted_iota(jnp.int32, (rows, PAIR), 1) < HS
    low_lanes = lax.broadcasted_iota(jnp.int32, (SUB, PAIR), 1) < HS
    low, high = lane_halves()
    ones = jnp.ones((SUB, PAIR), bf16)
    zeros = jnp.zeros((SUB, PAIR), bf16)
    sum_rows = lax.broadcasted_iota(jnp.int32, (2 * PAIR, 2 * PAIR), 0)
    sum_cols = lax.broadcasted_iota(jnp.int32, (2 * PAIR, 2 * PAIR), 1)
    same_head = (lax.rem(sum_rows, PAIR) // HS) == (sum_cols // PAIR)
    summing = jnp.where(same_head, -1.0 / HS, 0.0).astype(bf16)

    for pair in range(pairs):
        lanes = slice(pair * PAIR, (pair + 1) * PAIR)
        scaled = context_grad[:, lanes] * rden_ref[:, lanes].astype(f32)
        dnum_ref[:, lanes] = scaled.astype(bf16)
        product = scaled * ca_ref[:, lanes].astype(f32)
        product_high = product.astype(bf16)
        product_low = (product - product_high.astype(f32)).astype(bf16)
        dden = dot(jnp.concatenate([product_high, product_low], axis=1), summing)
        for side in range(2):
            part = dden[:, side * PAIR : (side + 1) * PAIR]
            top = part.astype(bf16).astype(f32)
            split = jnp.where(low_rows, part, part - top).astype(bf16)
            split_ref[:, (2 * pair + side) * PAIR : (2 * pair + side + 1) * PAIR] = split

    subs = rows // SUB
    chunk = min(inner, HIDDEN_CHUNK)
    chunks = inner // chunk
    done = 0

    def hidden_chunk(j):
        at = slice(j * chunk, (j + 1) * chunk)
        active_grad = dot_nt(bg, wo_ref[width + j * chunk : width + (j + 1) * chunk, :])
        grad = (active_grad * gp_ref[:, at].astype(f32)).astype(bf16)
        dz_ref[:, 3 * width + j * chunk : 3 * width + (j + 1) * chunk] = grad

    for sub in reversed(range(subs)):
        while done < (subs - sub) * chunks // subs:
            hidden_chunk(done)
            done += 1
        place = first_place + within * rows + sub * SUB
        rows_at, cols_at, allowed, carried, feeding, keeping = block_masks(
            starts_ref, seq, count, place
        )
        latest_cols = latest_start(starts_ref, seq, count, cols_at)
        flipped = (rows_at <= cols_at) & (rows_at >= latest_cols)
        carried_low = carried.astype(bf16)
        at = slice(sub * SUB, (sub + 1) * SUB)
        items = [dict(pair=pair) for pair in range(pairs)]
        for it in items:
            pair = it["pair"]
            it["q"] = qkv_ref[at, pair * PAIR : (pair + 1) * PAIR]
            it["k"] = qkv_ref[at, width + pair * PAIR : width + (pair + 1) * PAIR]
            it["v"] = qkv_ref[at, 2 * width + pair * PAIR : 2 * width + (pair + 1) * PAIR]
            it["dnum"] = dnum_ref[at, pair * PAIR : (pair + 1) * PAIR]
            it["split"] = [
                split_ref[at, (2 * pair + side) * PAIR : (2 * pair + side + 1) * PAIR]
                for side in range(2)
            ]
            first = (sub * pairs + pair) * PAIR
            it["state"] = states_ref[first : first + PAIR, :]
            it["later"] = state_ref[pair * PAIR : (pair + 1) * PAIR, :]
            it["later_low"] = it["later"].astype(bf16)
        for it in items:
            it["xs"] = jnp.concatenate(
                [
                    jnp.concatenate([it["dnum"] * low, it["split"][0]], axis=1),
                    jnp.concatenate([it["dnum"] * high, it["split"][1]], axis=1),
                ],
                axis=0,
            )
            valued = jnp.concatenate([it["v"], ones], axis=1)
            it["ahead"] = dot_nt(it["xs"], jnp.concatenate([valued, it["state"]], axis=0))
        for it in items:
            back = []
            for side, mask in enumerate((low, high)):
                back.append(
                    dot_nt(
                        jnp.concatenate([it["v"] * mask, ones], axis=1),
                        jnp.concatenate(
                            [
                                jnp.concatenate([it["dnum"], it["split"][side]], axis=1),
                                it["later_low"],
                            ],
                            axis=0,
                        ),
                    )
                )
            it["back"] = back
        for it in items:
            ks = jnp.concatenate([it["k"] * low, it["k"] * high], axis=0)
            it["q_turned"] = jnp.transpose(it["q"])
            it["over"] = dot(
                ks, jnp.concatenate([it["q_turned"], it["later_low"][:, :PAIR]], axis=1)
            )
        for it in items:
            qc = it["q"] * carried_low
            qs = jnp.concatenate([qc * low, qc * high], axis=0)
            added = lax.dot_general(qs, it["xs"], TN, preferred_element_type=f32)
            pair = it["pair"]
            state_ref[pair * PAIR : (pair + 1) * PAIR, :] = keeping * it["later"] + added
        for it in items:
            dscores = jnp.concatenate(
                [
                    jnp.where(allowed, it["ahead"][:SUB, :SUB], 0.0).astype(bf16),
                    jnp.where(allowed, it["ahead"][SUB:, :SUB], 0.0).astype(bf16),
                ],
                axis=0,
            )
            it["dq"] = dot(dscores, it["k"])
        for it in items:
            left = jnp.concatenate(
                [
                    jnp.concatenate(
                        [
                            jnp.where(flipped, it["back"][side][:, :SUB], 0.0).astype(bf16),
                            jnp.where(
                                flipped, it["over"][side * SUB : (side + 1) * SUB, :SUB], 0.0
                            ).astype(bf16),
                        ],
                        axis=1,
                    )
                    for side in range(2)
                ],
                axis=0,
            )
            right = jnp.concatenate(
                [
                    jnp.concatenate([it["q"], zeros], axis=1),
                    jnp.concatenate([zeros, it["dnum"]], axis=1),
                ],
                axis=0,
            )
            it["both"] = dot(left, right)
        for it in items:
            pair = it["pair"]
            dq, ahead, both, back, over = (
                it["dq"],
                it["ahead"],
                it["both"],
                it["back"],
                it["over"],
            )
            dq = (
                jnp.where(low_lanes, dq[:SUB], dq[SUB:])
                + jnp.where(low_lanes, ahead[:SUB, SUB:], ahead[SUB:, SUB:]) * carried
            )
            dk = (
                jnp.where(low_lanes, both[:SUB, :PAIR], both[SUB:, :PAIR])
                + jnp.where(low_lanes, back[0][:, SUB:], back[1][:, SUB:]) * feeding
            )
            dv = (
                jnp.where(low_lanes, both[:SUB, PAIR:], both[SUB:, PAIR:])
                + jnp.where(low_lanes, over[:SUB, SUB:], over[SUB:, SUB:]) * feeding
            )
            dqk_ref[at, pair * PAIR : (pair + 1) * PAIR] = (dq * it["q"].astype(f32)).astype(bf16)
            dqk_ref[at, width + pair * PAIR : width + (pair + 1) * PAIR] = (
                dk * it["k"].astype(f32)
            ).astype(bf16)
            dz_ref[at, 2 * width + pair * PAIR : 2 * width + (pair + 1) * PAIR] = dv.astype(bf16)

    cosine = cos_ref[...]
    sine = sin_ref[...]
    dctt = dctt_ref[...]
    for start in range(0, 2 * width, group):
        turned = dot(dqk_ref[:, start : start + group], dctt)
        for lane in range(0, group, PAIR):
            tile = turned[:, lane : lane + PAIR]
            back = tile * cosine - pltpu.roll(tile, HS, 1) * sine
            dz_ref[:, start + lane : start + lane + PAIR] = back.astype(bf16)

    dx = dot_nt(dz_ref[:, 3 * width :], wu_ref[...]) + dot_nt(dz_ref[:, : 3 * width], wq_ref[...])
    place_rows(seq, within, index, dx.astype(bf16), outs)
    db_ref[...] += jnp.sum(dz_ref[...].astype(f32), axis=0, keepdims=True)

    @pl.when(within == 0)
    def _():
        state_out_ref[0] = state_ref[...]


def out_weight_kernel(parts, steps, ways, index_ref, *refs):
    lefts = refs[:parts]
    rights, at = [], parts
    for count in ways:
        rights.append(refs[at : at + count])
        at += count
    grad_ref, total_ref = refs[at:]
    step = pl.program_id(0)
    per_part = steps // parts
    per_side = per_part // 2
    index = index_ref[0]

    @pl.when(step == 0)
    def _():
        total_ref[...] = jnp.zeros_like(total_ref)

    for part in range(parts):
        for side in range(2):
            first = part * per_part + side * per_side
            blocks = rights[2 * part + side]

            @pl.when((step >= first) & (step < first + per_side))
            def _():
                right = blocks[0][...]
                if len(blocks) == 2:
                    right = jnp.where(step - first == index, right, blocks[1][...])
                total_ref[...] += lax.dot_general(
                    lefts[part][...], right, TN, preferred_element_type=f32
                )

    @pl.when(step == steps - 1)
    def _():
        grad_ref[...] = total_ref[...].astype(bf16)


def in_weight_kernel(parts, steps, pieces, *refs):
    lefts, rights = refs[:parts], refs[parts : 2 * parts]
    db_ref, gains_ref, wq_ref, wu_ref = refs[2 * parts : 2 * parts + 4]
    grad_refs = refs[2 * parts + 4 : 2 * parts + 4 + pieces]
    sums_ref, total_ref = refs[2 * parts + 4 + pieces :]
    step = pl.program_id(0)
    per_part = steps // parts

    @pl.when(step == 0)
    def _():
        total_ref[...] = jnp.zeros_like(total_ref)

    for part in range(parts):

        @pl.when((step >= part * per_part) & (step < (part + 1) * per_part))
        def _():
            total_ref[...] += lax.dot_general(
                lefts[part][...], rights[part][...], TN, preferred_element_type=f32
            )

    @pl.when(step == steps - 1)
    def _():
        split = wq_ref.shape[1]
        rows = 128
        lane = lax.broadcasted_iota(jnp.int32, (rows, 128), 1)
        per_piece = total_ref.shape[0] // pieces
        for piece, grad_ref in enumerate(grad_refs):

            @pl.loop(0, per_piece // rows)
            def _(block):
                inside = pl.ds(pl.multiple_of(block * rows, rows), rows)
                at = pl.ds(pl.multiple_of(piece * per_piece + block * rows, rows), rows)
                columns = gains_ref[at, :]
                sums = jnp.zeros((rows, 128), f32)
                for j, (weight_ref, cols) in enumerate(
                    ((wq_ref, slice(0, split)), (wu_ref, slice(split, None)))
                ):
                    gain, shift = columns[:, j : j + 1], columns[:, 2 + j : 3 + j]
                    total = total_ref[at, cols]
                    bias = db_ref[:, cols]
                    weight = weight_ref[at, :].astype(f32)
                    grad_ref[inside, cols] = (gain * total + shift * bias).astype(bf16)
                    sums = sums + jnp.where(
                        lane == j, jnp.sum(weight * total, axis=1, keepdims=True), 0.0
                    )
                    sums = sums + jnp.where(
                        lane == 2 + j, jnp.sum(weight * bias, axis=1, keepdims=True), 0.0
                    )
                sums_ref[at, :] = sums


def with_token(kernel, inputs, waits):
    def body(*refs):
        outputs = refs[inputs + waits :]
        token_at = kernel.token
        outputs[token_at][...] = jnp.zeros_like(outputs[token_at])
        kernel.run(*refs[:inputs], *outputs[:token_at], *outputs[token_at + 1 :])

    return body


class Timed:
    def __init__(self, run, token):
        self.run = run
        self.token = token


class Order:
    def __init__(self):
        self.before = []
        self.token = None

    def after(self, array):
        if self.token is None:
            return array
        return array + self.token.astype(array.dtype).reshape((1,) * array.ndim)

    def call(self, run, scalars, operands, specs, out_specs, out_shape, **options):
        waits, self.before = self.before, []
        token_spec = pl.BlockSpec((1, 1), lambda i, *_: (0, 0))
        body = with_token(Timed(run, len(out_shape)), len(scalars) + len(operands), len(waits))
        *results, token = pl.pallas_call(
            body,
            grid_spec=pltpu.PrefetchScalarGridSpec(
                num_scalar_prefetch=len(scalars),
                grid=options.pop("grid"),
                in_specs=list(specs) + [pl.BlockSpec(memory_space=pl.ANY)] * len(waits),
                out_specs=list(out_specs) + [token_spec],
                scratch_shapes=options.pop("scratch_shapes", []),
            ),
            out_shape=list(out_shape) + [jax.ShapeDtypeStruct((1, 1), f32)],
            compiler_params=pltpu.CompilerParams(vmem_limit_bytes=56 * 1024 * 1024),
            cost_estimate=pl.CostEstimate(flops=0, bytes_accessed=0, transcendentals=0),
            **options,
        )(*scalars, *operands, *waits)
        self.token = token
        return results

    def mark(self, *arrays):
        self.before += arrays
        self.call(lambda *refs: None, [], [], [], [], [], grid=(1,), name="mark")


def whole_spec(array):
    return pl.BlockSpec(array.shape, lambda i, *_: (0,) * array.ndim)


def row_spec(block, cols, first, last, offset=0):
    return pl.BlockSpec((block, cols), lambda i, *_: (jnp.clip(i, first, last) - first + offset, 0))


def split_rows(source):
    return not isinstance(source[1], int)


def row_sources(sources, block, per_seq, step_of):
    arrays, specs, ways = [], [], []
    for side, source in enumerate(sources):
        first = side * per_seq
        model = source[0].shape[1]
        if split_rows(source):
            arrays += source
            specs += [pl.BlockSpec((block, model), lambda i, *_: (0, 0))] * 2
            ways.append(2)
        else:
            arrays.append(source[0])
            specs.append(
                pl.BlockSpec(
                    (block, model),
                    lambda i, *_, first=first, offset=source[1]: (
                        jnp.clip(step_of(i), first, first + per_seq - 1) - first + offset,
                        0,
                    ),
                )
            )
            ways.append(1)
    return arrays, specs, tuple(ways)


def row_outs(block, model, blocks, split, step_of):
    if split == 1:
        return [pl.BlockSpec((block, model), lambda i, *_: (step_of(i), 0))]
    return [pl.BlockSpec((block, model), lambda i, *_: (0, 0))] * 4


def forward_layer(when, own, other, starts, index, weights, dct, cosine, sine, state_in, part, parts, block):
    wq, bq, wu, bu, wo = weights
    model = wq.shape[0]
    seqs, count = starts.shape
    length = cosine.shape[0] // seqs // parts
    rows = length * seqs
    hidden = wu.shape[1]
    width = wo.shape[0] - hidden
    pairs = width // PAIR
    per_seq = length // block
    blocks = per_seq * seqs
    by_rows = lambda cols: pl.BlockSpec((block, cols), lambda i, *_: (i, 0))
    table = pl.BlockSpec(
        (block, PAIR),
        lambda i, *_: ((i // per_seq) * per_seq * parts + part * per_seq + lax.rem(i, per_seq), 0),
    )
    state_spec = pl.BlockSpec((1, pairs * PAIR, 2 * PAIR), lambda i, *_: (i // per_seq, 0, 0))
    state_rows = block // SUB * pairs * PAIR
    sources, source_specs, ways = row_sources((own, other), block, per_seq, lambda i: i)
    outs = row_outs(block, model, blocks, len(own) if split_rows(own) else 1, lambda i: i)
    return when.call(
        partial(forward_kernel, count, per_seq, part * length, (ways, len(outs))),
        [starts, index],
        [*sources, *weights, dct, cosine, sine, state_in],
        source_specs
            + [whole_spec(w) for w in (*weights, dct)]
            + [table, table, state_spec],
        [
                by_rows(model),
                by_rows(3 * width),
                by_rows(width + hidden),
                by_rows(width),
                by_rows(hidden),
                pl.BlockSpec((state_rows, 2 * PAIR), lambda i, *_: (i, 0)),
                state_spec,
                *outs,
            ],
        [
            jax.ShapeDtypeStruct((rows, model), bf16),
            jax.ShapeDtypeStruct((rows, 3 * width), bf16),
            jax.ShapeDtypeStruct((rows, width + hidden), bf16),
            jax.ShapeDtypeStruct((rows, width), bf16),
            jax.ShapeDtypeStruct((rows, hidden), bf16),
            jax.ShapeDtypeStruct((blocks * state_rows, 2 * PAIR), bf16),
            jax.ShapeDtypeStruct((seqs, pairs * PAIR, 2 * PAIR), f32),
            *[jax.ShapeDtypeStruct((rows // len(outs), model), bf16) for _ in outs],
        ],
        grid=(blocks,),
        scratch_shapes=[pltpu.VMEM((pairs * PAIR, 2 * PAIR), f32)],
        name="forward_layer",
    )


def backward_layer(
    when, own, other, starts, index, weights, dctt, cosine, sine, state_in, saved, part, parts, block
):
    wq, _, wu, _, wo = weights
    weights = (wq, wu, wo)
    model = wq.shape[0]
    seqs, count = starts.shape
    length = cosine.shape[0] // seqs // parts
    rows = length * seqs
    hidden = wu.shape[1]
    width = wo.shape[0] - hidden
    span = 3 * width + hidden
    pairs = width // PAIR
    per_seq = length // block
    blocks = per_seq * seqs
    by_rows = lambda cols: pl.BlockSpec((block, cols), lambda i, *_: (blocks - 1 - i, 0))

    def table_index(i, *_):
        at = blocks - 1 - i
        return (at // per_seq) * per_seq * parts + part * per_seq + lax.rem(at, per_seq), 0

    table = pl.BlockSpec((block, PAIR), table_index)
    state_spec = pl.BlockSpec(
        (1, pairs * PAIR, 2 * PAIR), lambda i, *_: ((blocks - 1 - i) // per_seq, 0, 0)
    )
    state_rows = block // SUB * pairs * PAIR
    back = lambda i: blocks - 1 - i
    sources, source_specs, ways = row_sources((own, other), block, per_seq, back)
    outs = row_outs(block, model, blocks, len(own) if split_rows(own) else 1, back)
    return when.call(
        partial(backward_kernel, count, per_seq, part * length, (ways, len(outs))),
        [starts, index],
        [*sources, *weights, dctt, cosine, sine, state_in, *saved],
        source_specs
            + [whole_spec(w) for w in (*weights, dctt)]
            + [
                table,
                table,
                state_spec,
                by_rows(3 * width),
                by_rows(width + hidden),
                by_rows(width),
                by_rows(hidden),
                pl.BlockSpec((state_rows, 2 * PAIR), lambda i, *_: (blocks - 1 - i, 0)),
            ],
        [
                by_rows(span),
                pl.BlockSpec((1, span), lambda i, *_: (0, 0)),
                state_spec,
                *outs,
            ],
        [
            jax.ShapeDtypeStruct((rows, span), bf16),
            jax.ShapeDtypeStruct((1, span), f32),
            jax.ShapeDtypeStruct((seqs, pairs * PAIR, 2 * PAIR), f32),
            *[jax.ShapeDtypeStruct((rows // len(outs), model), bf16) for _ in outs],
        ],
        grid=(blocks,),
        scratch_shapes=[
                pltpu.VMEM((pairs * PAIR, 2 * PAIR), f32),
                pltpu.VMEM((block, 2 * width), bf16),
                pltpu.VMEM((block, 2 * width), bf16),
                pltpu.VMEM((block, width), bf16),
            ],
        name="backward_layer",
    )


def out_weight_grad(when, cas, grads, index, length, block):
    parts = len(cas)
    per_side = length // block
    per_part = 2 * per_side
    steps = per_part * parts
    inner, model = cas[0].shape[1], grads[0][0][0].shape[1]
    rights, right_specs, ways = [], [], ()
    for p, pair in enumerate(grads):
        arrays, specs, count = row_sources(
            pair, block, per_side, lambda i, p=p: jnp.clip(i - p * per_part, 0, per_part - 1)
        )
        rights += arrays
        right_specs += specs
        ways += count
    return when.call(
        partial(out_weight_kernel, parts, steps, ways),
        [index],
        [*cas, *rights],
        [row_spec(block, inner, p * per_part, (p + 1) * per_part - 1) for p in range(parts)]
        + right_specs,
        [pl.BlockSpec((inner, model), lambda i, *_: (0, 0))],
        [jax.ShapeDtypeStruct((inner, model), bf16)],
        grid=(steps,),
        scratch_shapes=[pltpu.VMEM((inner, model), f32)],
        name="out_weight_grad",
    )


def in_weight_grad(when, xhs, dzs, db, columns, wq, wu, block, pieces):
    parts = len(xhs)
    per_part = xhs[0].shape[0] // block
    steps = per_part * parts
    model, span = xhs[0].shape[1], dzs[0].shape[1]
    rows_of = lambda cols: [
        row_spec(block, cols, p * per_part, (p + 1) * per_part - 1) for p in range(parts)
    ]
    per_piece = model // pieces
    return when.call(
        partial(in_weight_kernel, parts, steps, pieces),
        [],
        [*xhs, *dzs, db, columns, wq, wu],
        rows_of(model) + rows_of(span) + [whole_spec(a) for a in (db, columns, wq, wu)],
        [pl.BlockSpec((per_piece, span), lambda i, *_: (0, 0))] * pieces
        + [pl.BlockSpec((model, 128), lambda i, *_: (0, 0))],
        [jax.ShapeDtypeStruct((per_piece, span), bf16)] * pieces
        + [jax.ShapeDtypeStruct((model, 128), f32)],
        grid=(steps,),
        scratch_shapes=[pltpu.VMEM((model, span), f32)],
        name="in_weight_grad",
    )


def swapped(array, axis, distance):
    size = lax.axis_size(axis)
    return lax.ppermute(array, axis, [(i, i ^ distance) for i in range(size)])


def distances(size):
    return [1 << b for b in range(size.bit_length() - 1)]


def bit_of(axis, distance):
    return (lax.axis_index(axis) // distance) % 2


def joined(array, axis, distance):
    partner = swapped(array, axis, distance)
    upper = bit_of(axis, distance) == 1
    return jnp.concatenate(
        [jnp.where(upper, partner, array), jnp.where(upper, array, partner)], axis=0
    )


def gather_inner(rows, inner):
    for distance in distances(inner):
        rows = joined(rows, "tensor", distance)
    return rows


def inner_source(rows, inner):
    if inner == 2:
        return (rows, swapped(rows, "tensor", 1))
    return (gather_inner(rows, inner), 0)


def reduce_start(partial_sums, inner, when):
    if len(partial_sums) == 4:
        keep0, send0, keep1, send1 = partial_sums
        when.before += [send0, send1]
        return [keep0, keep1], [swapped(send0, "tensor", 1), swapped(send1, "tensor", 1)]
    model = partial_sums[0].shape[1]
    share = partial_sums[0].shape[0] // (2 * inner)
    now = [half.reshape(inner, share, model) for half in jnp.split(partial_sums[0], 2)]
    for distance in reversed(distances(inner)):
        half = now[0].shape[0] // 2
        bit = bit_of("tensor", distance)
        keep = [lax.dynamic_slice_in_dim(one, bit * half, half, 0) for one in now]
        send = [lax.dynamic_slice_in_dim(one, (1 - bit) * half, half, 0) for one in now]
        got = [swapped(one, "tensor", distance) for one in send]
        if distance > 1:
            now = reduce_join((keep, got), when)
    return [one.reshape(share, model) for one in keep], [one.reshape(share, model) for one in got]


def reduce_join(pending, when):
    keep, got = pending
    return [
        when.after(keep[side].astype(f32) + got[side].astype(f32)).astype(bf16)
        for side in range(2)
    ]


def sum_over_dp(array, order, when):
    now = array
    kept = []
    for distance in order[:-1]:
        half = now.shape[0] // 2
        bit = bit_of("dp", distance)
        send = lax.dynamic_slice_in_dim(now, (1 - bit) * half, half, 0)
        when.before.append(send)
        got = swapped(send, "dp", distance)
        yield
        keep = lax.dynamic_slice_in_dim(now, bit * half, half, 0)
        now = when.after(keep.astype(f32) + got.astype(f32)).astype(bf16)
        kept.append(distance)
    when.before.append(now)
    got = swapped(now, "dp", order[-1])
    yield
    now = when.after(now.astype(f32) + got.astype(f32)).astype(bf16)
    for distance in reversed(kept):
        when.before.append(now)
        got = swapped(now, "dp", distance)
        yield
        upper = bit_of("dp", distance) == 1
        now = jnp.concatenate(
            [when.after(jnp.where(upper, got, now)), when.after(jnp.where(upper, now, got))],
            axis=0,
        )
    return now


class Sum:
    def __init__(self, array, order, when):
        self.run = sum_over_dp(array, order, when)
        self.value = None
        self.step()

    def step(self):
        if self.value is None:
            try:
                next(self.run)
            except StopIteration as stop:
                self.value = stop.value

    def finish(self):
        while self.value is None:
            self.step()
        return self.value


def small_sum(array, axes):
    for axis in axes:
        for distance in distances(lax.axis_size(axis)):
            array = array + swapped(array, axis, distance)
    return array


def to_shares(rows, inner, parts):
    half = rows.shape[0] // 2
    if inner == 2 and parts == 2:
        upper = bit_of("tensor", 1)
        send = lax.dynamic_slice_in_dim(rows, (1 - upper) * half, half, 0)
        got = swapped(send, "tensor", 1)
        return [jnp.where(upper == 1, got, rows[:half]), jnp.where(upper == 1, rows[half:], got)]
    whole = gather_inner(rows, inner)
    part_rows = whole.shape[0] // parts
    share = part_rows // inner
    first = lax.rem(lax.axis_index("tensor"), inner) * share
    return [
        lax.dynamic_slice_in_dim(whole, part * part_rows + first, share, 0)
        for part in range(parts)
    ]


def to_placement(shares, inner):
    parts = len(shares)
    if inner == 2 and parts == 2:
        upper = bit_of("tensor", 1) == 1
        mine = jnp.where(upper, shares[1], shares[0])
        theirs = jnp.where(upper, shares[0], shares[1])
        got = swapped(theirs, "tensor", 1)
        return jnp.concatenate([jnp.where(upper, got, mine), jnp.where(upper, mine, got)], axis=0)
    whole = jnp.concatenate([gather_inner(rows, inner) for rows in shares], axis=0)
    rows = whole.shape[0] // inner
    index = lax.rem(lax.axis_index("tensor"), inner)
    return lax.dynamic_slice_in_dim(whole, index * rows, rows, 0)


def on_device(
    tokens,
    doc_starts,
    norm_gains,
    norm_shifts,
    qkv_weight,
    qkv_bias,
    dense_weight,
    dense_bias,
    up_weight,
    up_bias,
    down_weight,
    down_bias,
    out_grad,
):
    layers = qkv_weight.shape[0]
    seqs = doc_starts.shape[0]
    model = tokens.shape[1]
    size = lax.axis_size("tensor")
    inner = size // seqs
    index = lax.axis_index("tensor")
    inner_index = lax.rem(index, inner)
    length = tokens.shape[0] * inner
    heads = qkv_weight.shape[2] // (3 * HS)
    padded = heads + heads % 2
    width = padded * HS
    group = 2 * PAIR if padded % 4 == 0 else PAIR
    parts = PARTS
    part_rows = length // parts
    share = part_rows // inner
    block = share if inner == 2 else min(512, part_rows)
    per_part = part_rows // block
    dp_size = lax.axis_size("dp")
    early_x = distances(dp_size)
    late_x = early_x[1:] + early_x[:1]

    when = Order()
    order = jnp.asarray(column_order(heads), bf16)
    feature = feature_matrix(group)
    dct = jnp.asarray(feature, bf16)
    dctt = jnp.asarray(feature.T, bf16)
    starts = jnp.where(index < inner, doc_starts, doc_starts[::-1])
    cosine, sine = rotary_tables(starts, length)
    zero_state = jnp.zeros((seqs, padded // 2 * PAIR, 2 * PAIR), f32)
    gains = norm_gains.astype(f32)
    shifts = norm_shifts.astype(f32)

    last = layers - 1
    place = jnp.full((1,), inner_index, jnp.int32)

    xs = to_shares(tokens, inner, parts)
    def fold(l):
        qkv, up, dense, down = qkv_weight[l], up_weight[l], dense_weight[l], down_weight[l]
        gain_one, gain_two = gains[l, 0][:, None], gains[l, 1][:, None]
        if l > 0:
            gain_one, gain_two = when.after(gain_one), when.after(gain_two)
        ordered = dot(qkv, order).astype(bf16)
        wq = (gain_one * ordered.astype(f32)).astype(bf16)
        wu = (gain_two * up.astype(f32)).astype(bf16)
        bias_one = dot(norm_shifts[l, 0:1], qkv) + qkv_bias[l].astype(f32)[None]
        bq = jnp.dot(bias_one, order.astype(f32), precision=lax.Precision.HIGHEST)
        bu = dot(norm_shifts[l, 1:2], up) + up_bias[l].astype(f32)[None]
        if padded != heads:
            dense = jnp.concatenate([dense, jnp.zeros((width - heads * HS, model), bf16)], axis=0)
        wo = jnp.concatenate([dense, down], axis=0)
        return (wq, bq, wu, bu, wo), ordered

    folded = [None] * layers
    folded[0] = fold(0)
    crossing_x = [swapped(xs[0], "tensor", inner), None]
    when.mark(cosine, sine, *folded[0][0])
    x_parts = [None] * parts
    x_parts[0] = (
        inner_source(xs[0], inner),
        inner_source(when.after(crossing_x[0]), inner),
    )
    when.mark(crossing_x[0])
    sent = when.after(xs[1])
    crossing_x[1] = swapped(sent, "tensor", inner)
    when.before.append(sent)
    when.token = None
    inputs = [None] * layers
    saved = [[None] * parts for _ in range(layers)]
    sums = [[None] * parts for _ in range(layers)]

    def run_forward(l, part, state):
        own, other = x_parts[part]
        xh, qkv, ca, rden, gp, states, state, *out = forward_layer(
            when, own, other, starts, place, folded[l][0], dct, cosine, sine, state, part, parts, block
        )
        saved[l][part] = (xh, qkv, ca, rden, gp, states)
        sums[l][part] = out
        return state

    def begin_reduce(partial_sum):
        return reduce_start(partial_sum, inner, when)

    def cross_reduce(pending):
        mine, theirs = reduce_join(pending, when)
        when.before += [mine, theirs]
        return mine, swapped(theirs, "tensor", inner)

    def end_forward(l, part, crossing):
        mine, got = crossing
        biases = dense_bias[l].astype(f32) + down_bias[l].astype(f32)
        summed = when.after(mine.astype(f32) + got.astype(f32))
        rows = (inputs[l][part].astype(f32) + (summed + biases)).astype(bf16)
        when.before.append(rows)
        return rows

    def end_backward(l, part, crossing):
        mine, got = crossing
        normed_grad = when.after(mine.astype(f32) + got.astype(f32))
        rows_in = inputs[l][part].astype(f32)
        center = jnp.mean(rows_in, axis=-1, keepdims=True)
        shifted = rows_in - center
        spread = jnp.mean(shifted * shifted, axis=-1, keepdims=True)
        inverse = lax.rsqrt(spread + norm_eps)
        normal = shifted * inverse
        along = jnp.mean(normed_grad * normal, axis=-1, keepdims=True)
        level = jnp.mean(normed_grad, axis=-1, keepdims=True)
        rows = incoming[part] + inverse * (normed_grad - level - normal * along)
        when.before.append(rows)
        return rows

    def whole_part(share_rows, crossing):
        return inner_source(share_rows, inner), inner_source(when.after(crossing), inner)

    def send_across(rows):
        when.before.append(rows)
        return swapped(rows, "tensor", inner)

    out_grad_shares = to_shares(out_grad, inner, parts)
    incoming = [rows.astype(f32) for rows in out_grad_shares]
    grads = [None] * parts
    crossing_grad = [None] * parts

    def send_out_grad(part):
        crossing_grad[part] = send_across(when.after(out_grad_shares[part]))

    for l in range(layers):
        inputs[l] = xs
        state = run_forward(l, 0, zero_state)
        if l < last:
            pending = begin_reduce(sums[l][0])
            if l == 0:
                x_parts[1] = whole_part(xs[1], crossing_x[1])
            crossing0 = cross_reduce(pending)
            state = run_forward(l, 1, state)
            pending = begin_reduce(sums[l][1])
            x0 = end_forward(l, 0, crossing0)
            far0 = send_across(x0)
            when.mark(x0)
            crossing1 = cross_reduce(pending)
            folded[l + 1] = fold(l + 1)
            x1 = end_forward(l, 1, crossing1)
            far1 = send_across(x1)
            xs = [x0, x1]
            x_parts = [whole_part(x0, far0), None]
        else:
            x_parts[1] = whole_part(xs[1], far1)
            send_out_grad(1)
            state = run_forward(l, 1, state)
            grads[1] = whole_part(out_grad_shares[1], crossing_grad[1])
            send_out_grad(0)

    small = [None] * layers
    weight_sums = [None] * layers

    def run_backward(l, part, state):
        own, other = grads[part]
        xh, qkv, ca, rden, gp, states = saved[l][part]
        kept = (qkv, ca, rden, gp, states)
        dz, db, state, *dx = backward_layer(
            when,
            own,
            other,
            starts,
            place,
            folded[l][0],
            dctt,
            cosine,
            sine,
            state,
            kept,
            part,
            parts,
            block,
        )
        return dz, dx, db, state

    def out_weights(l):
        return out_weight_grad(
            when, [kept[2] for kept in saved[l]], grads, place, part_rows, block
        )[0]

    def in_weights(l, dzs, dbs, bias_grad, pieces):
        db = sum(dbs)
        columns = jnp.stack([gains[l, 0], gains[l, 1], shifts[l, 0], shifts[l, 1]], axis=1)
        *made, norm_sums = in_weight_grad(
            when,
            [kept[0] for kept in saved[l]],
            dzs,
            db,
            columns,
            folded[l][1],
            up_weight[l],
            block,
            pieces,
        )
        small[l] = (jnp.concatenate([norm_sums[:, :4].T, bias_grad], axis=0), db)
        return made

    running = []

    def advance():
        for one in running:
            one.step()

    def bias_sum():
        return sum(
            jnp.sum(rows.astype(bf16).astype(f32), axis=0, keepdims=True) for rows in incoming
        )

    for l in reversed(range(layers)):
        bias_grad = bias_sum()
        dz1, dx1, db1, state = run_backward(l, 1, zero_state)
        if l == last:
            grads[0] = whole_part(out_grad_shares[0], crossing_grad[0])
        else:
            grads[0] = whole_part(far0[0], far0[1])
        if l > 0:
            pending1 = begin_reduce(dx1)
            out_sum = out_weights(l)
            turned = list(range(dp_size))[::-1]
            out_sum = lax.psum(out_sum, "dp", axis_index_groups=[turned])
            crossing1 = cross_reduce(pending1)
            dz0, dx0, db0, state = run_backward(l, 0, state)
            g1 = end_backward(l, 1, crossing1)
            low1 = g1.astype(bf16)
            far1 = send_across(low1)
            pending0 = begin_reduce(dx0)
            crossing0 = cross_reduce(pending0)
            (made,) = in_weights(l, [dz0, dz1], [db0, db1], bias_grad, 1)
            when.before.append(made)
            weight_sums[l] = (out_sum, lax.psum(made, "dp"))
            g0 = end_backward(l, 0, crossing0)
            low0 = g0.astype(bf16)
            far0 = (low0, send_across(low0))
            grads = [None, whole_part(low1, far1)]
            incoming = [g0, g1]
        else:
            out_made = out_weights(l)
            if l < last:
                when.before.append(weight_sums[l + 1][0])
            dz0, dx0, db0, state = run_backward(l, 0, state)
            made = in_weights(l, [dz0, dz1], [db0, db1], bias_grad, 2)
            running += [
                Sum(made[0], early_x, when),
                Sum(made[1], late_x, when),
                Sum(out_made, early_x, when),
            ]
            weight_sums[l] = (running[2], running[0], running[1])
            pending = [begin_reduce(dx) for dx in (dx1, dx0)]
            crossing = [cross_reduce(one) for one in pending]
            incoming = [end_backward(l, part, crossing[1 - part]) for part in range(parts)]
            out_pending = [begin_reduce(one) for one in sums[last]]
            out_crossing = [cross_reduce(one) for one in out_pending]

    while any(one.value is None for one in running):
        advance()
    weight_grads = []
    for l in range(layers):
        out_sum, *in_sums = [
            one.finish() if isinstance(one, Sum) else one for one in weight_sums[l]
        ]
        weight_grads.append((out_sum, jnp.concatenate(in_sums, axis=0)))
    tokens_grad = to_placement(incoming, inner)
    result = to_placement(
        [end_forward(last, part, out_crossing[part]) for part in range(parts)], inner
    )
    norm_rows = jnp.concatenate([one[0] for one in small], axis=0)
    bias_rows = jnp.concatenate([one[1] for one in small], axis=0)
    span = bias_rows.shape[1]
    bias_rows = jnp.pad(bias_rows, ((0, 0), (0, -span % model))).reshape(-1, model)
    small_rows = small_sum(jnp.concatenate([norm_rows, bias_rows], axis=0), ("dp",))
    norm_rows = small_sum(small_rows[: 5 * layers], ("tensor",)).reshape(layers, 5, model)
    bias_rows = small_rows[5 * layers :].reshape(layers, -1)[:, :span]

    stack = lambda pick: jnp.stack([pick(l) for l in range(layers)])
    bias_total = norm_rows[:, 4]
    bias_one = bias_rows[:, : 3 * width]
    return (
        result,
        tokens_grad,
        norm_rows[:, 0:2],
        norm_rows[:, 2:4],
        lax.dot_general(
            stack(lambda l: weight_grads[l][1][:, : 3 * width]),
            order,
            (((2,), (1,)), ((), ())),
            preferred_element_type=f32,
        ),
        jnp.dot(bias_one, order.astype(f32).T, precision=lax.Precision.HIGHEST),
        stack(lambda l: weight_grads[l][0][: heads * HS]).astype(f32),
        bias_total,
        stack(lambda l: weight_grads[l][1][:, 3 * width :]).astype(f32),
        bias_rows[:, 3 * width :],
        stack(lambda l: weight_grads[l][0][width:]).astype(f32),
        bias_total,
    )


def solution(mesh):
    return jax.shard_map(
        on_device,
        mesh=mesh,
        in_specs=(
            P(("dp", "tensor"), None),
            P("dp", None),
            P(),
            P(),
            P(None, None, "tensor"),
            P(None, "tensor"),
            P(None, "tensor", None),
            P(),
            P(None, None, "tensor"),
            P(None, "tensor"),
            P(None, "tensor", None),
            P(),
            P(("dp", "tensor"), None),
        ),
        out_specs=(
            P(("dp", "tensor"), None),
            P(("dp", "tensor"), None),
            P(),
            P(),
            P(None, None, "tensor"),
            P(None, "tensor"),
            P(None, "tensor", None),
            P(),
            P(None, None, "tensor"),
            P(None, "tensor"),
            P(None, "tensor", None),
            P(),
        ),
        check_vma=False,
    )
```

time: 1230 us -> 912 us (0.74)
  waiting for transfers between devices: 468 us -> 247 us
  blocking collectives: 124 us -> 0 us
  Pallas kernels: 262 us -> 371 us
  local copies, waits for them, and re-layouts: 146 us -> 46.4 us
  matrix products: 98.9 us -> 29.2 us
  starting transfers between devices: 9.21 us -> 49.9 us
  other arithmetic: 102 us -> 136 us
    psum x1 -> x2, waiting for transfers between devices: 251 us -> 22.8 us  [the longest x1 22.8 us: on_device(): out_sum = lax.psum(out_sum, 'dp', axis_index_groups=[turned])]
    psum x2 -> x0, blocking collectives: 124 us -> none  [the longest x1 85.2 us: on_device(): lax.psum(tuple((jnp.stack([sums[l][j] for l in range(layers)]) for j in r...]
    pallas_call x4 -> x15, Pallas kernels: 262 us -> 371 us  [call(): pl.pallas_call(body, grid_spec=pltpu.PrefetchScalarGridSpec(num_scalar_pr...]
    dot_general x9 -> x6, matrix products: 88.6 us -> 19.9 us  [the longest x2 10.1 us: spread(): lax.dot_general(table, jnp.asarray(lanes), TN, precision=lax.Precision.HI...]
    ppermute x20 -> x72, starting transfers between devices: 9.17 us -> 49.8 us  [swapped(): return lax.ppermute(array, axis, [(i, i ^ distance) for i in range(size)])]
    dynamic_update_slice x15 -> x0, local copies, waits for them, and re-layouts: 31.9 us -> none  [gather_rows(): whole = lax.dynamic_update_slice_in_dim(whole, b, (own ^ m) * rows, 0)]
    unnamed x123 -> x187, local copies, waits for them, and re-layouts: 37.8 us -> 14.5 us
    concatenate x4 -> x1, local copies, waits for them, and re-layouts: 20.9 us -> 0.58 us  [on_device(): jnp.concatenate([norm_rows, bias_rows], axis=0)]
  transfers between devices with their start and end apart: 21 -> 74, of which waited for: 8 -> 15; matrix products, arithmetic and copies ran while one was open for 18% -> 21% of each run, Pallas kernels for 6% -> 41%
where the time goes in v2:
time: 912 us; the launch traced here: 901 us
  Pallas kernels  371 us (41%)
  waiting for transfers between devices  247 us (27%)
  other arithmetic  136 us (15%)
  starting transfers between devices  49.9 us (5%)
  local copies, waits for them, and re-layouts  46.4 us (5%)
  matrix products  29.2 us (3%)
  between operations  22.8 us (2%)
    pallas_call x15, Pallas kernels, call(): pl.pallas_call(body, grid_spec=pltpu.PrefetchScalarGridSpec(num_scalar_pr...  371 us
    ppermute x72, waiting for transfers between devices, swapped(): return lax.ppermute(array, axis, [(i, i ^ distance) for i in range(size)])  224 us
    ppermute x72, starting transfers between devices, swapped(): return lax.ppermute(array, axis, [(i, i ^ distance) for i in range(size)])  49.8 us
    convert_element_type x11, other arithmetic, reduce_join(): when.after(keep[side].astype(f32) + got[side].astype(f32)).astype(bf16)  27.4 us
    psum x1, waiting for transfers between devices, on_device(): out_sum = lax.psum(out_sum, 'dp', axis_index_groups=[turned])  22.8 us
    add x17, other arithmetic, after(): return array + self.token.astype(array.dtype).reshape((1,) * array.ndim)  21.2 us
  transfers between devices with their start and end apart: 74, of which 15 were waited for; matrix products, arithmetic and copies ran while one was open for 21% of the time, Pallas kernels for 41%

profile of v2, /device:TPU:0, one launch (start us, length us, event | category | flops | bytes accessed | tf_op | source)
XLA Modules:
  0.0 901.5 jit_solution(1375771035300041840)
XLA Ops:
  15.3 5.0 fusion.70.refs_1_.refs_13_.refs_11_
  20.4 5.0 convolution_add_fusion.refs_0_.refs_12_.refs_10_
  38.5 3.2 multiply_convert_fusion.3
  43.1 12.8 %collective-permute-done.2.refs_0_ = bf16[512,1024]{1,0:T(8,128)(2,1)S(1)} collective-permute-done((bf16[512,1024]{1,0:T(8,128)(2,1)S(1)}, bf16[512,1024]{1,0:T(8,128)(2,1)S(1)}, u32[]{:S(2)}, u32[]{:S(2)}) %collective-permute-start.2) | collective-permute-done | bytes 1048608 | tf_op jit(solution)/shard_map/ppermute | solution.py:915
  63.2 31.4 %forward_layer.4 = (bf16[2048,1024]{1,0:T(8,128)(2,1)}, bf16[2048,768]{1,0:T(8,128)(2,1)}, bf16[2048,1280]{1,0:T(8,128)(2,1)}, bf16[2048,256]{1,0:T(8,128)(2,1)}...) custom-call(s32[2,4]{1,0:T(2,128)} %copy-done.72, ...), custom_call_target="tpu_custom_call" | custom-call | tf_op jit(solution)/shard_map/forward_layer/pallas_call | solution.py:676
  105.4 31.6 %forward_layer.5 = (bf16[2048,1024]{1,0:T(8,128)(2,1)}, bf16[2048,768]{1,0:T(8,128)(2,1)}, bf16[2048,1280]{1,0:T(8,128)(2,1)}, bf16[2048,256]{1,0:T(8,128)(2,1)}...) custom-call(s32[2,4]{1,0:T(2,128)} %copy-done.72, ...), custom_call_target="tpu_custom_call" | custom-call | tf_op jit(solution)/shard_map/forward_layer/pallas_call | solution.py:676
  138.7 3.7 convert_reduce_fusion.2
  151.4 17.3 %collective-permute-done.11 = bf16[512,1024]{1,0:T(8,128)(2,1)} collective-permute-done((bf16[512,1024]{1,0:T(8,128)(2,1)}, bf16[512,1024]{1,0:T(8,128)(2,1)}, u32[]{:S(2)}, u32[]{:S(2)}) %collective-permute-start.11) | collective-permute-done | bytes 1048608 | tf_op jit(solution)/shard_map/ppermute | solution.py:915
  170.2 20.2 %collective-permute-done.15 = bf16[512,1024]{1,0:T(8,128)(2,1)S(1)} collective-permute-done((bf16[512,1024]{1,0:T(8,128)(2,1)S(1)}, bf16[512,1024]{1,0:T(8,128)(2,1)S(1)}, u32[]{:S(2)}, u32[]{:S(2)}) %collective-permute-start.15) | collective-permute-done | bytes 1048608 | tf_op jit(solution)/shard_map/ppermute | solution.py:915
  190.3 4.0 convert_reduce_fusion
  195.8 3.3 convert_reduce_fusion.5
  202.5 3.0 multiply_convert_fusion.2
  207.5 31.9 %forward_layer.6 = (bf16[2048,1024]{1,0:T(8,128)(2,1)}, bf16[2048,768]{1,0:T(8,128)(2,1)}, bf16[2048,1280]{1,0:T(8,128)(2,1)}, bf16[2048,256]{1,0:T(8,128)(2,1)}...) custom-call(s32[2,4]{1,0:T(2,128)} %copy-done.72, ...), custom_call_target="tpu_custom_call" | custom-call | tf_op jit(solution)/shard_map/forward_layer/pallas_call | solution.py:676
  245.7 31.5 %forward_layer.7 = (bf16[2048,1024]{1,0:T(8,128)(2,1)}, bf16[2048,768]{1,0:T(8,128)(2,1)}, bf16[2048,1280]{1,0:T(8,128)(2,1)}, bf16[2048,256]{1,0:T(8,128)(2,1)}...) custom-call(s32[2,4]{1,0:T(2,128)} %copy-done.72, ...), custom_call_target="tpu_custom_call" | custom-call | tf_op jit(solution)/shard_map/forward_layer/pallas_call | solution.py:676
  283.4 36.5 %backward_layer.4 = (bf16[2048,1792]{1,0:T(8,128)(2,1)}, f32[1,1792]{1,0:T(1,128)}, f32[2,256,256]{2,1,0:T(8,128)}, bf16[512,1024]{1,0:T(8,128)(2,1)}, bf16[512,...) custom-call(s32[2,4]{1,0:T(2,128)} %copy-done.72, ...), custom_call_target="tpu_custom_call" | custom-call | tf_op jit(solution)/shard_map/backward_layer/pallas_call | solution.py:676
  326.5 19.6 %out_weight_grad.2 = (bf16[1280,1024]{1,0:T(8,128)(2,1)}, f32[1,1]{1,0:T(1,128)}) custom-call(s32[1]{0:T(128)} %bitcast.refs_1_.refs_0_, bf16[2048,1280]{1,0:T(8,128)(2,1)} %get-tuple-element.123.refs_1_.refs_14_, bf16[2048,1280]{1,0:T(8,128)(2,1)} %get-tuple-element.116.refs_14_.refs_2_, bf16[512,1024]{1,0:T(8,128)(2,1)} %get-tuple-element.195.refs_3_.refs_2_, ...), custom_call_target="tpu_custom_call" | custom-call | tf_op jit(solution)/shard_map/out_weight_grad/pallas_call | solution.py:676
  352.1 36.8 %backward_layer.5 = (bf16[2048,1792]{1,0:T(8,128)(2,1)}, f32[1,1792]{1,0:T(1,128)}, f32[2,256,256]{2,1,0:T(8,128)}, bf16[512,1024]{1,0:T(8,128)(2,1)}, bf16[512,...) custom-call(s32[2,4]{1,0:T(2,128)} %copy-done.72, ...), custom_call_target="tpu_custom_call" | custom-call | tf_op jit(solution)/shard_map/backward_layer/pallas_call | solution.py:676
  391.0 4.7 convert_reduce_fusion.6
  403.2 3.6 add_convert_fusion.10.refs_12_
  406.8 28.8 %in_weight_grad.2 = (bf16[1024,1792]{1,0:T(8,128)(2,1)}, f32[1024,128]{1,0:T(8,128)}, f32[1,1]{1,0:T(1,128)}) custom-call(bf16[2048,1024]{1,0:T(8,128)(2,1)} %get-tuple-element.137.refs_0_, bf16[2048,1024]{1,0:T(8,128)(2,1)} %get-tuple-element.138.refs_1_, bf16[2048,1792]{1,0:T(8,128)(2,1)} %get-tuple-element.139.refs_2_, ...), custom_call_target="tpu_custom_call" | custom-call | tf_op jit(solution)/shard_map/in_weight_grad/pallas_call | solution.py:676
  439.2 4.4 collective-permute-done.31
  443.6 3.0 fusion.44
  446.7 5.0 convert_reduce_fusion.7
  453.7 36.5 %backward_layer.6 = (bf16[2048,1792]{1,0:T(8,128)(2,1)}, f32[1,1792]{1,0:T(1,128)}, f32[2,256,256]{2,1,0:T(8,128)}, bf16[512,1024]{1,0:T(8,128)(2,1)}, bf16[512,...) custom-call(s32[2,4]{1,0:T(2,128)} %copy-done.72, ...), custom_call_target="tpu_custom_call" | custom-call | tf_op jit(solution)/shard_map/backward_layer/pallas_call | solution.py:676
  496.5 22.8 %all-reduce.4.cloned.1.call-done.refs_18_ = bf16[1280,1024]{1,0:T(8,128)(2,1)} async-done(((bf16[1280,1024]{1,0:T(8,128)(2,1)}), bf16[1280,1024]{1,0:T(8,128)(2,1)}) %all-reduce.4.cloned.1.call-update) | async-done | bytes 2621456 | tf_op jit(solution)/shard_map/psum | solution.py:1294
  519.2 3.1 slice_bitcast_fusion
  524.8 37.5 %backward_layer.7 = (bf16[2048,1792]{1,0:T(8,128)(2,1)}, f32[1,1792]{1,0:T(1,128)}, f32[2,256,256]{2,1,0:T(8,128)}, bf16[512,1024]{1,0:T(8,128)(2,1)}, bf16[512,...) custom-call(s32[2,4]{1,0:T(2,128)} %copy-done.72, ...), custom_call_target="tpu_custom_call" | custom-call | tf_op jit(solution)/shard_map/backward_layer/pallas_call | solution.py:676
  563.6 27.8 %in_weight_grad.3 = (bf16[512,1792]{1,0:T(8,128)(2,1)}, bf16[512,1792]{1,0:T(8,128)(2,1)}, f32[1024,128]{1,0:T(8,128)}, f32[1,1]{1,0:T(1,128)}) custom-call(bf16[2048,1024]{1,0:T(8,128)(2,1)} %get-tuple-element.110.refs_0_, bf16[2048,1024]{1,0:T(8,128)(2,1)} %get-tuple-element.111.refs_1_, bf16[2048,1792]{1,0:T(8,128)(2,1)} %get-tuple-element.158.refs_2_, ...), custom_call_target="tpu_custom_call" | custom-call | tf_op jit(solution)/shard_map/in_weight_grad/pallas_call | solution.py:676
  595.3 3.7 add_convert_fusion.1
  600.4 3.4 add_convert_fusion.7
  606.3 3.3 add_convert_fusion.5
  613.1 19.4 %out_weight_grad.3 = (bf16[1280,1024]{1,0:T(8,128)(2,1)}, f32[1,1]{1,0:T(1,128)}) custom-call(s32[1]{0:T(128)} %bitcast.refs_1_.refs_0_, bf16[2048,1280]{1,0:T(8,128)(2,1)} %get-tuple-element.153.refs_14_.refs_1_, bf16[2048,1280]{1,0:T(8,128)(2,1)} %get-tuple-element.145.refs_14_.refs_2_, bf16[512,1024]{1,0:T(8,128)(2,1)} %get-tuple-element.200.refs_20_.refs_2_.refs_3_, ...), custom_call_target="tpu_custom_call" | custom-call | tf_op jit(solution)/shard_map/out_weight_grad/pallas_call | solution.py:676
  645.9 42.3 %collective-permute-done.62 = bf16[256,1792]{1,0:T(8,128)(2,1)} collective-permute-done((bf16[256,1792]{1,0:T(8,128)(2,1)}, bf16[256,1792]{1,0:T(8,128)(2,1)}, u32[]{:S(2)}, u32[]{:S(2)}) %collective-permute-start.62) | collective-permute-done | bytes 917536 | tf_op jit(solution)/shard_map/ppermute | solution.py:915
  692.6 3.1 fusion.47
  698.6 17.9 %collective-permute-done.40 = bf16[512,1024]{1,0:T(8,128)(2,1)S(1)} collective-permute-done((bf16[512,1024]{1,0:T(8,128)(2,1)S(1)}, bf16[512,1024]{1,0:T(8,128)(2,1)S(1)}, u32[]{:S(2)}, u32[]{:S(2)}) %collective-permute-start.40) | collective-permute-done | bytes 1048608 | tf_op jit(solution)/shard_map/ppermute | solution.py:915
  716.9 21.6 %collective-permute-done.43 = bf16[512,1024]{1,0:T(8,128)(2,1)S(1)} collective-permute-done((bf16[512,1024]{1,0:T(8,128)(2,1)S(1)}, bf16[512,1024]{1,0:T(8,128)(2,1)S(1)}, u32[]{:S(2)}, u32[]{:S(2)}) %collective-permute-start.43) | collective-permute-done | bytes 1048608 | tf_op jit(solution)/shard_map/ppermute | solution.py:915
  740.0 4.9 broadcast_select_fusion.7
  751.0 20.1 %collective-permute-done.59 = bf16[128,1792]{1,0:T(8,128)(2,1)S(1)} collective-permute-done((bf16[128,1792]{1,0:T(8,128)(2,1)S(1)}, bf16[128,1792]{1,0:T(8,128)(2,1)S(1)}, u32[]{:S(2)}, u32[]{:S(2)}) %collective-permute-start.59) | collective-permute-done | bytes 458784 | tf_op jit(solution)/shard_map/ppermute | solution.py:915
  773.4 10.1 %collective-permute-done.64 = bf16[128,1792]{1,0:T(8,128)(2,1)S(1)} collective-permute-done((bf16[128,1792]{1,0:T(8,128)(2,1)S(1)}, bf16[128,1792]{1,0:T(8,128)(2,1)S(1)}, u32[]{:S(2)}, u32[]{:S(2)}) %collective-permute-start.64) | collective-permute-done | bytes 458784 | tf_op jit(solution)/shard_map/ppermute | solution.py:915
  783.5 3.4 collective-permute-start.60
  794.7 6.4 broadcast_select_fusion.3
  802.9 23.1 %collective-permute-done.65 = bf16[128,1792]{1,0:T(8,128)(2,1)S(1)} collective-permute-done((bf16[128,1792]{1,0:T(8,128)(2,1)S(1)}, bf16[128,1792]{1,0:T(8,128)(2,1)S(1)}, u32[]{:S(2)}, u32[]{:S(2)}) %collective-permute-start.65) | collective-permute-done | bytes 458784 | tf_op jit(solution)/shard_map/ppermute | solution.py:915
  832.2 5.8 collective-permute-done.69
  840.3 14.3 %collective-permute-done.66 = bf16[256,1792]{1,0:T(8,128)(2,1)} collective-permute-done((bf16[256,1792]{1,0:T(8,128)(2,1)S(1)}, bf16[256,1792]{1,0:T(8,128)(2,1)}, u32[]{:S(2)}, u32[]{:S(2)}) %collective-permute-start.66) | collective-permute-done | bytes 917536 | tf_op jit(solution)/shard_map/ppermute | solution.py:915
  858.1 3.9 maximum_convert_fusion
  864.0 4.6 fusion
  873.5 12.5 %collective-permute-done.71 = bf16[640,1024]{1,0:T(8,128)(2,1)S(1)} collective-permute-done((bf16[640,1024]{1,0:T(8,128)(2,1)S(1)}, bf16[640,1024]{1,0:T(8,128)(2,1)S(1)}, u32[]{:S(2)}, u32[]{:S(2)}) %collective-permute-start.71) | collective-permute-done | bytes 1310752 | tf_op jit(solution)/shard_map/ppermute | solution.py:915
  888.4 3.9 maximum_convert_fusion.1
  (461 shorter events, 177.1 us)
Async XLA Ops:
  7.2 512.1 %all-reduce.4.cloned.1.call-start = ((), (), s32[]{:S(2)}) async-start(), calls=%async_computation | async-start | bytes 5242880 | tf_op jit(solution)/shard_map/psum | solution.py:1294
  29.5 26.4 %collective-permute-start.2 = (bf16[512,1024]{1,0:T(8,128)(2,1)S(1)}, bf16[512,1024]{1,0:T(8,128)(2,1)S(1)}, u32[]{:S(2)}, u32[]{:S(2)}) collective-permute-start(bf16[512,1024]{1,0:T(8,128)(2,1)S(1)} %get-tuple-element.208.refs_2_), channel_id=1, source_target_pairs={{0,2},{1,3},{2,0},{3,1},{4,6},{5,7},{6,4},{7,5},{8,10},{9,11},{10,... | collective-permute-start | bytes 3145736 | tf_op jit(solution)/shard_map/ppermute | solution.py:915
  60.6 35.4 %collective-permute-start.8 = (bf16[512,1024]{1,0:T(8,128)(2,1)}, bf16[512,1024]{1,0:T(8,128)(2,1)}, u32[]{:S(2)}, u32[]{:S(2)}) collective-permute-start(bf16[512,1024]{1,0:T(8,128)(2,1)} %broadcast_add_fusion.9.refs_15_), channel_id=1, source_target_pairs={{0,2},{1,3},{2,0},{3,1},{4,6},{5,7},{6,4},{7,5},{8,10},{9,11},{10,... | collective-permute-start | bytes 3145736 | tf_op jit(solution)/shard_map/ppermute | solution.py:915
  99.0 96.9 %collective-permute-start.17 = (bf16[512,1024]{1,0:T(8,128)(2,1)}, bf16[512,1024]{1,0:T(8,128)(2,1)}, u32[]{:S(2)}, u32[]{:S(2)}) collective-permute-start(bf16[512,1024]{1,0:T(8,128)(2,1)} %constant_dynamic-slice_fusion.6), channel_id=1, source_target_pairs={{0,1},{1,0},{2,3},{3,2},{4,5},{5,4},{6,7},{7,6},{8,9},{9,8},{10,11... | collective-permute-start | bytes 3145736 | tf_op jit(solution)/shard_map/ppermute | solution.py:915
  100.4 38.3 %collective-permute-start.6 = (bf16[512,1024]{1,0:T(8,128)(2,1)S(1)}, bf16[512,1024]{1,0:T(8,128)(2,1)}, u32[]{:S(2)}, u32[]{:S(2)}) collective-permute-start(bf16[512,1024]{1,0:T(8,128)(2,1)S(1)} %add_convert_fusion.15.refs_18_), channel_id=1, source_target_pairs={{0,2},{1,3},{2,0},{3,1},{4,6},{5,7},{6,4},{7,5},{8,10},{9,11},{10,... | collective-permute-start | bytes 3145736 | tf_op jit(solution)/shard_map/ppermute | solution.py:915
  138.3 31.8 %collective-permute-start.13 = (bf16[512,1024]{1,0:T(8,128)(2,1)}, bf16[512,1024]{1,0:T(8,128)(2,1)}, u32[]{:S(2)}, u32[]{:S(2)}) collective-permute-start(bf16[512,1024]{1,0:T(8,128)(2,1)} %get-tuple-element.104.refs_0_), channel_id=1, source_target_pairs={{0,1},{1,0},{2,3},{3,2},{4,5},{5,4},{6,7},{7,6},{8,9},{9,8},{10,11... | collective-permute-start | bytes 3145736 | tf_op jit(solution)/shard_map/ppermute | solution.py:915
  142.4 26.3 %collective-permute-start.11 = (bf16[512,1024]{1,0:T(8,128)(2,1)}, bf16[512,1024]{1,0:T(8,128)(2,1)}, u32[]{:S(2)}, u32[]{:S(2)}) collective-permute-start(bf16[512,1024]{1,0:T(8,128)(2,1)} %get-tuple-element.213.refs_2_.refs_3_.refs_4_), channel_id=1, source_target_pairs={{0,2},{1,3},{2,0},{3,1},{4,6},{5,7},{6,4},{7,5},{8,10},{9,11},{10,... | collective-permute-start | bytes 3145736 | tf_op jit(solution)/shard_map/ppermute | solution.py:915
  147.0 43.3 %collective-permute-start.15 = (bf16[512,1024]{1,0:T(8,128)(2,1)S(1)}, bf16[512,1024]{1,0:T(8,128)(2,1)S(1)}, u32[]{:S(2)}, u32[]{:S(2)}) collective-permute-start(bf16[512,1024]{1,0:T(8,128)(2,1)S(1)} %add_convert_fusion.13.refs_16_), channel_id=1, source_target_pairs={{0,2},{1,3},{2,0},{3,1},{4,6},{5,7},{6,4},{7,5},{8,10},{9,11},{10,... | collective-permute-start | bytes 3145736 | tf_op jit(solution)/shard_map/ppermute | solution.py:915
  151.4 54.2 %collective-permute-start.10 = (bf16[512,1024]{1,0:T(8,128)(2,1)}, bf16[512,1024]{1,0:T(8,128)(2,1)S(1)}, u32[]{:S(2)}, u32[]{:S(2)}) collective-permute-start(bf16[512,1024]{1,0:T(8,128)(2,1)} %get-tuple-element.213.refs_2_.refs_3_.refs_4_), channel_id=1, source_target_pairs={{0,1},{1,0},{2,3},{3,2},{4,5},{5,4},{6,7},{7,6},{8,9},{9,8},{10,11... | collective-permute-start | bytes 3145736 | tf_op jit(solution)/shard_map/ppermute | solution.py:915
  170.1 35.5 %collective-permute-start.12 = (bf16[512,1024]{1,0:T(8,128)(2,1)S(1)}, bf16[512,1024]{1,0:T(8,128)(2,1)S(1)}, u32[]{:S(2)}, u32[]{:S(2)}) collective-permute-start(bf16[512,1024]{1,0:T(8,128)(2,1)S(1)} %broadcast_add_fusion.7.refs_4_), channel_id=1, source_target_pairs={{0,1},{1,0},{2,3},{3,2},{4,5},{5,4},{6,7},{7,6},{8,9},{9,8},{10,11... | collective-permute-start | bytes 3145736 | tf_op jit(solution)/shard_map/ppermute | solution.py:915
  194.3 45.7 %collective-permute-start.20 = (bf16[512,1024]{1,0:T(8,128)(2,1)S(1)}, bf16[512,1024]{1,0:T(8,128)(2,1)}, u32[]{:S(2)}, u32[]{:S(2)}) collective-permute-start(bf16[512,1024]{1,0:T(8,128)(2,1)S(1)} %get-tuple-element.215.refs_17_.refs_18_.refs_2_), channel_id=1, source_target_pairs={{0,2},{1,3},{2,0},{3,1},{4,6},{5,7},{6,4},{7,5},{8,10},{9,11},{10,... | collective-permute-start | bytes 3145736 | tf_op jit(solution)/shard_map/ppermute | solution.py:915
  205.5 39.2 %collective-permute-start.19 = (bf16[512,1024]{1,0:T(8,128)(2,1)S(1)}, bf16[512,1024]{1,0:T(8,128)(2,1)}, u32[]{:S(2)}, u32[]{:S(2)}) collective-permute-start(bf16[512,1024]{1,0:T(8,128)(2,1)S(1)} %get-tuple-element.215.refs_17_.refs_18_.refs_2_), channel_id=1, source_target_pairs={{0,1},{1,0},{2,3},{3,2},{4,5},{5,4},{6,7},{7,6},{8,9},{9,8},{10,11... | collective-permute-start | bytes 3145736 | tf_op jit(solution)/shard_map/ppermute | solution.py:915
  244.2 33.8 %collective-permute-start.24 = (bf16[512,1024]{1,0:T(8,128)(2,1)}, bf16[512,1024]{1,0:T(8,128)(2,1)}, u32[]{:S(2)}, u32[]{:S(2)}) collective-permute-start(bf16[512,1024]{1,0:T(8,128)(2,1)} %broadcast_add_fusion.5.refs_15_), channel_id=1, source_target_pairs={{0,2},{1,3},{2,0},{3,1},{4,6},{5,7},{6,4},{7,5},{8,10},{9,11},{10,... | collective-permute-start | bytes 3145736 | tf_op jit(solution)/shard_map/ppermute | solution.py:915
  244.7 37.7 %collective-permute-start.23 = (bf16[512,1024]{1,0:T(8,128)(2,1)}, bf16[512,1024]{1,0:T(8,128)(2,1)}, u32[]{:S(2)}, u32[]{:S(2)}) collective-permute-start(bf16[512,1024]{1,0:T(8,128)(2,1)} %get-tuple-element.226.refs_2_.refs_7_), channel_id=1, source_target_pairs={{0,1},{1,0},{2,3},{3,2},{4,5},{5,4},{6,7},{7,6},{8,9},{9,8},{10,11... | collective-permute-start | bytes 3145736 | tf_op jit(solution)/shard_map/ppermute | solution.py:915
  280.9 39.6 %collective-permute-start.22 = (bf16[512,1024]{1,0:T(8,128)(2,1)}, bf16[512,1024]{1,0:T(8,128)(2,1)}, u32[]{:S(2)}, u32[]{:S(2)}) collective-permute-start(bf16[512,1024]{1,0:T(8,128)(2,1)} %broadcast_add_fusion.4.refs_18_), channel_id=1, source_target_pairs={{0,2},{1,3},{2,0},{3,1},{4,6},{5,7},{6,4},{7,5},{8,10},{9,11},{10,... | collective-permute-start | bytes 3145736 | tf_op jit(solution)/shard_map/ppermute | solution.py:915
  282.4 43.0 %collective-permute-start.18 = (bf16[512,1024]{1,0:T(8,128)(2,1)S(1)}, bf16[512,1024]{1,0:T(8,128)(2,1)}, u32[]{:S(2)}, u32[]{:S(2)}) collective-permute-start(bf16[512,1024]{1,0:T(8,128)(2,1)S(1)} %copy-done.7), channel_id=1, source_target_pairs={{0,1},{1,0},{2,3},{3,2},{4,5},{5,4},{6,7},{7,6},{8,9},{9,8},{10,11... | collective-permute-start | bytes 3145736 | tf_op jit(solution)/shard_map/ppermute | solution.py:915
  348.5 40.9 %collective-permute-start.32 = (bf16[512,1024]{1,0:T(8,128)(2,1)S(1)}, bf16[512,1024]{1,0:T(8,128)(2,1)S(1)}, u32[]{:S(2)}, u32[]{:S(2)}) collective-permute-start(bf16[512,1024]{1,0:T(8,128)(2,1)S(1)} %add_convert_fusion.11.refs_19_), channel_id=1, source_target_pairs={{0,2},{1,3},{2,0},{3,1},{4,6},{5,7},{6,4},{7,5},{8,10},{9,11},{10,... | collective-permute-start | bytes 3145736 | tf_op jit(solution)/shard_map/ppermute | solution.py:915
  395.7 40.6 %collective-permute-start.36 = (bf16[512,1024]{1,0:T(8,128)(2,1)}, bf16[512,1024]{1,0:T(8,128)(2,1)}, u32[]{:S(2)}, u32[]{:S(2)}) collective-permute-start(bf16[512,1024]{1,0:T(8,128)(2,1)} %get-tuple-element.197.refs_9_.refs_2_.refs_7_), channel_id=1, source_target_pairs={{0,2},{1,3},{2,0},{3,1},{4,6},{5,7},{6,4},{7,5},{8,10},{9,11},{10,... | collective-permute-start | bytes 3145736 | tf_op jit(solution)/shard_map/ppermute | solution.py:915
  398.7 44.8 %collective-permute-start.31 = (bf16[512,1024]{1,0:T(8,128)(2,1)}, bf16[512,1024]{1,0:T(8,128)(2,1)}, u32[]{:S(2)}, u32[]{:S(2)}) collective-permute-start(bf16[512,1024]{1,0:T(8,128)(2,1)} %add_convert_fusion.9.refs_13_), channel_id=1, source_target_pairs={{0,2},{1,3},{2,0},{3,1},{4,6},{5,7},{6,4},{7,5},{8,10},{9,11},{10,... | collective-permute-start | bytes 3145736 | tf_op jit(solution)/shard_map/ppermute | solution.py:915
  403.2 50.5 %collective-permute-start.35 = (bf16[512,1024]{1,0:T(8,128)(2,1)}, bf16[512,1024]{1,0:T(8,128)(2,1)}, u32[]{:S(2)}, u32[]{:S(2)}) collective-permute-start(bf16[512,1024]{1,0:T(8,128)(2,1)} %get-tuple-element.197.refs_9_.refs_2_.refs_7_), channel_id=1, source_target_pairs={{0,1},{1,0},{2,3},{3,2},{4,5},{5,4},{6,7},{7,6},{8,9},{9,8},{10,11... | collective-permute-start | bytes 3145736 | tf_op jit(solution)/shard_map/ppermute | solution.py:915
  451.6 39.4 %collective-permute-start.34 = (bf16[512,1024]{1,0:T(8,128)(2,1)}, bf16[512,1024]{1,0:T(8,128)(2,1)}, u32[]{:S(2)}, u32[]{:S(2)}) collective-permute-start(bf16[512,1024]{1,0:T(8,128)(2,1)} %get-tuple-element.200.refs_20_.refs_2_.refs_3_), channel_id=1, source_target_pairs={{0,2},{1,3},{2,0},{3,1},{4,6},{5,7},{6,4},{7,5},{8,10},{9,11},{10,... | collective-permute-start | bytes 3145736 | tf_op jit(solution)/shard_map/ppermute | solution.py:915
  453.7 70.6 %collective-permute-start.33 = (bf16[512,1024]{1,0:T(8,128)(2,1)}, bf16[512,1024]{1,0:T(8,128)(2,1)}, u32[]{:S(2)}, u32[]{:S(2)}) collective-permute-start(bf16[512,1024]{1,0:T(8,128)(2,1)} %get-tuple-element.200.refs_20_.refs_2_.refs_3_), channel_id=1, source_target_pairs={{0,1},{1,0},{2,3},{3,2},{4,5},{5,4},{6,7},{7,6},{8,9},{9,8},{10,11... | collective-permute-start | bytes 3145736 | tf_op jit(solution)/shard_map/ppermute | solution.py:915
  490.2 338.7 %all-reduce.6.cloned.1.call-start = ((), (), s32[]{:S(2)}) async-start(), calls=%async_computation.1 | async-start | bytes 7340032 | tf_op jit(solution)/shard_map/psum | solution.py:1304
  493.3 31.0 %collective-permute-start.38 = (bf16[512,1024]{1,0:T(8,128)(2,1)}, bf16[512,1024]{1,0:T(8,128)(2,1)}, u32[]{:S(2)}, u32[]{:S(2)}) collective-permute-start(bf16[512,1024]{1,0:T(8,128)(2,1)} %broadcast_add_fusion.refs_4_.refs_5_), channel_id=1, source_target_pairs={{0,1},{1,0},{2,3},{3,2},{4,5},{5,4},{6,7},{7,6},{8,9},{9,8},{10,11... | collective-permute-start | bytes 3145736 | tf_op jit(solution)/shard_map/ppermute | solution.py:915
  493.8 105.2 %collective-permute-start.39 = (bf16[512,1024]{1,0:T(8,128)(2,1)}, bf16[512,1024]{1,0:T(8,128)(2,1)}, u32[]{:S(2)}, u32[]{:S(2)}) collective-permute-start(bf16[512,1024]{1,0:T(8,128)(2,1)} %get-tuple-element.164), channel_id=1, source_target_pairs={{0,1},{1,0},{2,3},{3,2},{4,5},{5,4},{6,7},{7,6},{8,9},{9,8},{10,11... | collective-permute-start | bytes 3145736 | tf_op jit(solution)/shard_map/ppermute | solution.py:915
  493.8 204.5 %collective-permute-start.16 = (bf16[512,1024]{1,0:T(8,128)(2,1)}, bf16[512,1024]{1,0:T(8,128)(2,1)}, u32[]{:S(2)}, u32[]{:S(2)}) collective-permute-start(bf16[512,1024]{1,0:T(8,128)(2,1)} %get-tuple-element.109), channel_id=1, source_target_pairs={{0,1},{1,0},{2,3},{3,2},{4,5},{5,4},{6,7},{7,6},{8,9},{9,8},{10,11... | collective-permute-start | bytes 3145736 | tf_op jit(solution)/shard_map/ppermute | solution.py:915
  496.3 98.8 %collective-permute-start.49 = (bf16[512,1024]{1,0:T(8,128)(2,1)}, bf16[512,1024]{1,0:T(8,128)(2,1)}, u32[]{:S(2)}, u32[]{:S(2)}) collective-permute-start(bf16[512,1024]{1,0:T(8,128)(2,1)} %get-tuple-element.176), channel_id=1, source_target_pairs={{0,1},{1,0},{2,3},{3,2},{4,5},{5,4},{6,7},{7,6},{8,9},{9,8},{10,11... | collective-permute-start | bytes 3145736 | tf_op jit(solution)/shard_map/ppermute | solution.py:915
  524.3 81.9 %collective-permute-start.42 = (bf16[512,1024]{1,0:T(8,128)(2,1)}, bf16[512,1024]{1,0:T(8,128)(2,1)}, u32[]{:S(2)}, u32[]{:S(2)}) collective-permute-start(bf16[512,1024]{1,0:T(8,128)(2,1)} %get-tuple-element.168), channel_id=1, source_target_pairs={{0,1},{1,0},{2,3},{3,2},{4,5},{5,4},{6,7},{7,6},{8,9},{9,8},{10,11... | collective-permute-start | bytes 3145736 | tf_op jit(solution)/shard_map/ppermute | solution.py:915
  524.3 174.1 %collective-permute-start.41 = (bf16[512,1024]{1,0:T(8,128)(2,1)}, bf16[512,1024]{1,0:T(8,128)(2,1)}, u32[]{:S(2)}, u32[]{:S(2)}) collective-permute-start(bf16[512,1024]{1,0:T(8,128)(2,1)} %get-tuple-element.166), channel_id=1, source_target_pairs={{0,1},{1,0},{2,3},{3,2},{4,5},{5,4},{6,7},{7,6},{8,9},{9,8},{10,11... | collective-permute-start | bytes 3145736 | tf_op jit(solution)/shard_map/ppermute | solution.py:915
  595.1 95.3 %collective-permute-start.48 = (bf16[512,1024]{1,0:T(8,128)(2,1)}, bf16[512,1024]{1,0:T(8,128)(2,1)}, u32[]{:S(2)}, u32[]{:S(2)}) collective-permute-start(bf16[512,1024]{1,0:T(8,128)(2,1)} %get-tuple-element.174), channel_id=1, source_target_pairs={{0,1},{1,0},{2,3},{3,2},{4,5},{5,4},{6,7},{7,6},{8,9},{9,8},{10,11... | collective-permute-start | bytes 3145736 | tf_op jit(solution)/shard_map/ppermute | solution.py:915
  604.9 37.6 %collective-permute-start.57 = (bf16[256,1792]{1,0:T(8,128)(2,1)}, bf16[256,1792]{1,0:T(8,128)(2,1)}, u32[]{:S(2)}, u32[]{:S(2)}) collective-permute-start(bf16[256,1792]{1,0:T(8,128)(2,1)} %constant_dynamic-slice_fusion.5), channel_id=1, source_target_pairs={{0,4},{4,0},{8,12},{12,8},{16,20},{20,16},{24,28},{28,24},{1,5},{5... | collective-permute-start | bytes 2752520 | tf_op jit(solution)/shard_map/ppermute | solution.py:915
  640.9 47.3 %collective-permute-start.62 = (bf16[256,1792]{1,0:T(8,128)(2,1)}, bf16[256,1792]{1,0:T(8,128)(2,1)}, u32[]{:S(2)}, u32[]{:S(2)}) collective-permute-start(bf16[256,1792]{1,0:T(8,128)(2,1)} %constant_dynamic-slice_fusion.3), channel_id=1, source_target_pairs={{0,8},{4,12},{8,0},{12,4},{16,24},{20,28},{24,16},{28,20},{1,9},{5... | collective-permute-start | bytes 2752520 | tf_op jit(solution)/shard_map/ppermute | solution.py:915
  642.5 49.5 %collective-permute-start.50 = (bf16[512,1024]{1,0:T(8,128)(2,1)}, bf16[512,1024]{1,0:T(8,128)(2,1)S(1)}, u32[]{:S(2)}, u32[]{:S(2)}) collective-permute-start(bf16[512,1024]{1,0:T(8,128)(2,1)} %add_convert_fusion.1), channel_id=1, source_target_pairs={{0,2},{1,3},{2,0},{3,1},{4,6},{5,7},{6,4},{7,5},{8,10},{9,11},{10,... | collective-permute-start | bytes 3145736 | tf_op jit(solution)/shard_map/ppermute | solution.py:915
  690.4 26.0 %collective-permute-start.40 = (bf16[512,1024]{1,0:T(8,128)(2,1)S(1)}, bf16[512,1024]{1,0:T(8,128)(2,1)S(1)}, u32[]{:S(2)}, u32[]{:S(2)}) collective-permute-start(bf16[512,1024]{1,0:T(8,128)(2,1)S(1)} %copy-done.56), channel_id=1, source_target_pairs={{0,2},{1,3},{2,0},{3,1},{4,6},{5,7},{6,4},{7,5},{8,10},{9,11},{10,... | collective-permute-start | bytes 3145736 | tf_op jit(solution)/shard_map/ppermute | solution.py:915
  692.0 46.5 %collective-permute-start.43 = (bf16[512,1024]{1,0:T(8,128)(2,1)S(1)}, bf16[512,1024]{1,0:T(8,128)(2,1)S(1)}, u32[]{:S(2)}, u32[]{:S(2)}) collective-permute-start(bf16[512,1024]{1,0:T(8,128)(2,1)S(1)} %copy-done.57), channel_id=1, source_target_pairs={{0,2},{1,3},{2,0},{3,1},{4,6},{5,7},{6,4},{7,5},{8,10},{9,11},{10,... | collective-permute-start | bytes 3145736 | tf_op jit(solution)/shard_map/ppermute | solution.py:915
  695.8 49.1 %collective-permute-start.67 = (bf16[640,1024]{1,0:T(8,128)(2,1)S(1)}, bf16[640,1024]{1,0:T(8,128)(2,1)S(1)}, u32[]{:S(2)}, u32[]{:S(2)}) collective-permute-start(bf16[640,1024]{1,0:T(8,128)(2,1)S(1)} %copy-done.51), channel_id=1, source_target_pairs={{0,4},{4,0},{8,12},{12,8},{16,20},{20,16},{24,28},{28,24},{1,5},{5... | collective-permute-start | bytes 3932168 | tf_op jit(solution)/shard_map/ppermute | solution.py:915
  698.4 91.1 %collective-permute-start.45 = (bf16[512,1024]{1,0:T(8,128)(2,1)S(1)}, bf16[512,1024]{1,0:T(8,128)(2,1)S(1)}, u32[]{:S(2)}, u32[]{:S(2)}) collective-permute-start(bf16[512,1024]{1,0:T(8,128)(2,1)S(1)} %copy-done.89), channel_id=1, source_target_pairs={{0,1},{1,0},{2,3},{3,2},{4,5},{5,4},{6,7},{7,6},{8,9},{9,8},{10,11... | collective-permute-start | bytes 3145736 | tf_op jit(solution)/shard_map/ppermute | solution.py:915
  698.5 47.8 %collective-permute-start.58 = (bf16[128,1792]{1,0:T(8,128)(2,1)S(1)}, bf16[128,1792]{1,0:T(8,128)(2,1)S(1)}, u32[]{:S(2)}, u32[]{:S(2)}) collective-permute-start(bf16[128,1792]{1,0:T(8,128)(2,1)S(1)} %constant_dynamic-slice_fusion.4), channel_id=1, source_target_pairs={{0,8},{4,12},{8,0},{12,4},{16,24},{20,28},{24,16},{28,20},{1,9},{5... | collective-permute-start | bytes 1376264 | tf_op jit(solution)/shard_map/ppermute | solution.py:915
  716.4 30.8 %collective-permute-start.63 = (bf16[128,1792]{1,0:T(8,128)(2,1)S(1)}, bf16[128,1792]{1,0:T(8,128)(2,1)S(1)}, u32[]{:S(2)}, u32[]{:S(2)}) collective-permute-start(bf16[128,1792]{1,0:T(8,128)(2,1)S(1)} %constant_dynamic-slice_fusion.2), channel_id=1, source_target_pairs={{0,16},{4,20},{8,24},{12,28},{16,0},{20,4},{24,8},{28,12},{1,17},{... | collective-permute-start | bytes 1376264 | tf_op jit(solution)/shard_map/ppermute | solution.py:915
  738.5 54.0 %collective-permute-start.47 = (bf16[512,1024]{1,0:T(8,128)(2,1)S(1)}, bf16[512,1024]{1,0:T(8,128)(2,1)S(1)}, u32[]{:S(2)}, u32[]{:S(2)}) collective-permute-start(bf16[512,1024]{1,0:T(8,128)(2,1)S(1)} %add_convert_fusion.3), channel_id=1, source_target_pairs={{0,2},{1,3},{2,0},{3,1},{4,6},{5,7},{6,4},{7,5},{8,10},{9,11},{10,... | collective-permute-start | bytes 3145736 | tf_op jit(solution)/shard_map/ppermute | solution.py:915
  744.9 56.3 %collective-permute-start.44 = (bf16[512,1024]{1,0:T(8,128)(2,1)S(1)}, bf16[512,1024]{1,0:T(8,128)(2,1)S(1)}, u32[]{:S(2)}, u32[]{:S(2)}) collective-permute-start(bf16[512,1024]{1,0:T(8,128)(2,1)S(1)} %get-tuple-element.209), channel_id=1, source_target_pairs={{0,1},{1,0},{2,3},{3,2},{4,5},{5,4},{6,7},{7,6},{8,9},{9,8},{10,11... | collective-permute-start | bytes 3145736 | tf_op jit(solution)/shard_map/ppermute | solution.py:915
  746.3 41.4 %collective-permute-start.68 = (bf16[320,1024]{1,0:T(8,128)(2,1)S(1)}, bf16[320,1024]{1,0:T(8,128)(2,1)S(1)}, u32[]{:S(2)}, u32[]{:S(2)}) collective-permute-start(bf16[320,1024]{1,0:T(8,128)(2,1)S(1)} %constant_dynamic-slice_fusion), channel_id=1, source_target_pairs={{0,8},{4,12},{8,0},{12,4},{16,24},{20,28},{24,16},{28,20},{1,9},{5... | collective-permute-start | bytes 1966088 | tf_op jit(solution)/shard_map/ppermute | solution.py:915
  783.5 42.7 %collective-permute-start.60 = (bf16[128,1792]{1,0:T(8,128)(2,1)S(1)}, bf16[128,1792]{1,0:T(8,128)(2,1)S(1)}, u32[]{:S(2)}, u32[]{:S(2)}) collective-permute-start(bf16[128,1792]{1,0:T(8,128)(2,1)S(1)} %add_convert_fusion.23), channel_id=1, source_target_pairs={{0,8},{4,12},{8,0},{12,4},{16,24},{20,28},{24,16},{28,20},{1,9},{5... | collective-permute-start | bytes 1376264 | tf_op jit(solution)/shard_map/ppermute | solution.py:915
  787.7 38.3 %collective-permute-start.65 = (bf16[128,1792]{1,0:T(8,128)(2,1)S(1)}, bf16[128,1792]{1,0:T(8,128)(2,1)S(1)}, u32[]{:S(2)}, u32[]{:S(2)}) collective-permute-start(bf16[128,1792]{1,0:T(8,128)(2,1)S(1)} %add_convert_fusion.21), channel_id=1, source_target_pairs={{0,16},{4,20},{8,24},{12,28},{16,0},{20,4},{24,8},{28,12},{1,17},{... | collective-permute-start | bytes 1376264 | tf_op jit(solution)/shard_map/ppermute | solution.py:915
  789.5 48.5 %collective-permute-start.69 = (bf16[320,1024]{1,0:T(8,128)(2,1)}, bf16[320,1024]{1,0:T(8,128)(2,1)}, u32[]{:S(2)}, u32[]{:S(2)}) collective-permute-start(bf16[320,1024]{1,0:T(8,128)(2,1)} %add_convert_fusion.20), channel_id=1, source_target_pairs={{0,16},{4,20},{8,24},{12,28},{16,0},{20,4},{24,8},{28,12},{1,17},{... | collective-permute-start | bytes 1966088 | tf_op jit(solution)/shard_map/ppermute | solution.py:915
  801.1 67.5 %collective-permute-start.51 = (f32[512,1024]{1,0:T(8,128)}, f32[512,1024]{1,0:T(8,128)}, u32[]{:S(2)}, u32[]{:S(2)}) collective-permute-start(f32[512,1024]{1,0:T(8,128)} %get-tuple-element.202), channel_id=1, source_target_pairs={{0,1},{1,0},{2,3},{3,2},{4,5},{5,4},{6,7},{7,6},{8,9},{9,8},{10,11... | collective-permute-start | bytes 6291464 | tf_op jit(solution)/shard_map/ppermute | solution.py:915
  826.1 28.4 %collective-permute-start.66 = (bf16[256,1792]{1,0:T(8,128)(2,1)S(1)}, bf16[256,1792]{1,0:T(8,128)(2,1)}, u32[]{:S(2)}, u32[]{:S(2)}) collective-permute-start(bf16[256,1792]{1,0:T(8,128)(2,1)S(1)} %pad_maximum_fusion.10), channel_id=1, source_target_pairs={{0,8},{4,12},{8,0},{12,4},{16,24},{20,28},{24,16},{28,20},{1,9},{5... | collective-permute-start | bytes 2752520 | tf_op jit(solution)/shard_map/ppermute | solution.py:915
  827.4 28.8 %collective-permute-start.61 = (bf16[256,1792]{1,0:T(8,128)(2,1)}, bf16[256,1792]{1,0:T(8,128)(2,1)}, u32[]{:S(2)}, u32[]{:S(2)}) collective-permute-start(bf16[256,1792]{1,0:T(8,128)(2,1)} %pad_maximum_fusion.9), channel_id=1, source_target_pairs={{0,4},{4,0},{8,12},{12,8},{16,20},{20,16},{24,28},{28,24},{1,5},{5... | collective-permute-start | bytes 2752520 | tf_op jit(solution)/shard_map/ppermute | solution.py:915
  (118 other events, 1514.9 us)
Sparse Core Ops, SparseCore 0:
  402.7 116.5 all-reduce.3
  524.4 161.9 all-reduce.5

commit v3 on v2

--- a/solution.py
+++ b/solution.py
@@ -671,6 +671,8 @@
 
     def call(self, run, scalars, operands, specs, out_specs, out_shape, **options):
         waits, self.before = self.before, []
+        if self.token is not None:
+            waits = waits + [self.token]
         token_spec = pl.BlockSpec((1, 1), lambda i, *_: (0, 0))
         body = with_token(Timed(run, len(out_shape)), len(scalars) + len(operands), len(waits))
         *results, token = pl.pallas_call(
@@ -910,6 +912,210 @@
     )
 
 
+def join_pair_kernel(keep0, got0, keep1, got1, mine, theirs):
+    mine[...] = (keep0[...].astype(f32) + got0[...].astype(f32)).astype(bf16)
+    theirs[...] = (keep1[...].astype(f32) + got1[...].astype(f32)).astype(bf16)
+
+
+def end_forward_kernel(mine, got, base, dense_bias, down_bias, rows):
+    biases = dense_bias[...].astype(f32) + down_bias[...].astype(f32)
+    summed = mine[...].astype(f32) + got[...].astype(f32)
+    rows[...] = (base[...].astype(f32) + (summed + biases)).astype(bf16)
+
+
+def end_backward_kernel(mine, got, base, before, rows, low):
+    normed_grad = mine[...].astype(f32) + got[...].astype(f32)
+    rows_in = base[...].astype(f32)
+    center = jnp.mean(rows_in, axis=-1, keepdims=True)
+    shifted = rows_in - center
+    spread = jnp.mean(shifted * shifted, axis=-1, keepdims=True)
+    inverse = lax.rsqrt(spread + norm_eps)
+    normal = shifted * inverse
+    along = jnp.mean(normed_grad * normal, axis=-1, keepdims=True)
+    level = jnp.mean(normed_grad, axis=-1, keepdims=True)
+    total = before[...].astype(f32) + inverse * (normed_grad - level - normal * along)
+    rows[...] = total
+    low[...] = total.astype(bf16)
+
+
+def fold_kernel(qkv_ref, up_ref, order_ref, columns_ref, ordered_ref, wq_ref, wu_ref):
+    columns = columns_ref[...]
+    ordered = dot(qkv_ref[...], order_ref[...])
+    ordered_ref[...] = ordered.astype(bf16)
+    wq_ref[...] = (columns[:, 0:1] * ordered).astype(bf16)
+    wu_ref[...] = (columns[:, 1:2] * up_ref[...].astype(f32)).astype(bf16)
+
+
+def fold_gains(when, qkv, up, order, columns):
+    model, hidden = up.shape
+    span = order.shape[1]
+    rows = min(256, model)
+    by_rows = lambda cols: pl.BlockSpec((rows, cols), lambda i, *_: (i, 0))
+    return when.call(
+        fold_kernel,
+        [],
+        [qkv, up, order, columns],
+        [by_rows(qkv.shape[1]), by_rows(hidden), whole_spec(order), by_rows(columns.shape[1])],
+        [by_rows(span), by_rows(span), by_rows(hidden)],
+        [
+            jax.ShapeDtypeStruct((model, span), bf16),
+            jax.ShapeDtypeStruct((model, span), bf16),
+            jax.ShapeDtypeStruct((model, hidden), bf16),
+        ],
+        grid=(model // rows,),
+        name="fold_gains",
+    )
+
+
+def by_blocks(when, kernel, sets, small, types, name):
+    rows, cols = sets[0][0].shape
+    block = min(256, rows)
+    spec = pl.BlockSpec((block, cols), lambda i, *_: (i, 0))
+    each, made = len(sets[0]), len(types)
+
+    def body(*refs):
+        ins, outs = refs[: len(sets) * each + len(small)], refs[len(sets) * each + len(small) :]
+        for j in range(len(sets)):
+            kernel(
+                *ins[j * each : (j + 1) * each],
+                *ins[len(sets) * each :],
+                *outs[j * made : (j + 1) * made],
+            )
+
+    results = when.call(
+        body,
+        [],
+        [a for one in sets for a in one] + list(small),
+        [spec] * (len(sets) * each) + [whole_spec(a) for a in small],
+        [spec] * (len(sets) * made),
+        [jax.ShapeDtypeStruct((rows, cols), t) for _ in sets for t in types],
+        grid=(rows // block,),
+        name=name,
+    )
+    return [results[j * made : (j + 1) * made] for j in range(len(sets))]
+
+
+def join_halves(when, items):
+    scalars, operands, specs, outs, shapes, count = [], [], [], [], [], []
+    for j, (now, bit, got, after_bit) in enumerate(items):
+        half, cols = got.shape
+        block = half // 2
+        scalars += [jnp.int32(0) if bit is None else bit, jnp.int32(0) if after_bit is None else after_bit]
+
+        def chosen(g, table, j=j, split=after_bit is not None):
+            return jnp.where(g == 0, table[2 * j + 1], 1 - table[2 * j + 1]) if split else g
+
+        def now_index(g, table, j=j, chosen=chosen, whole=bit is not None):
+            at = chosen(g, table)
+            return (table[2 * j] * 2 + at if whole else at), 0
+
+        def got_index(g, table, chosen=chosen):
+            return chosen(g, table), 0
+
+        operands += [now, got]
+        specs += [pl.BlockSpec((block, cols), now_index), pl.BlockSpec((block, cols), got_index)]
+        if after_bit is None:
+            outs.append(pl.BlockSpec((block, cols), lambda g, table: (g, 0)))
+            shapes.append(jax.ShapeDtypeStruct((half, cols), bf16))
+            count.append(1)
+        else:
+            outs += [pl.BlockSpec((block, cols), lambda g, table: (0, 0))] * 2
+            shapes += [jax.ShapeDtypeStruct((block, cols), bf16)] * 2
+            count.append(2)
+
+    def kernel(table_ref, *refs):
+        ins, made = refs[: 2 * len(items)], refs[2 * len(items) :]
+        step = pl.program_id(0)
+        at = 0
+        for j, outputs in enumerate(count):
+            total = (ins[2 * j][...].astype(f32) + ins[2 * j + 1][...].astype(f32)).astype(bf16)
+            if outputs == 1:
+                made[at][...] = total
+            else:
+                for side in range(2):
+
+                    @pl.when(step == side)
+                    def _():
+                        made[at + side][...] = total
+
+            at += outputs
+
+    results = when.call(
+        kernel, [jnp.stack(scalars).astype(jnp.int32)], operands, specs, outs, shapes, grid=(2,), name="join_halves"
+    )
+    grouped, at = [], 0
+    for outputs in count:
+        grouped.append(results[at : at + outputs])
+        at += outputs
+    return grouped
+
+
+def assemble(when, pieces, own):
+    rows, cols = pieces[0].shape
+    count = len(pieces)
+
+    def kernel(own_ref, *refs):
+        ins, out = refs[:count], refs[count]
+        key = jnp.bitwise_xor(pl.program_id(0), own_ref[0])
+        for m in range(count):
+
+            @pl.when(key == m)
+            def _():
+                out[...] = ins[m][...]
+
+    return when.call(
+        kernel,
+        [jnp.reshape(own, (1,)).astype(jnp.int32)],
+        list(pieces),
+        [whole_spec(p) for p in pieces],
+        [pl.BlockSpec((rows, cols), lambda i, *_: (i, 0))],
+        [jax.ShapeDtypeStruct((rows * count, cols), bf16)],
+        grid=(count,),
+        name="assemble",
+    )[0]
+
+
+def finish_sums(when, held, constants, emit, shapes, name):
+    layers = len(held)
+    owns, operands, places = [], [], []
+    for l, arrays in enumerate(held):
+        first = 0
+        for pieces, own in arrays:
+            for m, piece in enumerate(pieces):
+                operands.append(piece)
+                places.append((l, len(owns), m, first))
+            owns.append(own)
+            first += piece.shape[0] * len(pieces)
+    cols = operands[0].shape[1]
+
+    def kernel(own_ref, *refs):
+        ins = refs[: len(operands)]
+        fixed = refs[len(operands) : len(operands) + len(constants)]
+        outs, rows_ref = refs[len(operands) + len(constants) : -1], refs[-1]
+        step = pl.program_id(0)
+        for ref, (l, j, m, start) in zip(ins, places):
+            count = ref.shape[0]
+
+            @pl.when(step == l)
+            def _():
+                place = start + jnp.bitwise_xor(own_ref[j], m) * count
+                rows_ref[pl.ds(pl.multiple_of(place, 16), count), :] = ref[...]
+
+        emit(rows_ref, fixed, outs)
+
+    return when.call(
+        kernel,
+        [jnp.stack([jnp.asarray(o, jnp.int32) for o in owns])],
+        operands + list(constants),
+        [whole_spec(a) for a in operands + list(constants)],
+        [pl.BlockSpec((1,) + shape, lambda i, *_: (i, 0, 0)) for shape in shapes],
+        [jax.ShapeDtypeStruct((layers,) + shape, f32) for shape in shapes],
+        grid=(layers,),
+        scratch_shapes=[pltpu.VMEM((first, cols), bf16)],
+        name=name,
+    )
+
+
 def swapped(array, axis, distance):
     size = lax.axis_size(axis)
     return lax.ppermute(array, axis, [(i, i ^ distance) for i in range(size)])
@@ -948,9 +1154,7 @@
         keep0, send0, keep1, send1 = partial_sums
         when.before += [send0, send1]
         return [keep0, keep1], [swapped(send0, "tensor", 1), swapped(send1, "tensor", 1)]
-    model = partial_sums[0].shape[1]
-    share = partial_sums[0].shape[0] // (2 * inner)
-    now = [half.reshape(inner, share, model) for half in jnp.split(partial_sums[0], 2)]
+    now = jnp.split(partial_sums[0], 2)
     for distance in reversed(distances(inner)):
         half = now[0].shape[0] // 2
         bit = bit_of("tensor", distance)
@@ -958,50 +1162,69 @@
         send = [lax.dynamic_slice_in_dim(one, (1 - bit) * half, half, 0) for one in now]
         got = [swapped(one, "tensor", distance) for one in send]
         if distance > 1:
-            now = reduce_join((keep, got), when)
-    return [one.reshape(share, model) for one in keep], [one.reshape(share, model) for one in got]
+            (now,) = reduce_join([(keep, got)], when)
+    return keep, got
 
 
 def reduce_join(pending, when):
-    keep, got = pending
-    return [
-        when.after(keep[side].astype(f32) + got[side].astype(f32)).astype(bf16)
-        for side in range(2)
-    ]
-
-
-def sum_over_dp(array, order, when):
-    now = array
-    kept = []
-    for distance in order[:-1]:
-        half = now.shape[0] // 2
-        bit = bit_of("dp", distance)
-        send = lax.dynamic_slice_in_dim(now, (1 - bit) * half, half, 0)
+    return by_blocks(
+        when,
+        join_pair_kernel,
+        [[keep[0], got[0], keep[1], got[1]] for keep, got in pending],
+        [],
+        [bf16, bf16],
+        "join_pair",
+    )
+
+
+def sum_over_dp(arrays, orders, when, whole=False):
+    nows, gots, wholes = list(arrays), [], []
+    for array, order in zip(arrays, orders):
+        half = array.shape[0] // 2
+        bit = bit_of("dp", order[0])
+        send = lax.dynamic_slice_in_dim(array, (1 - bit) * half, half, 0)
         when.before.append(send)
-        got = swapped(send, "dp", distance)
+        gots.append(swapped(send, "dp", order[0]))
+        wholes.append(bit)
+    yield
+    for stage in range(1, len(orders[0])):
+        halving = stage < len(orders[0]) - 1
+        items = [
+            (now, whole, got, bit_of("dp", order[stage]) if halving else None)
+            for now, whole, got, order in zip(nows, wholes, gots, orders)
+        ]
+        made = join_halves(when, items)
+        nows = [one[0] for one in made]
+        gots = [swapped(one[-1], "dp", order[stage]) for one, order in zip(made, orders)]
+        wholes = [None] * len(nows)
         yield
-        keep = lax.dynamic_slice_in_dim(now, bit * half, half, 0)
-        now = when.after(keep.astype(f32) + got.astype(f32)).astype(bf16)
-        kept.append(distance)
-    when.before.append(now)
-    got = swapped(now, "dp", order[-1])
+    items = [(now, None, got, None) for now, got in zip(nows, gots)]
+    nows = [one[0] for one in join_halves(when, items)]
+    held = []
+    for now, order in zip(nows, orders):
+        pieces = {0: now}
+        kept = order[:-1]
+        for j in reversed(range(len(kept))):
+            key = 1 << (len(kept) - 1 - j)
+            pieces.update(
+                {m | key: swapped(p, "dp", kept[j]) for m, p in list(pieces.items())}
+            )
+        held.append(pieces)
     yield
-    now = when.after(now.astype(f32) + got.astype(f32)).astype(bf16)
-    for distance in reversed(kept):
-        when.before.append(now)
-        got = swapped(now, "dp", distance)
-        yield
-        upper = bit_of("dp", distance) == 1
-        now = jnp.concatenate(
-            [when.after(jnp.where(upper, got, now)), when.after(jnp.where(upper, now, got))],
-            axis=0,
-        )
-    return now
+    results = []
+    for pieces, order in zip(held, orders):
+        kept = order[:-1]
+        own = sum(bit_of("dp", d) * (1 << (len(kept) - 1 - j)) for j, d in enumerate(kept))
+        pieces = [pieces[m] for m in range(len(pieces))]
+        if whole:
+            pieces, own = [assemble(when, pieces, own)], 0
+        results.append((pieces, own))
+    return results
 
 
 class Sum:
-    def __init__(self, array, order, when):
-        self.run = sum_over_dp(array, order, when)
+    def __init__(self, arrays, orders, when, whole=False):
+        self.run = sum_over_dp(arrays, orders, when, whole)
         self.value = None
         self.step()
 
@@ -1107,14 +1330,14 @@
     place = jnp.full((1,), inner_index, jnp.int32)
 
     xs = to_shares(tokens, inner, parts)
+    columns = [
+        jnp.stack([gains[l, 0], gains[l, 1], shifts[l, 0], shifts[l, 1]], axis=1)
+        for l in range(layers)
+    ]
+
     def fold(l):
         qkv, up, dense, down = qkv_weight[l], up_weight[l], dense_weight[l], down_weight[l]
-        gain_one, gain_two = gains[l, 0][:, None], gains[l, 1][:, None]
-        if l > 0:
-            gain_one, gain_two = when.after(gain_one), when.after(gain_two)
-        ordered = dot(qkv, order).astype(bf16)
-        wq = (gain_one * ordered.astype(f32)).astype(bf16)
-        wu = (gain_two * up.astype(f32)).astype(bf16)
+        ordered, wq, wu = fold_gains(when, qkv, up, order, columns[l])
         bias_one = dot(norm_shifts[l, 0:1], qkv) + qkv_bias[l].astype(f32)[None]
         bq = jnp.dot(bias_one, order.astype(f32), precision=lax.Precision.HIGHEST)
         bu = dot(norm_shifts[l, 1:2], up) + up_bias[l].astype(f32)[None]
@@ -1124,9 +1347,9 @@
         return (wq, bq, wu, bu, wo), ordered
 
     folded = [None] * layers
+    when.before += [cosine, sine, *xs]
     folded[0] = fold(0)
     crossing_x = [swapped(xs[0], "tensor", inner), None]
-    when.mark(cosine, sine, *folded[0][0])
     x_parts = [None] * parts
     x_parts[0] = (
         inner_source(xs[0], inner),
@@ -1136,7 +1359,7 @@
     sent = when.after(xs[1])
     crossing_x[1] = swapped(sent, "tensor", inner)
     when.before.append(sent)
-    when.token = None
+
     inputs = [None] * layers
     saved = [[None] * parts for _ in range(layers)]
     sums = [[None] * parts for _ in range(layers)]
@@ -1153,33 +1376,32 @@
     def begin_reduce(partial_sum):
         return reduce_start(partial_sum, inner, when)
 
-    def cross_reduce(pending):
-        mine, theirs = reduce_join(pending, when)
-        when.before += [mine, theirs]
-        return mine, swapped(theirs, "tensor", inner)
-
-    def end_forward(l, part, crossing):
-        mine, got = crossing
-        biases = dense_bias[l].astype(f32) + down_bias[l].astype(f32)
-        summed = when.after(mine.astype(f32) + got.astype(f32))
-        rows = (inputs[l][part].astype(f32) + (summed + biases)).astype(bf16)
-        when.before.append(rows)
-        return rows
-
-    def end_backward(l, part, crossing):
-        mine, got = crossing
-        normed_grad = when.after(mine.astype(f32) + got.astype(f32))
-        rows_in = inputs[l][part].astype(f32)
-        center = jnp.mean(rows_in, axis=-1, keepdims=True)
-        shifted = rows_in - center
-        spread = jnp.mean(shifted * shifted, axis=-1, keepdims=True)
-        inverse = lax.rsqrt(spread + norm_eps)
-        normal = shifted * inverse
-        along = jnp.mean(normed_grad * normal, axis=-1, keepdims=True)
-        level = jnp.mean(normed_grad, axis=-1, keepdims=True)
-        rows = incoming[part] + inverse * (normed_grad - level - normal * along)
-        when.before.append(rows)
-        return rows
+    def cross_reduce(*pending):
+        crossings = [
+            (mine, swapped(theirs, "tensor", inner)) for mine, theirs in reduce_join(pending, when)
+        ]
+        return crossings if len(crossings) > 1 else crossings[0]
+
+    def end_forward(l, ends):
+        made = by_blocks(
+            when,
+            end_forward_kernel,
+            [[*crossing, inputs[l][part]] for part, crossing in ends],
+            [dense_bias[l : l + 1], down_bias[l : l + 1]],
+            [bf16],
+            "end_forward",
+        )
+        return [one[0] for one in made]
+
+    def end_backward(l, ends):
+        return by_blocks(
+            when,
+            end_backward_kernel,
+            [[*crossing, inputs[l][part], incoming[part]] for part, crossing in ends],
+            [],
+            [f32, bf16],
+            "end_backward",
+        )
 
     def whole_part(share_rows, crossing):
         return inner_source(share_rows, inner), inner_source(when.after(crossing), inner)
@@ -1189,7 +1411,7 @@
         return swapped(rows, "tensor", inner)
 
     out_grad_shares = to_shares(out_grad, inner, parts)
-    incoming = [rows.astype(f32) for rows in out_grad_shares]
+    incoming = out_grad_shares
     grads = [None] * parts
     crossing_grad = [None] * parts
 
@@ -1206,15 +1428,14 @@
             crossing0 = cross_reduce(pending)
             state = run_forward(l, 1, state)
             pending = begin_reduce(sums[l][1])
-            x0 = end_forward(l, 0, crossing0)
+            (x0,) = end_forward(l, [(0, crossing0)])
             far0 = send_across(x0)
-            when.mark(x0)
             crossing1 = cross_reduce(pending)
             folded[l + 1] = fold(l + 1)
-            x1 = end_forward(l, 1, crossing1)
+            x_parts = [whole_part(x0, far0), None]
+            (x1,) = end_forward(l, [(1, crossing1)])
             far1 = send_across(x1)
             xs = [x0, x1]
-            x_parts = [whole_part(x0, far0), None]
         else:
             x_parts[1] = whole_part(xs[1], far1)
             send_out_grad(1)
@@ -1254,13 +1475,12 @@
 
     def in_weights(l, dzs, dbs, bias_grad, pieces):
         db = sum(dbs)
-        columns = jnp.stack([gains[l, 0], gains[l, 1], shifts[l, 0], shifts[l, 1]], axis=1)
         *made, norm_sums = in_weight_grad(
             when,
             [kept[0] for kept in saved[l]],
             dzs,
             db,
-            columns,
+            columns[l],
             folded[l][1],
             up_weight[l],
             block,
@@ -1289,63 +1509,110 @@
             grads[0] = whole_part(far0[0], far0[1])
         if l > 0:
             pending1 = begin_reduce(dx1)
-            out_sum = out_weights(l)
-            turned = list(range(dp_size))[::-1]
-            out_sum = lax.psum(out_sum, "dp", axis_index_groups=[turned])
+            out_sum = Sum([out_weights(l)], [early_x], when, True)
+            running.append(out_sum)
             crossing1 = cross_reduce(pending1)
             dz0, dx0, db0, state = run_backward(l, 0, state)
-            g1 = end_backward(l, 1, crossing1)
-            low1 = g1.astype(bf16)
+            ((g1, low1),) = end_backward(l, [(1, crossing1)])
             far1 = send_across(low1)
             pending0 = begin_reduce(dx0)
+            advance()
             crossing0 = cross_reduce(pending0)
-            (made,) = in_weights(l, [dz0, dz1], [db0, db1], bias_grad, 1)
-            when.before.append(made)
-            weight_sums[l] = (out_sum, lax.psum(made, "dp"))
-            g0 = end_backward(l, 0, crossing0)
-            low0 = g0.astype(bf16)
+            made = in_weights(l, [dz0, dz1], [db0, db1], bias_grad, 1)
+            advance()
+            grads = [None, whole_part(low1, far1)]
+            in_sum = Sum(made, [early_x], when, True)
+            running.append(in_sum)
+            weight_sums[l] = (out_sum, in_sum)
+            ((g0, low0),) = end_backward(l, [(0, crossing0)])
             far0 = (low0, send_across(low0))
-            grads = [None, whole_part(low1, far1)]
             incoming = [g0, g1]
         else:
-            out_made = out_weights(l)
-            if l < last:
-                when.before.append(weight_sums[l + 1][0])
+            advance()
+            out_sum = Sum([out_weights(l)], [early_x], when)
+            advance()
+            running.append(out_sum)
             dz0, dx0, db0, state = run_backward(l, 0, state)
+            advance()
             made = in_weights(l, [dz0, dz1], [db0, db1], bias_grad, 2)
-            running += [
-                Sum(made[0], early_x, when),
-                Sum(made[1], late_x, when),
-                Sum(out_made, early_x, when),
-            ]
-            weight_sums[l] = (running[2], running[0], running[1])
-            pending = [begin_reduce(dx) for dx in (dx1, dx0)]
-            crossing = [cross_reduce(one) for one in pending]
-            incoming = [end_backward(l, part, crossing[1 - part]) for part in range(parts)]
-            out_pending = [begin_reduce(one) for one in sums[last]]
-            out_crossing = [cross_reduce(one) for one in out_pending]
-
+            final = Sum(made, [early_x, late_x], when)
+            weight_sums[l] = (out_sum, final)
+
+    norm_rows = jnp.concatenate([one[0] for one in small], axis=0)
+    span = small[0][1].shape[1]
+    norm_rows = jnp.pad(norm_rows, ((0, 0), (0, max(span - model, 0))))
+    bias_rows = jnp.concatenate([one[1] for one in small], axis=0)
+    bias_rows = jnp.pad(bias_rows, ((0, 0), (0, max(model - span, 0))))
+    small_rows = jnp.concatenate([norm_rows, bias_rows], axis=0)
+    small_exchanges = [("dp", d) for d in distances(dp_size)]
+    small_exchanges += [("tensor", d) for d in distances(size)]
+
+    def small_steps(rows):
+        for axis, distance in small_exchanges:
+            sent = when.after(rows)
+            when.before.append(sent)
+            got = swapped(sent, axis, distance)
+            yield
+            summed = when.after(rows + got)
+            if axis == "tensor":
+                summed = jnp.concatenate([summed[: 5 * layers], rows[5 * layers :]], axis=0)
+            rows = summed
+        yield rows
+
+    small_run = small_steps(small_rows)
+
+    pending = [begin_reduce(one) for one in (dx0, dx1)]
+    advance()
+    crossing = cross_reduce(*pending)
+    next(small_run)
+    final.step()
+    next(small_run)
+    pending = [begin_reduce(one) for one in sums[last]]
+    out_crossing = cross_reduce(*pending)
+    advance()
+    final.step()
+    next(small_run)
+    incoming = [one[0] for one in end_backward(0, list(enumerate(crossing)))]
+    tokens_grad = to_placement(incoming, inner)
+    advance()
+    final.step()
+    next(small_run)
+    results = end_forward(last, list(enumerate(out_crossing)))
+    result = to_placement(results, inner)
     while any(one.value is None for one in running):
         advance()
-    weight_grads = []
-    for l in range(layers):
-        out_sum, *in_sums = [
-            one.finish() if isinstance(one, Sum) else one for one in weight_sums[l]
-        ]
-        weight_grads.append((out_sum, jnp.concatenate(in_sums, axis=0)))
-    tokens_grad = to_placement(incoming, inner)
-    result = to_placement(
-        [end_forward(last, part, out_crossing[part]) for part in range(parts)], inner
-    )
-    norm_rows = jnp.concatenate([one[0] for one in small], axis=0)
-    bias_rows = jnp.concatenate([one[1] for one in small], axis=0)
-    span = bias_rows.shape[1]
-    bias_rows = jnp.pad(bias_rows, ((0, 0), (0, -span % model))).reshape(-1, model)
-    small_rows = small_sum(jnp.concatenate([norm_rows, bias_rows], axis=0), ("dp",))
-    norm_rows = small_sum(small_rows[: 5 * layers], ("tensor",)).reshape(layers, 5, model)
-    bias_rows = small_rows[5 * layers :].reshape(layers, -1)[:, :span]
-
-    stack = lambda pick: jnp.stack([pick(l) for l in range(layers)])
+    for small_rows in small_run:
+        pass
+    def emit_out(rows_ref, fixed, outs):
+        outs[0][0] = rows_ref[: heads * HS, :].astype(f32)
+        outs[1][0] = rows_ref[width:, :].astype(f32)
+
+    def emit_in(rows_ref, fixed, outs):
+        outs[0][0] = dot_nt(rows_ref[:, : 3 * width], fixed[0][...])
+        outs[1][0] = rows_ref[:, 3 * width :].astype(f32)
+
+    hidden_size = up_weight.shape[2]
+    when.before.append(tokens_grad)
+    dense_total, down_total = finish_sums(
+        when,
+        [sums_of[0].finish() for sums_of in weight_sums],
+        [],
+        emit_out,
+        [(heads * HS, model), (hidden_size, model)],
+        "finish_out",
+    )
+    when.before.append(result)
+    qkv_total, up_total = finish_sums(
+        when,
+        [sums_of[1].finish() for sums_of in weight_sums],
+        [order],
+        emit_in,
+        [(model, heads * 3 * HS), (model, hidden_size)],
+        "finish_in",
+    )
+    bias_rows = small_rows[5 * layers :, :span]
+    norm_rows = small_rows[: 5 * layers, :model].reshape(layers, 5, model)
+
     bias_total = norm_rows[:, 4]
     bias_one = bias_rows[:, : 3 * width]
     return (
@@ -1353,18 +1620,13 @@
         tokens_grad,
         norm_rows[:, 0:2],
         norm_rows[:, 2:4],
-        lax.dot_general(
-            stack(lambda l: weight_grads[l][1][:, : 3 * width]),
-            order,
-            (((2,), (1,)), ((), ())),
-            preferred_element_type=f32,
-        ),
+        qkv_total,
         jnp.dot(bias_one, order.astype(f32).T, precision=lax.Precision.HIGHEST),
-        stack(lambda l: weight_grads[l][0][: heads * HS]).astype(f32),
+        dense_total,
         bias_total,
-        stack(lambda l: weight_grads[l][1][:, 3 * width :]).astype(f32),
+        up_total,
         bias_rows[:, 3 * width :],
-        stack(lambda l: weight_grads[l][0][width:]).astype(f32),
+        down_total,
         bias_total,
     )
 

time: 912 us -> 862 us (0.945)
  Pallas kernels: 371 us -> 525 us
  waiting for transfers between devices: 247 us -> 142 us
  other arithmetic: 136 us -> 40.9 us
  between operations: 22.8 us -> 8.13 us
  starting transfers between devices: 49.9 us -> 59.5 us
  local copies, waits for them, and re-layouts: 46.4 us -> 55.6 us
    pallas_call x15 -> x43, Pallas kernels: 371 us -> 525 us  [call(): pl.pallas_call(body, grid_spec=pltpu.PrefetchScalarGridSpec(num_scalar_pr...]
    ppermute x72 -> x87, waiting for transfers between devices: 224 us -> 142 us  [swapped(): return lax.ppermute(array, axis, [(i, i ^ distance) for i in range(size)])]
    convert_element_type x25 -> x0, other arithmetic: 53.3 us -> none  [the longest x11 27.4 us: reduce_join(): when.after(keep[side].astype(f32) + got[side].astype(f32)).astype(bf16)]
    psum x2 -> x0, waiting for transfers between devices: 22.8 us -> none  [the longest x1 22.8 us: on_device(): out_sum = lax.psum(out_sum, 'dp', axis_index_groups=[turned])]
    reduce_sum x9 -> x0, other arithmetic: 21.2 us -> none  [the longest x3 9.72 us: end_backward(): center = jnp.mean(rows_in, axis=-1, keepdims=True)]
    reduce_sum x3, other arithmetic: 13 us -> 2.28 us  [bias_sum(): jnp.sum(rows.astype(bf16).astype(f32), axis=0, keepdims=True)]
    ppermute x72 -> x87, starting transfers between devices: 49.8 us -> 59.5 us  [swapped(): return lax.ppermute(array, axis, [(i, i ^ distance) for i in range(size)])]
    add x17 -> x18, other arithmetic: 21.2 us -> 14 us  [after(): return array + self.token.astype(array.dtype).reshape((1,) * array.ndim)]
  transfers between devices with their start and end apart: 74 -> 87, of which waited for: 15 -> 18; matrix products, arithmetic and copies ran while one was open for 21% -> 11% of each run, Pallas kernels for 41% -> 59%
where the time goes in v3:
time: 862 us; the launch traced here: 851 us
  Pallas kernels  525 us (61%)
  waiting for transfers between devices  142 us (16%)
  starting transfers between devices  59.5 us (7%)
  local copies, waits for them, and re-layouts  55.6 us (6%)
  other arithmetic  40.9 us (5%)
  matrix products  20.2 us (2%)
    pallas_call x43, Pallas kernels, call(): pl.pallas_call(body, grid_spec=pltpu.PrefetchScalarGridSpec(num_scalar_pr...  525 us
    ppermute x87, waiting for transfers between devices, swapped(): return lax.ppermute(array, axis, [(i, i ^ distance) for i in range(size)])  142 us
    ppermute x87, starting transfers between devices, swapped(): return lax.ppermute(array, axis, [(i, i ^ distance) for i in range(size)])  59.5 us
    unnamed x201, local copies, waits for them, and re-layouts  21.5 us
  transfers between devices with their start and end apart: 87, of which 18 were waited for; matrix products, arithmetic and copies ran while one was open for 11% of the time, Pallas kernels for 59%

profile of v3, /device:TPU:0, one launch (start us, length us, event | category | flops | bytes accessed | tf_op | source)
XLA Modules:
  0.0 851.5 jit_solution(14551610699742098217)
XLA Ops:
  8.1 5.0 fusion.refs_5_.refs_13_.refs_11_
  17.9 5.0 convolution_add_fusion.refs_4_.refs_12_.refs_10_
  22.9 3.9 slice_bitcast_fusion.4
  29.5 6.6 fold_gains.2
  36.7 3.9 collective-permute-done.2.refs_0_
  53.0 32.1 %forward_layer.4 = (bf16[2048,1024]{1,0:T(8,128)(2,1)}, bf16[2048,768]{1,0:T(8,128)(2,1)}, bf16[2048,1280]{1,0:T(8,128)(2,1)}, bf16[2048,256]{1,0:T(8,128)(2,1)}...) custom-call(s32[2,4]{1,0:T(2,128)} %copy-done.84, ...), custom_call_target="tpu_custom_call" | custom-call | tf_op jit(solution)/shard_map/forward_layer/pallas_call | solution.py:678
  92.6 4.0 join_pair.6
  99.4 32.7 %forward_layer.5 = (bf16[2048,1024]{1,0:T(8,128)(2,1)}, bf16[2048,768]{1,0:T(8,128)(2,1)}, bf16[2048,1280]{1,0:T(8,128)(2,1)}, bf16[2048,256]{1,0:T(8,128)(2,1)}...) custom-call(s32[2,4]{1,0:T(2,128)} %copy-done.84, ...), custom_call_target="tpu_custom_call" | custom-call | tf_op jit(solution)/shard_map/forward_layer/pallas_call | solution.py:678
  139.9 4.1 join_pair.7
  150.0 6.9 fold_gains.3
  157.5 6.5 collective-permute-done.11
  165.1 20.6 %collective-permute-done.15.refs_1_ = bf16[512,1024]{1,0:T(8,128)(2,1)S(1)} collective-permute-done((bf16[512,1024]{1,0:T(8,128)(2,1)}, bf16[512,1024]{1,0:T(8,128)(2,1)S(1)}, u32[]{:S(2)}, u32[]{:S(2)}) %collective-permute-start.15) | collective-permute-done | bytes 1048608 | tf_op jit(solution)/shard_map/ppermute | solution.py:1121
  197.8 32.3 %forward_layer.6 = (bf16[2048,1024]{1,0:T(8,128)(2,1)}, bf16[2048,768]{1,0:T(8,128)(2,1)}, bf16[2048,1280]{1,0:T(8,128)(2,1)}, bf16[2048,256]{1,0:T(8,128)(2,1)}...) custom-call(s32[2,4]{1,0:T(2,128)} %copy-done.84, ...), custom_call_target="tpu_custom_call" | custom-call | tf_op jit(solution)/shard_map/forward_layer/pallas_call | solution.py:678
  235.9 32.1 %forward_layer.7 = (bf16[2048,1024]{1,0:T(8,128)(2,1)}, bf16[2048,768]{1,0:T(8,128)(2,1)}, bf16[2048,1280]{1,0:T(8,128)(2,1)}, bf16[2048,256]{1,0:T(8,128)(2,1)}...) custom-call(s32[2,4]{1,0:T(2,128)} %copy-done.84, ...), custom_call_target="tpu_custom_call" | custom-call | tf_op jit(solution)/shard_map/forward_layer/pallas_call | solution.py:678
  273.8 37.2 %backward_layer.4 = (bf16[2048,1792]{1,0:T(8,128)(2,1)}, f32[1,1792]{1,0:T(1,128)}, f32[2,256,256]{2,1,0:T(8,128)}, bf16[512,1024]{1,0:T(8,128)(2,1)}, bf16[512,...) custom-call(s32[2,4]{1,0:T(2,128)} %copy-done.84, ...), custom_call_target="tpu_custom_call" | custom-call | tf_op jit(solution)/shard_map/backward_layer/pallas_call | solution.py:678
  316.0 20.0 %out_weight_grad.2 = (bf16[1280,1024]{1,0:T(8,128)(2,1)}, f32[1,1]{1,0:T(1,128)}) custom-call(s32[1]{0:T(128)} %bitcast.refs_1_.refs_0_, bf16[2048,1280]{1,0:T(8,128)(2,1)} %get-tuple-element.234.refs_1_.refs_14_, bf16[2048,1280]{1,0:T(8,128)(2,1)} %get-tuple-element.227.refs_14_.refs_2_, bf16[512,1024]{1,0:T(8,128)(2,1)} %copy-done.4, ...), custom_call_target="tpu_custom_call" | custom-call | tf_op jit(solution)/shard_map/out_weight_grad/pallas_call | solution.py:678
  338.5 4.1 join_pair.8
  345.4 37.7 %backward_layer.5 = (bf16[2048,1792]{1,0:T(8,128)(2,1)}, f32[1,1792]{1,0:T(1,128)}, f32[2,256,256]{2,1,0:T(8,128)}, bf16[512,1024]{1,0:T(8,128)(2,1)}, bf16[512,...) custom-call(s32[2,4]{1,0:T(2,128)} %copy-done.84, ...), custom_call_target="tpu_custom_call" | custom-call | tf_op jit(solution)/shard_map/backward_layer/pallas_call | solution.py:678
  384.7 4.9 end_backward.3
  390.9 4.4 join_halves.12
  396.3 4.1 join_pair.9
  404.5 28.4 %in_weight_grad.2 = (bf16[1024,1792]{1,0:T(8,128)(2,1)}, f32[1024,128]{1,0:T(8,128)}, f32[1,1]{1,0:T(1,128)}) custom-call(bf16[2048,1024]{1,0:T(8,128)(2,1)} %get-tuple-element.257.refs_0_, bf16[2048,1024]{1,0:T(8,128)(2,1)} %get-tuple-element.258.refs_1_, bf16[2048,1792]{1,0:T(8,128)(2,1)} %get-tuple-element.259.refs_2_, ...), custom_call_target="tpu_custom_call" | custom-call | tf_op jit(solution)/shard_map/in_weight_grad/pallas_call | solution.py:678
  441.9 4.9 end_backward.4
  451.6 37.2 %backward_layer.6 = (bf16[2048,1792]{1,0:T(8,128)(2,1)}, f32[1,1792]{1,0:T(1,128)}, f32[2,256,256]{2,1,0:T(8,128)}, bf16[512,1024]{1,0:T(8,128)(2,1)}, bf16[512,...) custom-call(s32[2,4]{1,0:T(2,128)} %copy-done.84, ...), custom_call_target="tpu_custom_call" | custom-call | tf_op jit(solution)/shard_map/backward_layer/pallas_call | solution.py:678
  494.7 5.0 join_halves.15
  502.5 8.2 collective-permute-done.47.refs_2_
  513.0 20.1 %out_weight_grad.3 = (bf16[1280,1024]{1,0:T(8,128)(2,1)}, f32[1,1]{1,0:T(1,128)}) custom-call(s32[1]{0:T(128)} %bitcast.refs_1_.refs_0_, bf16[2048,1280]{1,0:T(8,128)(2,1)} %get-tuple-element.280.refs_1_.refs_14_, bf16[2048,1280]{1,0:T(8,128)(2,1)} %get-tuple-element.272.refs_14_.refs_2_, bf16[512,1024]{1,0:T(8,128)(2,1)} %get-tuple-element.270.refs_18_.refs_3_.refs_2_, ...), custom_call_target="tpu_custom_call" | custom-call | tf_op jit(solution)/shard_map/out_weight_grad/pallas_call | solution.py:678
  535.6 4.5 assemble.2
  545.5 37.6 %backward_layer.7 = (bf16[2048,1792]{1,0:T(8,128)(2,1)}, f32[1,1792]{1,0:T(1,128)}, f32[2,256,256]{2,1,0:T(8,128)}, bf16[512,1024]{1,0:T(8,128)(2,1)}, bf16[512,...) custom-call(s32[2,4]{1,0:T(2,128)} %copy-done.84, ...), custom_call_target="tpu_custom_call" | custom-call | tf_op jit(solution)/shard_map/backward_layer/pallas_call | solution.py:678
  592.1 20.0 %collective-permute-done.57.refs_2_ = bf16[256,1792]{1,0:T(8,128)(2,1)} collective-permute-done((bf16[256,1792]{1,0:T(8,128)(2,1)}, bf16[256,1792]{1,0:T(8,128)(2,1)}, u32[]{:S(2)}, u32[]{:S(2)}) %collective-permute-start.57) | collective-permute-done | bytes 917536 | tf_op jit(solution)/shard_map/ppermute | solution.py:1121
  613.6 4.5 join_halves.18
  621.2 28.4 %in_weight_grad.3 = (bf16[512,1792]{1,0:T(8,128)(2,1)}, bf16[512,1792]{1,0:T(8,128)(2,1)}, f32[1024,128]{1,0:T(8,128)}, f32[1,1]{1,0:T(1,128)}) custom-call(bf16[2048,1024]{1,0:T(8,128)(2,1)} %get-tuple-element.223.refs_0_, bf16[2048,1024]{1,0:T(8,128)(2,1)} %get-tuple-element.224.refs_1_, bf16[2048,1792]{1,0:T(8,128)(2,1)} %get-tuple-element.294.refs_2_, ...), custom_call_target="tpu_custom_call" | custom-call | tf_op jit(solution)/shard_map/in_weight_grad/pallas_call | solution.py:678
  661.4 5.0 assemble.3
  669.9 5.7 join_pair.10
  681.0 4.9 join_halves.20
  689.8 28.5 %collective-permute-done.68.refs_2_ = bf16[320,1024]{1,0:T(8,128)(2,1)} collective-permute-done((bf16[320,1024]{1,0:T(8,128)(2,1)}, bf16[320,1024]{1,0:T(8,128)(2,1)}, u32[]{:S(2)}, u32[]{:S(2)}) %collective-permute-start.68) | collective-permute-done | bytes 655392 | tf_op jit(solution)/shard_map/ppermute | solution.py:1121
  718.9 6.1 join_pair.11
  730.9 3.7 join_halves.22
  739.4 7.5 end_backward.5
  750.4 10.8 %collective-permute-done.70.refs_2_ = bf16[128,1792]{1,0:T(8,128)(2,1)S(1)} collective-permute-done((bf16[128,1792]{1,0:T(8,128)(2,1)}, bf16[128,1792]{1,0:T(8,128)(2,1)S(1)}, u32[]{:S(2)}, u32[]{:S(2)}) %collective-permute-start.70) | collective-permute-done | bytes 458784 | tf_op jit(solution)/shard_map/ppermute | solution.py:1121
  762.1 3.9 join_halves.23
  768.0 8.1 collective-permute-done.64.refs_4_
  777.0 4.7 end_forward.5
  798.6 11.6 %collective-permute-done.78.refs_2_ = bf16[128,1792]{1,0:T(8,128)(2,1)} collective-permute-done((bf16[128,1792]{1,0:T(8,128)(2,1)}, bf16[128,1792]{1,0:T(8,128)(2,1)}, u32[]{:S(2)}, u32[]{:S(2)}) %collective-permute-start.78) | collective-permute-done | bytes 458784 | tf_op jit(solution)/shard_map/ppermute | solution.py:1121
  811.4 5.9 collective-permute-done.81.refs_6_
  823.2 4.9 collective-permute-done.86.refs_4_
  828.9 8.3 finish_out.1
  838.6 12.1 %finish_in.1 = (f32[2,1024,768]{2,1,0:T(8,128)}, f32[2,1024,1024]{2,1,0:T(8,128)}, f32[1,1]{1,0:T(1,128)}) custom-call(s32[3]{0:T(128)} %pad_add_fusion.2.refs_0_, bf16[128,1792]{1,0:T(8,128)(2,1)} %get-tuple-element.350.refs_1_, bf16[128,1792]{1,0:T(8,128)(2,1)} %collective-permute-done.78.refs_2_, bf16[128,1792]{1,0:T(8,128)(2,1)} %copy-done.77, ...), custom_call_target="tpu_custom_call" | custom-call | tf_op jit(solution)/shard_map/finish_in/pallas_call | solution.py:678
  (462 shorter events, 204.6 us)
Async XLA Ops:
  44.2 42.1 %collective-permute-start.8 = (bf16[512,1024]{1,0:T(8,128)(2,1)S(1)}, bf16[512,1024]{1,0:T(8,128)(2,1)S(1)}, u32[]{:S(2)}, u32[]{:S(2)}) collective-permute-start(bf16[512,1024]{1,0:T(8,128)(2,1)S(1)} %broadcast_add_fusion.9.refs_15_), channel_id=1, source_target_pairs={{0,2},{1,3},{2,0},{3,1},{4,6},{5,7},{6,4},{7,5},{8,10},{9,11},{10,... | collective-permute-start | bytes 3145736 | tf_op jit(solution)/shard_map/ppermute | solution.py:1121
  50.9 47.0 %collective-permute-start.7 = (bf16[512,1024]{1,0:T(8,128)(2,1)S(1)}, bf16[512,1024]{1,0:T(8,128)(2,1)S(1)}, u32[]{:S(2)}, u32[]{:S(2)}) collective-permute-start(bf16[512,1024]{1,0:T(8,128)(2,1)S(1)} %copy-done.2), channel_id=1, source_target_pairs={{0,1},{1,0},{2,3},{3,2},{4,5},{5,4},{6,7},{7,6},{8,9},{9,8},{10,11... | collective-permute-start | bytes 3145736 | tf_op jit(solution)/shard_map/ppermute | solution.py:1121
  96.6 36.7 %collective-permute-start.6 = (bf16[512,1024]{1,0:T(8,128)(2,1)}, bf16[512,1024]{1,0:T(8,128)(2,1)S(1)}, u32[]{:S(2)}, u32[]{:S(2)}) collective-permute-start(bf16[512,1024]{1,0:T(8,128)(2,1)} %get-tuple-element.195), channel_id=1, source_target_pairs={{0,2},{1,3},{2,0},{3,1},{4,6},{5,7},{6,4},{7,5},{8,10},{9,11},{10,... | collective-permute-start | bytes 3145736 | tf_op jit(solution)/shard_map/ppermute | solution.py:1121
  144.1 41.6 %collective-permute-start.15 = (bf16[512,1024]{1,0:T(8,128)(2,1)}, bf16[512,1024]{1,0:T(8,128)(2,1)S(1)}, u32[]{:S(2)}, u32[]{:S(2)}) collective-permute-start(bf16[512,1024]{1,0:T(8,128)(2,1)} %get-tuple-element.210), channel_id=1, source_target_pairs={{0,2},{1,3},{2,0},{3,1},{4,6},{5,7},{6,4},{7,5},{8,10},{9,11},{10,... | collective-permute-start | bytes 3145736 | tf_op jit(solution)/shard_map/ppermute | solution.py:1121
  146.5 48.5 %collective-permute-start.21 = (bf16[512,1024]{1,0:T(8,128)(2,1)}, bf16[512,1024]{1,0:T(8,128)(2,1)}, u32[]{:S(2)}, u32[]{:S(2)}) collective-permute-start(bf16[512,1024]{1,0:T(8,128)(2,1)} %constant_dynamic-slice_fusion.5), channel_id=1, source_target_pairs={{0,1},{1,0},{2,3},{3,2},{4,5},{5,4},{6,7},{7,6},{8,9},{9,8},{10,11... | collective-permute-start | bytes 3145736 | tf_op jit(solution)/shard_map/ppermute | solution.py:1121
  149.5 48.3 %collective-permute-start.10 = (bf16[512,1024]{1,0:T(8,128)(2,1)S(1)}, bf16[512,1024]{1,0:T(8,128)(2,1)}, u32[]{:S(2)}, u32[]{:S(2)}) collective-permute-start(bf16[512,1024]{1,0:T(8,128)(2,1)S(1)} %copy-done.7), channel_id=1, source_target_pairs={{0,1},{1,0},{2,3},{3,2},{4,5},{5,4},{6,7},{7,6},{8,9},{9,8},{10,11... | collective-permute-start | bytes 3145736 | tf_op jit(solution)/shard_map/ppermute | solution.py:1121
  165.1 32.7 %collective-permute-start.14 = (bf16[512,1024]{1,0:T(8,128)(2,1)}, bf16[512,1024]{1,0:T(8,128)(2,1)}, u32[]{:S(2)}, u32[]{:S(2)}) collective-permute-start(bf16[512,1024]{1,0:T(8,128)(2,1)} %broadcast_add_fusion.7.refs_4_), channel_id=1, source_target_pairs={{0,1},{1,0},{2,3},{3,2},{4,5},{5,4},{6,7},{7,6},{8,9},{9,8},{10,11... | collective-permute-start | bytes 3145736 | tf_op jit(solution)/shard_map/ppermute | solution.py:1121
  190.3 40.5 %collective-permute-start.19 = (bf16[512,1024]{1,0:T(8,128)(2,1)}, bf16[512,1024]{1,0:T(8,128)(2,1)}, u32[]{:S(2)}, u32[]{:S(2)}) collective-permute-start(bf16[512,1024]{1,0:T(8,128)(2,1)} %get-tuple-element.211.refs_15_.refs_2_.refs_5_), channel_id=1, source_target_pairs={{0,2},{1,3},{2,0},{3,1},{4,6},{5,7},{6,4},{7,5},{8,10},{9,11},{10,... | collective-permute-start | bytes 3145736 | tf_op jit(solution)/shard_map/ppermute | solution.py:1121
  197.7 36.3 %collective-permute-start.18 = (bf16[512,1024]{1,0:T(8,128)(2,1)S(1)}, bf16[512,1024]{1,0:T(8,128)(2,1)}, u32[]{:S(2)}, u32[]{:S(2)}) collective-permute-start(bf16[512,1024]{1,0:T(8,128)(2,1)S(1)} %copy-done.8), channel_id=1, source_target_pairs={{0,1},{1,0},{2,3},{3,2},{4,5},{5,4},{6,7},{7,6},{8,9},{9,8},{10,11... | collective-permute-start | bytes 3145736 | tf_op jit(solution)/shard_map/ppermute | solution.py:1121
  232.7 36.0 %collective-permute-start.27 = (bf16[512,1024]{1,0:T(8,128)(2,1)S(1)}, bf16[512,1024]{1,0:T(8,128)(2,1)}, u32[]{:S(2)}, u32[]{:S(2)}) collective-permute-start(bf16[512,1024]{1,0:T(8,128)(2,1)S(1)} %broadcast_add_fusion.5.refs_15_), channel_id=1, source_target_pairs={{0,2},{1,3},{2,0},{3,1},{4,6},{5,7},{6,4},{7,5},{8,10},{9,11},{10,... | collective-permute-start | bytes 3145736 | tf_op jit(solution)/shard_map/ppermute | solution.py:1121
  234.1 37.9 %collective-permute-start.26 = (bf16[512,1024]{1,0:T(8,128)(2,1)S(1)}, bf16[512,1024]{1,0:T(8,128)(2,1)S(1)}, u32[]{:S(2)}, u32[]{:S(2)}) collective-permute-start(bf16[512,1024]{1,0:T(8,128)(2,1)S(1)} %get-tuple-element.379.refs_2_.refs_7_.refs_3_), channel_id=1, source_target_pairs={{0,1},{1,0},{2,3},{3,2},{4,5},{5,4},{6,7},{7,6},{8,9},{9,8},{10,11... | collective-permute-start | bytes 3145736 | tf_op jit(solution)/shard_map/ppermute | solution.py:1121
  270.6 41.1 %collective-permute-start.25 = (bf16[512,1024]{1,0:T(8,128)(2,1)S(1)}, bf16[512,1024]{1,0:T(8,128)(2,1)}, u32[]{:S(2)}, u32[]{:S(2)}) collective-permute-start(bf16[512,1024]{1,0:T(8,128)(2,1)S(1)} %broadcast_add_fusion.4.refs_18_), channel_id=1, source_target_pairs={{0,2},{1,3},{2,0},{3,1},{4,6},{5,7},{6,4},{7,5},{8,10},{9,11},{10,... | collective-permute-start | bytes 3145736 | tf_op jit(solution)/shard_map/ppermute | solution.py:1121
  271.9 42.0 %collective-permute-start.24 = (bf16[512,1024]{1,0:T(8,128)(2,1)S(1)}, bf16[512,1024]{1,0:T(8,128)(2,1)}, u32[]{:S(2)}, u32[]{:S(2)}) collective-permute-start(bf16[512,1024]{1,0:T(8,128)(2,1)S(1)} %get-tuple-element.369.refs_3_.refs_2_), channel_id=1, source_target_pairs={{0,1},{1,0},{2,3},{3,2},{4,5},{5,4},{6,7},{7,6},{8,9},{9,8},{10,11... | collective-permute-start | bytes 3145736 | tf_op jit(solution)/shard_map/ppermute | solution.py:1121
  342.6 41.1 %collective-permute-start.35 = (bf16[512,1024]{1,0:T(8,128)(2,1)}, bf16[512,1024]{1,0:T(8,128)(2,1)S(1)}, u32[]{:S(2)}, u32[]{:S(2)}) collective-permute-start(bf16[512,1024]{1,0:T(8,128)(2,1)} %get-tuple-element.250), channel_id=1, source_target_pairs={{0,2},{1,3},{2,0},{3,1},{4,6},{5,7},{6,4},{7,5},{8,10},{9,11},{10,... | collective-permute-start | bytes 3145736 | tf_op jit(solution)/shard_map/ppermute | solution.py:1121
  343.8 47.1 %collective-permute-start.34 = (bf16[640,1024]{1,0:T(8,128)(2,1)S(1)}, bf16[640,1024]{1,0:T(8,128)(2,1)}, u32[]{:S(2)}, u32[]{:S(2)}) collective-permute-start(bf16[640,1024]{1,0:T(8,128)(2,1)S(1)} %copy-done.22), channel_id=1, source_target_pairs={{0,4},{4,0},{8,12},{12,8},{16,20},{20,16},{24,28},{28,24},{1,5},{5... | collective-permute-start | bytes 3932168 | tf_op jit(solution)/shard_map/ppermute | solution.py:1121
  389.6 50.5 %collective-permute-start.41 = (bf16[512,1024]{1,0:T(8,128)(2,1)}, bf16[512,1024]{1,0:T(8,128)(2,1)}, u32[]{:S(2)}, u32[]{:S(2)}) collective-permute-start(bf16[512,1024]{1,0:T(8,128)(2,1)} %get-tuple-element.252.refs_3_.refs_2_.refs_7_), channel_id=1, source_target_pairs={{0,2},{1,3},{2,0},{3,1},{4,6},{5,7},{6,4},{7,5},{8,10},{9,11},{10,... | collective-permute-start | bytes 3145736 | tf_op jit(solution)/shard_map/ppermute | solution.py:1121
  400.4 41.6 %collective-permute-start.36 = (bf16[512,1024]{1,0:T(8,128)(2,1)}, bf16[512,1024]{1,0:T(8,128)(2,1)}, u32[]{:S(2)}, u32[]{:S(2)}) collective-permute-start(bf16[512,1024]{1,0:T(8,128)(2,1)} %get-tuple-element.256), channel_id=1, source_target_pairs={{0,2},{1,3},{2,0},{3,1},{4,6},{5,7},{6,4},{7,5},{8,10},{9,11},{10,... | collective-permute-start | bytes 3145736 | tf_op jit(solution)/shard_map/ppermute | solution.py:1121
  401.6 33.5 %collective-permute-start.37 = (bf16[320,1024]{1,0:T(8,128)(2,1)}, bf16[320,1024]{1,0:T(8,128)(2,1)S(1)}, u32[]{:S(2)}, u32[]{:S(2)}) collective-permute-start(bf16[320,1024]{1,0:T(8,128)(2,1)} %get-tuple-element.267), channel_id=1, source_target_pairs={{0,8},{4,12},{8,0},{12,4},{16,24},{20,28},{24,16},{28,20},{1,9},{5... | collective-permute-start | bytes 1966088 | tf_op jit(solution)/shard_map/ppermute | solution.py:1121
  404.5 45.8 %collective-permute-start.40 = (bf16[512,1024]{1,0:T(8,128)(2,1)S(1)}, bf16[512,1024]{1,0:T(8,128)(2,1)S(1)}, u32[]{:S(2)}, u32[]{:S(2)}) collective-permute-start(bf16[512,1024]{1,0:T(8,128)(2,1)S(1)} %copy-done.12), channel_id=1, source_target_pairs={{0,1},{1,0},{2,3},{3,2},{4,5},{5,4},{6,7},{7,6},{8,9},{9,8},{10,11... | collective-permute-start | bytes 3145736 | tf_op jit(solution)/shard_map/ppermute | solution.py:1121
  434.5 60.1 %collective-permute-start.44 = (bf16[512,1792]{1,0:T(8,128)(2,1)S(1)}, bf16[512,1792]{1,0:T(8,128)(2,1)}, u32[]{:S(2)}, u32[]{:S(2)}) collective-permute-start(bf16[512,1792]{1,0:T(8,128)(2,1)S(1)} %constant_dynamic-slice_fusion.3.refs_4_), channel_id=1, source_target_pairs={{0,4},{4,0},{8,12},{12,8},{16,20},{20,16},{24,28},{28,24},{1,5},{5... | collective-permute-start | bytes 5505032 | tf_op jit(solution)/shard_map/ppermute | solution.py:1121
  446.8 46.4 %collective-permute-start.39 = (bf16[512,1024]{1,0:T(8,128)(2,1)}, bf16[512,1024]{1,0:T(8,128)(2,1)}, u32[]{:S(2)}, u32[]{:S(2)}) collective-permute-start(bf16[512,1024]{1,0:T(8,128)(2,1)} %get-tuple-element.270.refs_18_.refs_3_.refs_2_), channel_id=1, source_target_pairs={{0,2},{1,3},{2,0},{3,1},{4,6},{5,7},{6,4},{7,5},{8,10},{9,11},{10,... | collective-permute-start | bytes 3145736 | tf_op jit(solution)/shard_map/ppermute | solution.py:1121
  447.7 41.8 %collective-permute-start.45 = (bf16[320,1024]{1,0:T(8,128)(2,1)S(1)}, bf16[320,1024]{1,0:T(8,128)(2,1)}, u32[]{:S(2)}, u32[]{:S(2)}) collective-permute-start(bf16[320,1024]{1,0:T(8,128)(2,1)S(1)} %copy-done.65), channel_id=1, source_target_pairs={{0,16},{4,20},{8,24},{12,28},{16,0},{20,4},{24,8},{28,12},{1,17},{... | collective-permute-start | bytes 1966088 | tf_op jit(solution)/shard_map/ppermute | solution.py:1121
  450.3 61.7 %collective-permute-start.38 = (bf16[512,1024]{1,0:T(8,128)(2,1)}, bf16[512,1024]{1,0:T(8,128)(2,1)}, u32[]{:S(2)}, u32[]{:S(2)}) collective-permute-start(bf16[512,1024]{1,0:T(8,128)(2,1)} %get-tuple-element.270.refs_18_.refs_3_.refs_2_), channel_id=1, source_target_pairs={{0,1},{1,0},{2,3},{3,2},{4,5},{5,4},{6,7},{7,6},{8,9},{9,8},{10,11... | collective-permute-start | bytes 3145736 | tf_op jit(solution)/shard_map/ppermute | solution.py:1121
  499.7 40.5 %collective-permute-start.46 = (bf16[256,1792]{1,0:T(8,128)(2,1)}, bf16[256,1792]{1,0:T(8,128)(2,1)}, u32[]{:S(2)}, u32[]{:S(2)}) collective-permute-start(bf16[256,1792]{1,0:T(8,128)(2,1)} %get-tuple-element.287), channel_id=1, source_target_pairs={{0,8},{4,12},{8,0},{12,4},{16,24},{20,28},{24,16},{28,20},{1,9},{5... | collective-permute-start | bytes 2752520 | tf_op jit(solution)/shard_map/ppermute | solution.py:1121
  501.3 34.3 %collective-permute-start.48 = (bf16[320,1024]{1,0:T(8,128)(2,1)}, bf16[320,1024]{1,0:T(8,128)(2,1)}, u32[]{:S(2)}, u32[]{:S(2)}) collective-permute-start(bf16[320,1024]{1,0:T(8,128)(2,1)} %get-tuple-element.288.refs_1_), channel_id=1, source_target_pairs={{0,4},{4,0},{8,12},{12,8},{16,20},{20,16},{24,28},{28,24},{1,5},{5... | collective-permute-start | bytes 1966088 | tf_op jit(solution)/shard_map/ppermute | solution.py:1121
  543.8 41.2 %collective-permute-start.51 = (bf16[256,1792]{1,0:T(8,128)(2,1)}, bf16[256,1792]{1,0:T(8,128)(2,1)S(1)}, u32[]{:S(2)}, u32[]{:S(2)}) collective-permute-start(bf16[256,1792]{1,0:T(8,128)(2,1)} %get-tuple-element.299.refs_1_), channel_id=1, source_target_pairs={{0,16},{4,20},{8,24},{12,28},{16,0},{20,4},{24,8},{28,12},{1,17},{... | collective-permute-start | bytes 2752520 | tf_op jit(solution)/shard_map/ppermute | solution.py:1121
  544.2 45.5 %collective-permute-start.16 = (bf16[512,1024]{1,0:T(8,128)(2,1)S(1)}, bf16[512,1024]{1,0:T(8,128)(2,1)S(1)}, u32[]{:S(2)}, u32[]{:S(2)}) collective-permute-start(bf16[512,1024]{1,0:T(8,128)(2,1)S(1)} %copy-done.44), channel_id=1, source_target_pairs={{0,1},{1,0},{2,3},{3,2},{4,5},{5,4},{6,7},{7,6},{8,9},{9,8},{10,11... | collective-permute-start | bytes 3145736 | tf_op jit(solution)/shard_map/ppermute | solution.py:1121
  544.2 46.0 %collective-permute-start.54 = (bf16[512,1024]{1,0:T(8,128)(2,1)}, bf16[512,1024]{1,0:T(8,128)(2,1)}, u32[]{:S(2)}, u32[]{:S(2)}) collective-permute-start(bf16[512,1024]{1,0:T(8,128)(2,1)} %get-tuple-element.312.refs_9_), channel_id=1, source_target_pairs={{0,1},{1,0},{2,3},{3,2},{4,5},{5,4},{6,7},{7,6},{8,9},{9,8},{10,11... | collective-permute-start | bytes 3145736 | tf_op jit(solution)/shard_map/ppermute | solution.py:1121
  544.7 45.5 %collective-permute-start.50 = (bf16[640,1024]{1,0:T(8,128)(2,1)S(1)}, bf16[640,1024]{1,0:T(8,128)(2,1)S(1)}, u32[]{:S(2)}, u32[]{:S(2)}) collective-permute-start(bf16[640,1024]{1,0:T(8,128)(2,1)S(1)} %copy-done.21), channel_id=1, source_target_pairs={{0,4},{4,0},{8,12},{12,8},{16,20},{20,16},{24,28},{28,24},{1,5},{5... | collective-permute-start | bytes 3932168 | tf_op jit(solution)/shard_map/ppermute | solution.py:1121
  589.5 28.5 %collective-permute-start.55 = (bf16[512,1024]{1,0:T(8,128)(2,1)}, bf16[512,1024]{1,0:T(8,128)(2,1)}, u32[]{:S(2)}, u32[]{:S(2)}) collective-permute-start(bf16[512,1024]{1,0:T(8,128)(2,1)} %get-tuple-element.314.refs_10_), channel_id=1, source_target_pairs={{0,1},{1,0},{2,3},{3,2},{4,5},{5,4},{6,7},{7,6},{8,9},{9,8},{10,11... | collective-permute-start | bytes 3145736 | tf_op jit(solution)/shard_map/ppermute | solution.py:1121
  589.6 60.0 %collective-permute-start.52 = (bf16[512,1024]{1,0:T(8,128)(2,1)}, bf16[512,1024]{1,0:T(8,128)(2,1)}, u32[]{:S(2)}, u32[]{:S(2)}) collective-permute-start(bf16[512,1024]{1,0:T(8,128)(2,1)} %get-tuple-element.308.refs_7_), channel_id=1, source_target_pairs={{0,1},{1,0},{2,3},{3,2},{4,5},{5,4},{6,7},{7,6},{8,9},{9,8},{10,11... | collective-permute-start | bytes 3145736 | tf_op jit(solution)/shard_map/ppermute | solution.py:1121
  590.1 61.9 %collective-permute-start.53 = (bf16[512,1024]{1,0:T(8,128)(2,1)}, bf16[512,1024]{1,0:T(8,128)(2,1)}, u32[]{:S(2)}, u32[]{:S(2)}) collective-permute-start(bf16[512,1024]{1,0:T(8,128)(2,1)} %get-tuple-element.310.refs_8_), channel_id=1, source_target_pairs={{0,1},{1,0},{2,3},{3,2},{4,5},{5,4},{6,7},{7,6},{8,9},{9,8},{10,11... | collective-permute-start | bytes 3145736 | tf_op jit(solution)/shard_map/ppermute | solution.py:1121
  591.3 63.3 %collective-permute-start.58 = (bf16[256,1792]{1,0:T(8,128)(2,1)}, bf16[256,1792]{1,0:T(8,128)(2,1)}, u32[]{:S(2)}, u32[]{:S(2)}) collective-permute-start(bf16[256,1792]{1,0:T(8,128)(2,1)} %get-tuple-element.317.refs_1_), channel_id=1, source_target_pairs={{0,4},{4,0},{8,12},{12,8},{16,20},{20,16},{24,28},{28,24},{1,5},{5... | collective-permute-start | bytes 2752520 | tf_op jit(solution)/shard_map/ppermute | solution.py:1121
  612.1 44.4 %collective-permute-start.59 = (bf16[256,1792]{1,0:T(8,128)(2,1)}, bf16[256,1792]{1,0:T(8,128)(2,1)}, u32[]{:S(2)}, u32[]{:S(2)}) collective-permute-start(bf16[256,1792]{1,0:T(8,128)(2,1)} %collective-permute-done.57.refs_2_), channel_id=1, source_target_pairs={{0,4},{4,0},{8,12},{12,8},{16,20},{20,16},{24,28},{28,24},{1,5},{5... | collective-permute-start | bytes 2752520 | tf_op jit(solution)/shard_map/ppermute | solution.py:1121
  618.0 36.7 %collective-permute-start.56 = (bf16[320,1024]{1,0:T(8,128)(2,1)}, bf16[320,1024]{1,0:T(8,128)(2,1)}, u32[]{:S(2)}, u32[]{:S(2)}) collective-permute-start(bf16[320,1024]{1,0:T(8,128)(2,1)} %get-tuple-element.316), channel_id=1, source_target_pairs={{0,8},{4,12},{8,0},{12,4},{16,24},{20,28},{24,16},{28,20},{1,9},{5... | collective-permute-start | bytes 1966088 | tf_op jit(solution)/shard_map/ppermute | solution.py:1121
  654.6 31.3 %collective-permute-start.23 = (bf16[512,1024]{1,0:T(8,128)(2,1)}, bf16[512,1024]{1,0:T(8,128)(2,1)}, u32[]{:S(2)}, u32[]{:S(2)}) collective-permute-start(bf16[512,1024]{1,0:T(8,128)(2,1)} %get-tuple-element.222.refs_12_), channel_id=1, source_target_pairs={{0,1},{1,0},{2,3},{3,2},{4,5},{5,4},{6,7},{7,6},{8,9},{9,8},{10,11... | collective-permute-start | bytes 3145736 | tf_op jit(solution)/shard_map/ppermute | solution.py:1121
  675.7 61.2 %collective-permute-start.72 = (bf16[512,1024]{1,0:T(8,128)(2,1)}, bf16[512,1024]{1,0:T(8,128)(2,1)}, u32[]{:S(2)}, u32[]{:S(2)}) collective-permute-start(bf16[512,1024]{1,0:T(8,128)(2,1)} %get-tuple-element.340), channel_id=1, source_target_pairs={{0,2},{1,3},{2,0},{3,1},{4,6},{5,7},{6,4},{7,5},{8,10},{9,11},{10,... | collective-permute-start | bytes 3145736 | tf_op jit(solution)/shard_map/ppermute | solution.py:1121
  677.0 41.2 %collective-permute-start.68 = (bf16[320,1024]{1,0:T(8,128)(2,1)}, bf16[320,1024]{1,0:T(8,128)(2,1)}, u32[]{:S(2)}, u32[]{:S(2)}) collective-permute-start(bf16[320,1024]{1,0:T(8,128)(2,1)} %get-tuple-element.333.refs_1_), channel_id=1, source_target_pairs={{0,16},{4,20},{8,24},{12,28},{16,0},{20,4},{24,8},{28,12},{1,17},{... | collective-permute-start | bytes 1966088 | tf_op jit(solution)/shard_map/ppermute | solution.py:1121
  679.4 59.4 %collective-permute-start.73 = (bf16[512,1024]{1,0:T(8,128)(2,1)}, bf16[512,1024]{1,0:T(8,128)(2,1)}, u32[]{:S(2)}, u32[]{:S(2)}) collective-permute-start(bf16[512,1024]{1,0:T(8,128)(2,1)} %get-tuple-element.342), channel_id=1, source_target_pairs={{0,2},{1,3},{2,0},{3,1},{4,6},{5,7},{6,4},{7,5},{8,10},{9,11},{10,... | collective-permute-start | bytes 3145736 | tf_op jit(solution)/shard_map/ppermute | solution.py:1121
  685.9 42.4 %collective-permute-start.66 = (bf16[128,1792]{1,0:T(8,128)(2,1)}, bf16[128,1792]{1,0:T(8,128)(2,1)S(1)}, u32[]{:S(2)}, u32[]{:S(2)}) collective-permute-start(bf16[128,1792]{1,0:T(8,128)(2,1)} %get-tuple-element.330), channel_id=1, source_target_pairs={{0,8},{4,12},{8,0},{12,4},{16,24},{20,28},{24,16},{28,20},{1,9},{5... | collective-permute-start | bytes 1376264 | tf_op jit(solution)/shard_map/ppermute | solution.py:1121
  687.5 41.7 %collective-permute-start.67 = (bf16[128,1792]{1,0:T(8,128)(2,1)}, bf16[128,1792]{1,0:T(8,128)(2,1)S(1)}, u32[]{:S(2)}, u32[]{:S(2)}) collective-permute-start(bf16[128,1792]{1,0:T(8,128)(2,1)} %get-tuple-element.332), channel_id=1, source_target_pairs={{0,16},{4,20},{8,24},{12,28},{16,0},{20,4},{24,8},{28,12},{1,17},{... | collective-permute-start | bytes 1376264 | tf_op jit(solution)/shard_map/ppermute | solution.py:1121
  728.3 39.1 %collective-permute-start.63 = (bf16[512,1024]{1,0:T(8,128)(2,1)}, bf16[512,1024]{1,0:T(8,128)(2,1)S(1)}, u32[]{:S(2)}, u32[]{:S(2)}) collective-permute-start(bf16[512,1024]{1,0:T(8,128)(2,1)} %get-tuple-element.326), channel_id=1, source_target_pairs={{0,2},{1,3},{2,0},{3,1},{4,6},{5,7},{6,4},{7,5},{8,10},{9,11},{10,... | collective-permute-start | bytes 3145736 | tf_op jit(solution)/shard_map/ppermute | solution.py:1121
  729.2 46.9 %collective-permute-start.64 = (bf16[512,1024]{1,0:T(8,128)(2,1)}, bf16[512,1024]{1,0:T(8,128)(2,1)S(1)}, u32[]{:S(2)}, u32[]{:S(2)}) collective-permute-start(bf16[512,1024]{1,0:T(8,128)(2,1)} %get-tuple-element.328), channel_id=1, source_target_pairs={{0,2},{1,3},{2,0},{3,1},{4,6},{5,7},{6,4},{7,5},{8,10},{9,11},{10,... | collective-permute-start | bytes 3145736 | tf_op jit(solution)/shard_map/ppermute | solution.py:1121
  761.1 36.3 %collective-permute-start.84 = (bf16[320,1024]{1,0:T(8,128)(2,1)}, bf16[320,1024]{1,0:T(8,128)(2,1)}, u32[]{:S(2)}, u32[]{:S(2)}) collective-permute-start(bf16[320,1024]{1,0:T(8,128)(2,1)} %get-tuple-element.353.refs_1_), channel_id=1, source_target_pairs={{0,8},{4,12},{8,0},{12,4},{16,24},{20,28},{24,16},{28,20},{1,9},{5... | collective-permute-start | bytes 1966088 | tf_op jit(solution)/shard_map/ppermute | solution.py:1121
  761.2 37.1 %collective-permute-start.85 = (bf16[320,1024]{1,0:T(8,128)(2,1)}, bf16[320,1024]{1,0:T(8,128)(2,1)}, u32[]{:S(2)}, u32[]{:S(2)}) collective-permute-start(bf16[320,1024]{1,0:T(8,128)(2,1)} %get-tuple-element.353.refs_1_), channel_id=1, source_target_pairs={{0,4},{4,0},{8,12},{12,8},{16,20},{20,16},{24,28},{28,24},{1,5},{5... | collective-permute-start | bytes 1966088 | tf_op jit(solution)/shard_map/ppermute | solution.py:1121
  766.0 52.1 %collective-permute-start.75 = (f32[512,1024]{1,0:T(8,128)}, f32[512,1024]{1,0:T(8,128)}, u32[]{:S(2)}, u32[]{:S(2)}) collective-permute-start(f32[512,1024]{1,0:T(8,128)} %broadcast_select_fusion.3), channel_id=1, source_target_pairs={{0,1},{1,0},{2,3},{3,2},{4,5},{5,4},{6,7},{7,6},{8,9},{9,8},{10,11... | collective-permute-start | bytes 6291464 | tf_op jit(solution)/shard_map/ppermute | solution.py:1121
  797.5 39.8 %collective-permute-start.79 = (bf16[128,1792]{1,0:T(8,128)(2,1)}, bf16[128,1792]{1,0:T(8,128)(2,1)S(1)}, u32[]{:S(2)}, u32[]{:S(2)}) collective-permute-start(bf16[128,1792]{1,0:T(8,128)(2,1)} %get-tuple-element.350.refs_1_), channel_id=1, source_target_pairs={{0,4},{4,0},{8,12},{12,8},{16,20},{20,16},{24,28},{28,24},{1,5},{5... | collective-permute-start | bytes 1376264 | tf_op jit(solution)/shard_map/ppermute | solution.py:1121
  798.3 39.0 %collective-permute-start.82 = (bf16[128,1792]{1,0:T(8,128)(2,1)S(1)}, bf16[128,1792]{1,0:T(8,128)(2,1)S(1)}, u32[]{:S(2)}, u32[]{:S(2)}) collective-permute-start(bf16[128,1792]{1,0:T(8,128)(2,1)S(1)} %copy-done.75), channel_id=1, source_target_pairs={{0,8},{4,12},{8,0},{12,4},{16,24},{20,28},{24,16},{28,20},{1,9},{5... | collective-permute-start | bytes 1376264 | tf_op jit(solution)/shard_map/ppermute | solution.py:1121
  (138 other events, 1377.7 us)

commit v4 on v3

--- a/solution.py
+++ b/solution.py
@@ -1569,8 +1569,8 @@
     next(small_run)
     pending = [begin_reduce(one) for one in sums[last]]
     out_crossing = cross_reduce(*pending)
+    final.step()
     advance()
-    final.step()
     next(small_run)
     incoming = [one[0] for one in end_backward(0, list(enumerate(crossing)))]
     tokens_grad = to_placement(incoming, inner)

time: 862 us -> 861 us (level)
    unnamed x201 -> x207, local copies, waits for them, and re-layouts: 21.5 us -> 21.5 us
  transfers between devices with their start and end apart: 87 -> 87, of which waited for: 18 -> 21; matrix products, arithmetic and copies ran while one was open for 11% -> 10% of each run, Pallas kernels for 59% -> 59%
where the time goes in v4:
time: 861 us; the launch traced here: 852 us
  Pallas kernels  525 us (61%)
  waiting for transfers between devices  143 us (17%)
  starting transfers between devices  62.4 us (7%)
  local copies, waits for them, and re-layouts  50.8 us (6%)
  other arithmetic  41.4 us (5%)
  matrix products  20.2 us (2%)
    pallas_call x43, Pallas kernels, call(): pl.pallas_call(body, grid_spec=pltpu.PrefetchScalarGridSpec(num_scalar_pr...  525 us
    ppermute x87, waiting for transfers between devices, swapped(): return lax.ppermute(array, axis, [(i, i ^ distance) for i in range(size)])  143 us
    ppermute x87, starting transfers between devices, swapped(): return lax.ppermute(array, axis, [(i, i ^ distance) for i in range(size)])  62.4 us
    unnamed x207, local copies, waits for them, and re-layouts  21.5 us
  transfers between devices with their start and end apart: 87, of which 21 were waited for; matrix products, arithmetic and copies ran while one was open for 10% of the time, Pallas kernels for 59%

profile of v4, /device:TPU:0, one launch (start us, length us, event | category | flops | bytes accessed | tf_op | source)
XLA Modules:
  0.0 851.5 jit_solution(6754669808391199262)
XLA Ops:
  8.1 5.0 fusion.refs_5_.refs_13_.refs_11_
  17.9 5.1 convolution_add_fusion.refs_4_.refs_12_.refs_10_
  22.9 3.9 slice_bitcast_fusion.4
  29.5 6.6 fold_gains.2
  36.7 3.9 collective-permute-done.2.refs_0_
  53.0 32.1 %forward_layer.4 = (bf16[2048,1024]{1,0:T(8,128)(2,1)}, bf16[2048,768]{1,0:T(8,128)(2,1)}, bf16[2048,1280]{1,0:T(8,128)(2,1)}, bf16[2048,256]{1,0:T(8,128)(2,1)}...) custom-call(s32[2,4]{1,0:T(2,128)} %copy-done.84, ...), custom_call_target="tpu_custom_call" | custom-call | tf_op jit(solution)/shard_map/forward_layer/pallas_call | solution.py:678
  92.6 4.0 join_pair.6
  99.4 32.7 %forward_layer.5 = (bf16[2048,1024]{1,0:T(8,128)(2,1)}, bf16[2048,768]{1,0:T(8,128)(2,1)}, bf16[2048,1280]{1,0:T(8,128)(2,1)}, bf16[2048,256]{1,0:T(8,128)(2,1)}...) custom-call(s32[2,4]{1,0:T(2,128)} %copy-done.84, ...), custom_call_target="tpu_custom_call" | custom-call | tf_op jit(solution)/shard_map/forward_layer/pallas_call | solution.py:678
  140.1 4.1 join_pair.7
  150.1 6.9 fold_gains.3
  157.7 6.4 collective-permute-done.11
  165.2 20.5 %collective-permute-done.15.refs_1_ = bf16[512,1024]{1,0:T(8,128)(2,1)S(1)} collective-permute-done((bf16[512,1024]{1,0:T(8,128)(2,1)}, bf16[512,1024]{1,0:T(8,128)(2,1)S(1)}, u32[]{:S(2)}, u32[]{:S(2)}) %collective-permute-start.15) | collective-permute-done | bytes 1048608 | tf_op jit(solution)/shard_map/ppermute | solution.py:1121
  186.7 3.6 end_forward.4
  197.9 32.4 %forward_layer.6 = (bf16[2048,1024]{1,0:T(8,128)(2,1)}, bf16[2048,768]{1,0:T(8,128)(2,1)}, bf16[2048,1280]{1,0:T(8,128)(2,1)}, bf16[2048,256]{1,0:T(8,128)(2,1)}...) custom-call(s32[2,4]{1,0:T(2,128)} %copy-done.84, ...), custom_call_target="tpu_custom_call" | custom-call | tf_op jit(solution)/shard_map/forward_layer/pallas_call | solution.py:678
  236.1 32.1 %forward_layer.7 = (bf16[2048,1024]{1,0:T(8,128)(2,1)}, bf16[2048,768]{1,0:T(8,128)(2,1)}, bf16[2048,1280]{1,0:T(8,128)(2,1)}, bf16[2048,256]{1,0:T(8,128)(2,1)}...) custom-call(s32[2,4]{1,0:T(2,128)} %copy-done.84, ...), custom_call_target="tpu_custom_call" | custom-call | tf_op jit(solution)/shard_map/forward_layer/pallas_call | solution.py:678
  274.0 37.2 %backward_layer.4 = (bf16[2048,1792]{1,0:T(8,128)(2,1)}, f32[1,1792]{1,0:T(1,128)}, f32[2,256,256]{2,1,0:T(8,128)}, bf16[512,1024]{1,0:T(8,128)(2,1)}, bf16[512,...) custom-call(s32[2,4]{1,0:T(2,128)} %copy-done.84, ...), custom_call_target="tpu_custom_call" | custom-call | tf_op jit(solution)/shard_map/backward_layer/pallas_call | solution.py:678
  316.1 20.0 %out_weight_grad.2 = (bf16[1280,1024]{1,0:T(8,128)(2,1)}, f32[1,1]{1,0:T(1,128)}) custom-call(s32[1]{0:T(128)} %bitcast.refs_1_.refs_0_, bf16[2048,1280]{1,0:T(8,128)(2,1)} %get-tuple-element.234.refs_1_.refs_14_, bf16[2048,1280]{1,0:T(8,128)(2,1)} %get-tuple-element.227.refs_14_.refs_2_, bf16[512,1024]{1,0:T(8,128)(2,1)} %copy-done.4, ...), custom_call_target="tpu_custom_call" | custom-call | tf_op jit(solution)/shard_map/out_weight_grad/pallas_call | solution.py:678
  338.6 4.1 join_pair.8
  345.4 37.6 %backward_layer.5 = (bf16[2048,1792]{1,0:T(8,128)(2,1)}, f32[1,1792]{1,0:T(1,128)}, f32[2,256,256]{2,1,0:T(8,128)}, bf16[512,1024]{1,0:T(8,128)(2,1)}, bf16[512,...) custom-call(s32[2,4]{1,0:T(2,128)} %copy-done.84, ...), custom_call_target="tpu_custom_call" | custom-call | tf_op jit(solution)/shard_map/backward_layer/pallas_call | solution.py:678
  384.6 4.9 end_backward.3
  390.8 4.4 join_halves.12
  396.2 4.0 join_pair.9
  404.4 28.5 %in_weight_grad.2 = (bf16[1024,1792]{1,0:T(8,128)(2,1)}, f32[1024,128]{1,0:T(8,128)}, f32[1,1]{1,0:T(1,128)}) custom-call(bf16[2048,1024]{1,0:T(8,128)(2,1)} %get-tuple-element.257.refs_0_, bf16[2048,1024]{1,0:T(8,128)(2,1)} %get-tuple-element.258.refs_1_, bf16[2048,1792]{1,0:T(8,128)(2,1)} %get-tuple-element.259.refs_2_, ...), custom_call_target="tpu_custom_call" | custom-call | tf_op jit(solution)/shard_map/in_weight_grad/pallas_call | solution.py:678
  442.0 4.9 end_backward.4
  451.6 37.2 %backward_layer.6 = (bf16[2048,1792]{1,0:T(8,128)(2,1)}, f32[1,1792]{1,0:T(1,128)}, f32[2,256,256]{2,1,0:T(8,128)}, bf16[512,1024]{1,0:T(8,128)(2,1)}, bf16[512,...) custom-call(s32[2,4]{1,0:T(2,128)} %copy-done.84, ...), custom_call_target="tpu_custom_call" | custom-call | tf_op jit(solution)/shard_map/backward_layer/pallas_call | solution.py:678
  494.8 5.1 join_halves.15
  502.7 8.1 collective-permute-done.47.refs_2_
  513.0 20.1 %out_weight_grad.3 = (bf16[1280,1024]{1,0:T(8,128)(2,1)}, f32[1,1]{1,0:T(1,128)}) custom-call(s32[1]{0:T(128)} %bitcast.refs_1_.refs_0_, bf16[2048,1280]{1,0:T(8,128)(2,1)} %get-tuple-element.280.refs_1_.refs_14_, bf16[2048,1280]{1,0:T(8,128)(2,1)} %get-tuple-element.272.refs_14_.refs_2_, bf16[512,1024]{1,0:T(8,128)(2,1)} %get-tuple-element.270.refs_18_.refs_3_.refs_2_, ...), custom_call_target="tpu_custom_call" | custom-call | tf_op jit(solution)/shard_map/out_weight_grad/pallas_call | solution.py:678
  535.6 4.5 assemble.2
  545.1 37.5 %backward_layer.7 = (bf16[2048,1792]{1,0:T(8,128)(2,1)}, f32[1,1792]{1,0:T(1,128)}, f32[2,256,256]{2,1,0:T(8,128)}, bf16[512,1024]{1,0:T(8,128)(2,1)}, bf16[512,...) custom-call(s32[2,4]{1,0:T(2,128)} %copy-done.84, ...), custom_call_target="tpu_custom_call" | custom-call | tf_op jit(solution)/shard_map/backward_layer/pallas_call | solution.py:678
  592.0 20.1 %collective-permute-done.57.refs_2_ = bf16[256,1792]{1,0:T(8,128)(2,1)} collective-permute-done((bf16[256,1792]{1,0:T(8,128)(2,1)}, bf16[256,1792]{1,0:T(8,128)(2,1)}, u32[]{:S(2)}, u32[]{:S(2)}) %collective-permute-start.57) | collective-permute-done | bytes 917536 | tf_op jit(solution)/shard_map/ppermute | solution.py:1121
  613.5 4.4 join_halves.18
  620.9 28.4 %in_weight_grad.3 = (bf16[512,1792]{1,0:T(8,128)(2,1)}, bf16[512,1792]{1,0:T(8,128)(2,1)}, f32[1024,128]{1,0:T(8,128)}, f32[1,1]{1,0:T(1,128)}) custom-call(bf16[2048,1024]{1,0:T(8,128)(2,1)} %get-tuple-element.223.refs_0_, bf16[2048,1024]{1,0:T(8,128)(2,1)} %get-tuple-element.224.refs_1_, bf16[2048,1792]{1,0:T(8,128)(2,1)} %get-tuple-element.294.refs_2_, ...), custom_call_target="tpu_custom_call" | custom-call | tf_op jit(solution)/shard_map/in_weight_grad/pallas_call | solution.py:678
  658.1 4.9 assemble.3
  666.4 5.7 join_pair.10
  679.9 5.1 join_halves.20
  688.1 18.8 %collective-permute-done.67.refs_2_ = bf16[128,1792]{1,0:T(8,128)(2,1)} collective-permute-done((bf16[128,1792]{1,0:T(8,128)(2,1)}, bf16[128,1792]{1,0:T(8,128)(2,1)}, u32[]{:S(2)}, u32[]{:S(2)}) %collective-permute-start.67) | collective-permute-done | bytes 458784 | tf_op jit(solution)/shard_map/ppermute | solution.py:1121
  707.5 6.0 join_pair.11
  713.5 13.2 %collective-permute-done.68.refs_4_ = bf16[128,1792]{1,0:T(8,128)(2,1)S(1)} collective-permute-done((bf16[128,1792]{1,0:T(8,128)(2,1)}, bf16[128,1792]{1,0:T(8,128)(2,1)S(1)}, u32[]{:S(2)}, u32[]{:S(2)}) %collective-permute-start.68) | collective-permute-done | bytes 458784 | tf_op jit(solution)/shard_map/ppermute | solution.py:1121
  728.5 3.7 join_halves.21
  742.2 7.5 end_backward.5
  749.7 12.0 %collective-permute-done.70.refs_2_ = bf16[128,1792]{1,0:T(8,128)(2,1)S(1)} collective-permute-done((bf16[128,1792]{1,0:T(8,128)(2,1)}, bf16[128,1792]{1,0:T(8,128)(2,1)S(1)}, u32[]{:S(2)}, u32[]{:S(2)}) %collective-permute-start.70) | collective-permute-done | bytes 458784 | tf_op jit(solution)/shard_map/ppermute | solution.py:1121
  762.6 3.9 join_halves.23
  774.3 4.7 end_forward.5
  797.7 12.6 %collective-permute-done.78.refs_2_ = bf16[128,1792]{1,0:T(8,128)(2,1)} collective-permute-done((bf16[128,1792]{1,0:T(8,128)(2,1)}, bf16[128,1792]{1,0:T(8,128)(2,1)}, u32[]{:S(2)}, u32[]{:S(2)}) %collective-permute-start.78) | collective-permute-done | bytes 458784 | tf_op jit(solution)/shard_map/ppermute | solution.py:1121
  819.5 8.6 %collective-permute-done.86.refs_4_ = bf16[320,1024]{1,0:T(8,128)(2,1)S(1)} collective-permute-done((bf16[320,1024]{1,0:T(8,128)(2,1)}, bf16[320,1024]{1,0:T(8,128)(2,1)S(1)}, u32[]{:S(2)}, u32[]{:S(2)}) %collective-permute-start.86) | collective-permute-done | bytes 655392 | tf_op jit(solution)/shard_map/ppermute | solution.py:1121
  829.0 8.3 finish_out.1
  838.6 12.1 %finish_in.1 = (f32[2,1024,768]{2,1,0:T(8,128)}, f32[2,1024,1024]{2,1,0:T(8,128)}, f32[1,1]{1,0:T(1,128)}) custom-call(s32[3]{0:T(128)} %pad_add_fusion.2.refs_0_, bf16[128,1792]{1,0:T(8,128)(2,1)} %get-tuple-element.350.refs_1_, bf16[128,1792]{1,0:T(8,128)(2,1)} %collective-permute-done.78.refs_2_, bf16[128,1792]{1,0:T(8,128)(2,1)} %copy-done.77, ...), custom_call_target="tpu_custom_call" | custom-call | tf_op jit(solution)/shard_map/finish_in/pallas_call | solution.py:678
  (468 shorter events, 205.6 us)
Async XLA Ops:
  44.2 42.2 %collective-permute-start.8 = (bf16[512,1024]{1,0:T(8,128)(2,1)S(1)}, bf16[512,1024]{1,0:T(8,128)(2,1)S(1)}, u32[]{:S(2)}, u32[]{:S(2)}) collective-permute-start(bf16[512,1024]{1,0:T(8,128)(2,1)S(1)} %broadcast_add_fusion.9.refs_15_), channel_id=1, source_target_pairs={{0,2},{1,3},{2,0},{3,1},{4,6},{5,7},{6,4},{7,5},{8,10},{9,11},{10,... | collective-permute-start | bytes 3145736 | tf_op jit(solution)/shard_map/ppermute | solution.py:1121
  50.9 47.0 %collective-permute-start.7 = (bf16[512,1024]{1,0:T(8,128)(2,1)S(1)}, bf16[512,1024]{1,0:T(8,128)(2,1)S(1)}, u32[]{:S(2)}, u32[]{:S(2)}) collective-permute-start(bf16[512,1024]{1,0:T(8,128)(2,1)S(1)} %copy-done.2), channel_id=1, source_target_pairs={{0,1},{1,0},{2,3},{3,2},{4,5},{5,4},{6,7},{7,6},{8,9},{9,8},{10,11... | collective-permute-start | bytes 3145736 | tf_op jit(solution)/shard_map/ppermute | solution.py:1121
  96.6 36.7 %collective-permute-start.6 = (bf16[512,1024]{1,0:T(8,128)(2,1)}, bf16[512,1024]{1,0:T(8,128)(2,1)S(1)}, u32[]{:S(2)}, u32[]{:S(2)}) collective-permute-start(bf16[512,1024]{1,0:T(8,128)(2,1)} %get-tuple-element.195), channel_id=1, source_target_pairs={{0,2},{1,3},{2,0},{3,1},{4,6},{5,7},{6,4},{7,5},{8,10},{9,11},{10,... | collective-permute-start | bytes 3145736 | tf_op jit(solution)/shard_map/ppermute | solution.py:1121
  144.2 41.6 %collective-permute-start.15 = (bf16[512,1024]{1,0:T(8,128)(2,1)}, bf16[512,1024]{1,0:T(8,128)(2,1)S(1)}, u32[]{:S(2)}, u32[]{:S(2)}) collective-permute-start(bf16[512,1024]{1,0:T(8,128)(2,1)} %get-tuple-element.210), channel_id=1, source_target_pairs={{0,2},{1,3},{2,0},{3,1},{4,6},{5,7},{6,4},{7,5},{8,10},{9,11},{10,... | collective-permute-start | bytes 3145736 | tf_op jit(solution)/shard_map/ppermute | solution.py:1121
  146.6 48.5 %collective-permute-start.21 = (bf16[512,1024]{1,0:T(8,128)(2,1)}, bf16[512,1024]{1,0:T(8,128)(2,1)}, u32[]{:S(2)}, u32[]{:S(2)}) collective-permute-start(bf16[512,1024]{1,0:T(8,128)(2,1)} %constant_dynamic-slice_fusion.5), channel_id=1, source_target_pairs={{0,1},{1,0},{2,3},{3,2},{4,5},{5,4},{6,7},{7,6},{8,9},{9,8},{10,11... | collective-permute-start | bytes 3145736 | tf_op jit(solution)/shard_map/ppermute | solution.py:1121
  149.6 48.3 %collective-permute-start.10 = (bf16[512,1024]{1,0:T(8,128)(2,1)S(1)}, bf16[512,1024]{1,0:T(8,128)(2,1)}, u32[]{:S(2)}, u32[]{:S(2)}) collective-permute-start(bf16[512,1024]{1,0:T(8,128)(2,1)S(1)} %copy-done.7), channel_id=1, source_target_pairs={{0,1},{1,0},{2,3},{3,2},{4,5},{5,4},{6,7},{7,6},{8,9},{9,8},{10,11... | collective-permute-start | bytes 3145736 | tf_op jit(solution)/shard_map/ppermute | solution.py:1121
  165.2 32.8 %collective-permute-start.14 = (bf16[512,1024]{1,0:T(8,128)(2,1)}, bf16[512,1024]{1,0:T(8,128)(2,1)}, u32[]{:S(2)}, u32[]{:S(2)}) collective-permute-start(bf16[512,1024]{1,0:T(8,128)(2,1)} %broadcast_add_fusion.7.refs_4_), channel_id=1, source_target_pairs={{0,1},{1,0},{2,3},{3,2},{4,5},{5,4},{6,7},{7,6},{8,9},{9,8},{10,11... | collective-permute-start | bytes 3145736 | tf_op jit(solution)/shard_map/ppermute | solution.py:1121
  190.4 40.6 %collective-permute-start.19 = (bf16[512,1024]{1,0:T(8,128)(2,1)}, bf16[512,1024]{1,0:T(8,128)(2,1)}, u32[]{:S(2)}, u32[]{:S(2)}) collective-permute-start(bf16[512,1024]{1,0:T(8,128)(2,1)} %get-tuple-element.211.refs_15_.refs_2_.refs_5_), channel_id=1, source_target_pairs={{0,2},{1,3},{2,0},{3,1},{4,6},{5,7},{6,4},{7,5},{8,10},{9,11},{10,... | collective-permute-start | bytes 3145736 | tf_op jit(solution)/shard_map/ppermute | solution.py:1121
  197.8 36.4 %collective-permute-start.18 = (bf16[512,1024]{1,0:T(8,128)(2,1)S(1)}, bf16[512,1024]{1,0:T(8,128)(2,1)}, u32[]{:S(2)}, u32[]{:S(2)}) collective-permute-start(bf16[512,1024]{1,0:T(8,128)(2,1)S(1)} %copy-done.8), channel_id=1, source_target_pairs={{0,1},{1,0},{2,3},{3,2},{4,5},{5,4},{6,7},{7,6},{8,9},{9,8},{10,11... | collective-permute-start | bytes 3145736 | tf_op jit(solution)/shard_map/ppermute | solution.py:1121
  233.0 36.0 %collective-permute-start.27 = (bf16[512,1024]{1,0:T(8,128)(2,1)S(1)}, bf16[512,1024]{1,0:T(8,128)(2,1)}, u32[]{:S(2)}, u32[]{:S(2)}) collective-permute-start(bf16[512,1024]{1,0:T(8,128)(2,1)S(1)} %broadcast_add_fusion.5.refs_15_), channel_id=1, source_target_pairs={{0,2},{1,3},{2,0},{3,1},{4,6},{5,7},{6,4},{7,5},{8,10},{9,11},{10,... | collective-permute-start | bytes 3145736 | tf_op jit(solution)/shard_map/ppermute | solution.py:1121
  234.3 37.8 %collective-permute-start.26 = (bf16[512,1024]{1,0:T(8,128)(2,1)S(1)}, bf16[512,1024]{1,0:T(8,128)(2,1)S(1)}, u32[]{:S(2)}, u32[]{:S(2)}) collective-permute-start(bf16[512,1024]{1,0:T(8,128)(2,1)S(1)} %get-tuple-element.379.refs_2_.refs_7_.refs_3_), channel_id=1, source_target_pairs={{0,1},{1,0},{2,3},{3,2},{4,5},{5,4},{6,7},{7,6},{8,9},{9,8},{10,11... | collective-permute-start | bytes 3145736 | tf_op jit(solution)/shard_map/ppermute | solution.py:1121
  270.8 41.1 %collective-permute-start.25 = (bf16[512,1024]{1,0:T(8,128)(2,1)S(1)}, bf16[512,1024]{1,0:T(8,128)(2,1)}, u32[]{:S(2)}, u32[]{:S(2)}) collective-permute-start(bf16[512,1024]{1,0:T(8,128)(2,1)S(1)} %broadcast_add_fusion.4.refs_18_), channel_id=1, source_target_pairs={{0,2},{1,3},{2,0},{3,1},{4,6},{5,7},{6,4},{7,5},{8,10},{9,11},{10,... | collective-permute-start | bytes 3145736 | tf_op jit(solution)/shard_map/ppermute | solution.py:1121
  272.1 42.1 %collective-permute-start.24 = (bf16[512,1024]{1,0:T(8,128)(2,1)S(1)}, bf16[512,1024]{1,0:T(8,128)(2,1)}, u32[]{:S(2)}, u32[]{:S(2)}) collective-permute-start(bf16[512,1024]{1,0:T(8,128)(2,1)S(1)} %get-tuple-element.369.refs_3_.refs_2_), channel_id=1, source_target_pairs={{0,1},{1,0},{2,3},{3,2},{4,5},{5,4},{6,7},{7,6},{8,9},{9,8},{10,11... | collective-permute-start | bytes 3145736 | tf_op jit(solution)/shard_map/ppermute | solution.py:1121
  342.7 41.0 %collective-permute-start.35 = (bf16[512,1024]{1,0:T(8,128)(2,1)}, bf16[512,1024]{1,0:T(8,128)(2,1)S(1)}, u32[]{:S(2)}, u32[]{:S(2)}) collective-permute-start(bf16[512,1024]{1,0:T(8,128)(2,1)} %get-tuple-element.250), channel_id=1, source_target_pairs={{0,2},{1,3},{2,0},{3,1},{4,6},{5,7},{6,4},{7,5},{8,10},{9,11},{10,... | collective-permute-start | bytes 3145736 | tf_op jit(solution)/shard_map/ppermute | solution.py:1121
  343.9 46.9 %collective-permute-start.34 = (bf16[640,1024]{1,0:T(8,128)(2,1)S(1)}, bf16[640,1024]{1,0:T(8,128)(2,1)}, u32[]{:S(2)}, u32[]{:S(2)}) collective-permute-start(bf16[640,1024]{1,0:T(8,128)(2,1)S(1)} %copy-done.22), channel_id=1, source_target_pairs={{0,4},{4,0},{8,12},{12,8},{16,20},{20,16},{24,28},{28,24},{1,5},{5... | collective-permute-start | bytes 3932168 | tf_op jit(solution)/shard_map/ppermute | solution.py:1121
  389.5 50.6 %collective-permute-start.41 = (bf16[512,1024]{1,0:T(8,128)(2,1)}, bf16[512,1024]{1,0:T(8,128)(2,1)}, u32[]{:S(2)}, u32[]{:S(2)}) collective-permute-start(bf16[512,1024]{1,0:T(8,128)(2,1)} %get-tuple-element.252.refs_3_.refs_2_.refs_7_), channel_id=1, source_target_pairs={{0,2},{1,3},{2,0},{3,1},{4,6},{5,7},{6,4},{7,5},{8,10},{9,11},{10,... | collective-permute-start | bytes 3145736 | tf_op jit(solution)/shard_map/ppermute | solution.py:1121
  400.3 41.7 %collective-permute-start.36 = (bf16[512,1024]{1,0:T(8,128)(2,1)}, bf16[512,1024]{1,0:T(8,128)(2,1)}, u32[]{:S(2)}, u32[]{:S(2)}) collective-permute-start(bf16[512,1024]{1,0:T(8,128)(2,1)} %get-tuple-element.256), channel_id=1, source_target_pairs={{0,2},{1,3},{2,0},{3,1},{4,6},{5,7},{6,4},{7,5},{8,10},{9,11},{10,... | collective-permute-start | bytes 3145736 | tf_op jit(solution)/shard_map/ppermute | solution.py:1121
  401.5 33.6 %collective-permute-start.37 = (bf16[320,1024]{1,0:T(8,128)(2,1)}, bf16[320,1024]{1,0:T(8,128)(2,1)S(1)}, u32[]{:S(2)}, u32[]{:S(2)}) collective-permute-start(bf16[320,1024]{1,0:T(8,128)(2,1)} %get-tuple-element.267), channel_id=1, source_target_pairs={{0,8},{4,12},{8,0},{12,4},{16,24},{20,28},{24,16},{28,20},{1,9},{5... | collective-permute-start | bytes 1966088 | tf_op jit(solution)/shard_map/ppermute | solution.py:1121
  404.4 45.9 %collective-permute-start.40 = (bf16[512,1024]{1,0:T(8,128)(2,1)S(1)}, bf16[512,1024]{1,0:T(8,128)(2,1)S(1)}, u32[]{:S(2)}, u32[]{:S(2)}) collective-permute-start(bf16[512,1024]{1,0:T(8,128)(2,1)S(1)} %copy-done.12), channel_id=1, source_target_pairs={{0,1},{1,0},{2,3},{3,2},{4,5},{5,4},{6,7},{7,6},{8,9},{9,8},{10,11... | collective-permute-start | bytes 3145736 | tf_op jit(solution)/shard_map/ppermute | solution.py:1121
  434.5 60.2 %collective-permute-start.44 = (bf16[512,1792]{1,0:T(8,128)(2,1)S(1)}, bf16[512,1792]{1,0:T(8,128)(2,1)}, u32[]{:S(2)}, u32[]{:S(2)}) collective-permute-start(bf16[512,1792]{1,0:T(8,128)(2,1)S(1)} %constant_dynamic-slice_fusion.3.refs_4_), channel_id=1, source_target_pairs={{0,4},{4,0},{8,12},{12,8},{16,20},{20,16},{24,28},{28,24},{1,5},{5... | collective-permute-start | bytes 5505032 | tf_op jit(solution)/shard_map/ppermute | solution.py:1121
  446.9 46.5 %collective-permute-start.39 = (bf16[512,1024]{1,0:T(8,128)(2,1)}, bf16[512,1024]{1,0:T(8,128)(2,1)}, u32[]{:S(2)}, u32[]{:S(2)}) collective-permute-start(bf16[512,1024]{1,0:T(8,128)(2,1)} %get-tuple-element.270.refs_18_.refs_3_.refs_2_), channel_id=1, source_target_pairs={{0,2},{1,3},{2,0},{3,1},{4,6},{5,7},{6,4},{7,5},{8,10},{9,11},{10,... | collective-permute-start | bytes 3145736 | tf_op jit(solution)/shard_map/ppermute | solution.py:1121
  447.7 41.8 %collective-permute-start.45 = (bf16[320,1024]{1,0:T(8,128)(2,1)S(1)}, bf16[320,1024]{1,0:T(8,128)(2,1)}, u32[]{:S(2)}, u32[]{:S(2)}) collective-permute-start(bf16[320,1024]{1,0:T(8,128)(2,1)S(1)} %copy-done.66), channel_id=1, source_target_pairs={{0,16},{4,20},{8,24},{12,28},{16,0},{20,4},{24,8},{28,12},{1,17},{... | collective-permute-start | bytes 1966088 | tf_op jit(solution)/shard_map/ppermute | solution.py:1121
  450.3 61.8 %collective-permute-start.38 = (bf16[512,1024]{1,0:T(8,128)(2,1)}, bf16[512,1024]{1,0:T(8,128)(2,1)}, u32[]{:S(2)}, u32[]{:S(2)}) collective-permute-start(bf16[512,1024]{1,0:T(8,128)(2,1)} %get-tuple-element.270.refs_18_.refs_3_.refs_2_), channel_id=1, source_target_pairs={{0,1},{1,0},{2,3},{3,2},{4,5},{5,4},{6,7},{7,6},{8,9},{9,8},{10,11... | collective-permute-start | bytes 3145736 | tf_op jit(solution)/shard_map/ppermute | solution.py:1121
  499.9 40.2 %collective-permute-start.46 = (bf16[256,1792]{1,0:T(8,128)(2,1)}, bf16[256,1792]{1,0:T(8,128)(2,1)}, u32[]{:S(2)}, u32[]{:S(2)}) collective-permute-start(bf16[256,1792]{1,0:T(8,128)(2,1)} %get-tuple-element.287), channel_id=1, source_target_pairs={{0,8},{4,12},{8,0},{12,4},{16,24},{20,28},{24,16},{28,20},{1,9},{5... | collective-permute-start | bytes 2752520 | tf_op jit(solution)/shard_map/ppermute | solution.py:1121
  501.5 34.1 %collective-permute-start.48 = (bf16[320,1024]{1,0:T(8,128)(2,1)}, bf16[320,1024]{1,0:T(8,128)(2,1)}, u32[]{:S(2)}, u32[]{:S(2)}) collective-permute-start(bf16[320,1024]{1,0:T(8,128)(2,1)} %get-tuple-element.288.refs_1_), channel_id=1, source_target_pairs={{0,4},{4,0},{8,12},{12,8},{16,20},{20,16},{24,28},{28,24},{1,5},{5... | collective-permute-start | bytes 1966088 | tf_op jit(solution)/shard_map/ppermute | solution.py:1121
  543.8 41.2 %collective-permute-start.51 = (bf16[256,1792]{1,0:T(8,128)(2,1)}, bf16[256,1792]{1,0:T(8,128)(2,1)S(1)}, u32[]{:S(2)}, u32[]{:S(2)}) collective-permute-start(bf16[256,1792]{1,0:T(8,128)(2,1)} %get-tuple-element.299.refs_1_), channel_id=1, source_target_pairs={{0,16},{4,20},{8,24},{12,28},{16,0},{20,4},{24,8},{28,12},{1,17},{... | collective-permute-start | bytes 2752520 | tf_op jit(solution)/shard_map/ppermute | solution.py:1121
  544.1 45.5 %collective-permute-start.16 = (bf16[512,1024]{1,0:T(8,128)(2,1)S(1)}, bf16[512,1024]{1,0:T(8,128)(2,1)S(1)}, u32[]{:S(2)}, u32[]{:S(2)}) collective-permute-start(bf16[512,1024]{1,0:T(8,128)(2,1)S(1)} %copy-done.44), channel_id=1, source_target_pairs={{0,1},{1,0},{2,3},{3,2},{4,5},{5,4},{6,7},{7,6},{8,9},{9,8},{10,11... | collective-permute-start | bytes 3145736 | tf_op jit(solution)/shard_map/ppermute | solution.py:1121
  544.1 46.1 %collective-permute-start.50 = (bf16[640,1024]{1,0:T(8,128)(2,1)S(1)}, bf16[640,1024]{1,0:T(8,128)(2,1)S(1)}, u32[]{:S(2)}, u32[]{:S(2)}) collective-permute-start(bf16[640,1024]{1,0:T(8,128)(2,1)S(1)} %copy-done.21), channel_id=1, source_target_pairs={{0,4},{4,0},{8,12},{12,8},{16,20},{20,16},{24,28},{28,24},{1,5},{5... | collective-permute-start | bytes 3932168 | tf_op jit(solution)/shard_map/ppermute | solution.py:1121
  545.0 45.2 %collective-permute-start.54 = (bf16[512,1024]{1,0:T(8,128)(2,1)}, bf16[512,1024]{1,0:T(8,128)(2,1)}, u32[]{:S(2)}, u32[]{:S(2)}) collective-permute-start(bf16[512,1024]{1,0:T(8,128)(2,1)} %get-tuple-element.312.refs_9_), channel_id=1, source_target_pairs={{0,1},{1,0},{2,3},{3,2},{4,5},{5,4},{6,7},{7,6},{8,9},{9,8},{10,11... | collective-permute-start | bytes 3145736 | tf_op jit(solution)/shard_map/ppermute | solution.py:1121
  589.6 28.4 %collective-permute-start.55 = (bf16[512,1024]{1,0:T(8,128)(2,1)}, bf16[512,1024]{1,0:T(8,128)(2,1)}, u32[]{:S(2)}, u32[]{:S(2)}) collective-permute-start(bf16[512,1024]{1,0:T(8,128)(2,1)} %get-tuple-element.314.refs_10_), channel_id=1, source_target_pairs={{0,1},{1,0},{2,3},{3,2},{4,5},{5,4},{6,7},{7,6},{8,9},{9,8},{10,11... | collective-permute-start | bytes 3145736 | tf_op jit(solution)/shard_map/ppermute | solution.py:1121
  589.7 59.7 %collective-permute-start.52 = (bf16[512,1024]{1,0:T(8,128)(2,1)}, bf16[512,1024]{1,0:T(8,128)(2,1)}, u32[]{:S(2)}, u32[]{:S(2)}) collective-permute-start(bf16[512,1024]{1,0:T(8,128)(2,1)} %get-tuple-element.308.refs_7_), channel_id=1, source_target_pairs={{0,1},{1,0},{2,3},{3,2},{4,5},{5,4},{6,7},{7,6},{8,9},{9,8},{10,11... | collective-permute-start | bytes 3145736 | tf_op jit(solution)/shard_map/ppermute | solution.py:1121
  590.1 62.3 %collective-permute-start.53 = (bf16[512,1024]{1,0:T(8,128)(2,1)}, bf16[512,1024]{1,0:T(8,128)(2,1)}, u32[]{:S(2)}, u32[]{:S(2)}) collective-permute-start(bf16[512,1024]{1,0:T(8,128)(2,1)} %get-tuple-element.310.refs_8_), channel_id=1, source_target_pairs={{0,1},{1,0},{2,3},{3,2},{4,5},{5,4},{6,7},{7,6},{8,9},{9,8},{10,11... | collective-permute-start | bytes 3145736 | tf_op jit(solution)/shard_map/ppermute | solution.py:1121
  591.3 61.5 %collective-permute-start.58 = (bf16[256,1792]{1,0:T(8,128)(2,1)}, bf16[256,1792]{1,0:T(8,128)(2,1)}, u32[]{:S(2)}, u32[]{:S(2)}) collective-permute-start(bf16[256,1792]{1,0:T(8,128)(2,1)} %get-tuple-element.317.refs_1_), channel_id=1, source_target_pairs={{0,4},{4,0},{8,12},{12,8},{16,20},{20,16},{24,28},{28,24},{1,5},{5... | collective-permute-start | bytes 2752520 | tf_op jit(solution)/shard_map/ppermute | solution.py:1121
  612.1 42.6 %collective-permute-start.59 = (bf16[256,1792]{1,0:T(8,128)(2,1)}, bf16[256,1792]{1,0:T(8,128)(2,1)}, u32[]{:S(2)}, u32[]{:S(2)}) collective-permute-start(bf16[256,1792]{1,0:T(8,128)(2,1)} %collective-permute-done.57.refs_2_), channel_id=1, source_target_pairs={{0,4},{4,0},{8,12},{12,8},{16,20},{20,16},{24,28},{28,24},{1,5},{5... | collective-permute-start | bytes 2752520 | tf_op jit(solution)/shard_map/ppermute | solution.py:1121
  617.9 35.1 %collective-permute-start.56 = (bf16[320,1024]{1,0:T(8,128)(2,1)}, bf16[320,1024]{1,0:T(8,128)(2,1)}, u32[]{:S(2)}, u32[]{:S(2)}) collective-permute-start(bf16[320,1024]{1,0:T(8,128)(2,1)} %get-tuple-element.316), channel_id=1, source_target_pairs={{0,8},{4,12},{8,0},{12,4},{16,24},{20,28},{24,16},{28,20},{1,9},{5... | collective-permute-start | bytes 1966088 | tf_op jit(solution)/shard_map/ppermute | solution.py:1121
  652.8 32.2 %collective-permute-start.23 = (bf16[512,1024]{1,0:T(8,128)(2,1)}, bf16[512,1024]{1,0:T(8,128)(2,1)}, u32[]{:S(2)}, u32[]{:S(2)}) collective-permute-start(bf16[512,1024]{1,0:T(8,128)(2,1)} %get-tuple-element.222.refs_12_), channel_id=1, source_target_pairs={{0,1},{1,0},{2,3},{3,2},{4,5},{5,4},{6,7},{7,6},{8,9},{9,8},{10,11... | collective-permute-start | bytes 3145736 | tf_op jit(solution)/shard_map/ppermute | solution.py:1121
  672.1 64.4 %collective-permute-start.72 = (bf16[512,1024]{1,0:T(8,128)(2,1)}, bf16[512,1024]{1,0:T(8,128)(2,1)}, u32[]{:S(2)}, u32[]{:S(2)}) collective-permute-start(bf16[512,1024]{1,0:T(8,128)(2,1)} %get-tuple-element.340), channel_id=1, source_target_pairs={{0,2},{1,3},{2,0},{3,1},{4,6},{5,7},{6,4},{7,5},{8,10},{9,11},{10,... | collective-permute-start | bytes 3145736 | tf_op jit(solution)/shard_map/ppermute | solution.py:1121
  675.7 56.5 %collective-permute-start.66 = (bf16[320,1024]{1,0:T(8,128)(2,1)}, bf16[320,1024]{1,0:T(8,128)(2,1)S(1)}, u32[]{:S(2)}, u32[]{:S(2)}) collective-permute-start(bf16[320,1024]{1,0:T(8,128)(2,1)} %get-tuple-element.329.refs_1_), channel_id=1, source_target_pairs={{0,16},{4,20},{8,24},{12,28},{16,0},{20,4},{24,8},{28,12},{1,17},{... | collective-permute-start | bytes 1966088 | tf_op jit(solution)/shard_map/ppermute | solution.py:1121
  677.8 60.8 %collective-permute-start.73 = (bf16[512,1024]{1,0:T(8,128)(2,1)}, bf16[512,1024]{1,0:T(8,128)(2,1)S(1)}, u32[]{:S(2)}, u32[]{:S(2)}) collective-permute-start(bf16[512,1024]{1,0:T(8,128)(2,1)} %get-tuple-element.342), channel_id=1, source_target_pairs={{0,2},{1,3},{2,0},{3,1},{4,6},{5,7},{6,4},{7,5},{8,10},{9,11},{10,... | collective-permute-start | bytes 3145736 | tf_op jit(solution)/shard_map/ppermute | solution.py:1121
  685.5 41.3 %collective-permute-start.68 = (bf16[128,1792]{1,0:T(8,128)(2,1)}, bf16[128,1792]{1,0:T(8,128)(2,1)S(1)}, u32[]{:S(2)}, u32[]{:S(2)}) collective-permute-start(bf16[128,1792]{1,0:T(8,128)(2,1)} %get-tuple-element.333), channel_id=1, source_target_pairs={{0,16},{4,20},{8,24},{12,28},{16,0},{20,4},{24,8},{28,12},{1,17},{... | collective-permute-start | bytes 1376264 | tf_op jit(solution)/shard_map/ppermute | solution.py:1121
  706.9 29.6 %collective-permute-start.65 = (f32[12,1792]{1,0:T(8,128)S(1)}, f32[12,1792]{1,0:T(8,128)S(1)}, u32[]{:S(2)}, u32[]{:S(2)}) collective-permute-start(f32[12,1792]{1,0:T(8,128)S(1)} %get-tuple-element.364.refs_8_), channel_id=1, source_target_pairs={{0,8},{4,12},{8,0},{12,4},{16,24},{20,28},{24,16},{28,20},{1,9},{5... | collective-permute-start | bytes 258056 | tf_op jit(solution)/shard_map/ppermute | solution.py:1121
  726.8 44.5 %collective-permute-start.63 = (bf16[512,1024]{1,0:T(8,128)(2,1)}, bf16[512,1024]{1,0:T(8,128)(2,1)S(1)}, u32[]{:S(2)}, u32[]{:S(2)}) collective-permute-start(bf16[512,1024]{1,0:T(8,128)(2,1)} %get-tuple-element.326), channel_id=1, source_target_pairs={{0,2},{1,3},{2,0},{3,1},{4,6},{5,7},{6,4},{7,5},{8,10},{9,11},{10,... | collective-permute-start | bytes 3145736 | tf_op jit(solution)/shard_map/ppermute | solution.py:1121
  732.3 41.0 %collective-permute-start.64 = (bf16[512,1024]{1,0:T(8,128)(2,1)}, bf16[512,1024]{1,0:T(8,128)(2,1)S(1)}, u32[]{:S(2)}, u32[]{:S(2)}) collective-permute-start(bf16[512,1024]{1,0:T(8,128)(2,1)} %get-tuple-element.328), channel_id=1, source_target_pairs={{0,2},{1,3},{2,0},{3,1},{4,6},{5,7},{6,4},{7,5},{8,10},{9,11},{10,... | collective-permute-start | bytes 3145736 | tf_op jit(solution)/shard_map/ppermute | solution.py:1121
  761.7 35.2 %collective-permute-start.84 = (bf16[320,1024]{1,0:T(8,128)(2,1)}, bf16[320,1024]{1,0:T(8,128)(2,1)}, u32[]{:S(2)}, u32[]{:S(2)}) collective-permute-start(bf16[320,1024]{1,0:T(8,128)(2,1)} %get-tuple-element.353.refs_1_), channel_id=1, source_target_pairs={{0,8},{4,12},{8,0},{12,4},{16,24},{20,28},{24,16},{28,20},{1,9},{5... | collective-permute-start | bytes 1966088 | tf_op jit(solution)/shard_map/ppermute | solution.py:1121
  761.7 35.9 %collective-permute-start.85 = (bf16[320,1024]{1,0:T(8,128)(2,1)}, bf16[320,1024]{1,0:T(8,128)(2,1)}, u32[]{:S(2)}, u32[]{:S(2)}) collective-permute-start(bf16[320,1024]{1,0:T(8,128)(2,1)} %get-tuple-element.353.refs_1_), channel_id=1, source_target_pairs={{0,4},{4,0},{8,12},{12,8},{16,20},{20,16},{24,28},{28,24},{1,5},{5... | collective-permute-start | bytes 1966088 | tf_op jit(solution)/shard_map/ppermute | solution.py:1121
  771.3 43.3 %collective-permute-start.75 = (f32[512,1024]{1,0:T(8,128)}, f32[512,1024]{1,0:T(8,128)}, u32[]{:S(2)}, u32[]{:S(2)}) collective-permute-start(f32[512,1024]{1,0:T(8,128)} %broadcast_select_fusion.3), channel_id=1, source_target_pairs={{0,1},{1,0},{2,3},{3,2},{4,5},{5,4},{6,7},{7,6},{8,9},{9,8},{10,11... | collective-permute-start | bytes 6291464 | tf_op jit(solution)/shard_map/ppermute | solution.py:1121
  796.9 40.4 %collective-permute-start.79 = (bf16[128,1792]{1,0:T(8,128)(2,1)}, bf16[128,1792]{1,0:T(8,128)(2,1)S(1)}, u32[]{:S(2)}, u32[]{:S(2)}) collective-permute-start(bf16[128,1792]{1,0:T(8,128)(2,1)} %get-tuple-element.350.refs_1_), channel_id=1, source_target_pairs={{0,4},{4,0},{8,12},{12,8},{16,20},{20,16},{24,28},{28,24},{1,5},{5... | collective-permute-start | bytes 1376264 | tf_op jit(solution)/shard_map/ppermute | solution.py:1121
  797.6 39.7 %collective-permute-start.82 = (bf16[128,1792]{1,0:T(8,128)(2,1)S(1)}, bf16[128,1792]{1,0:T(8,128)(2,1)S(1)}, u32[]{:S(2)}, u32[]{:S(2)}) collective-permute-start(bf16[128,1792]{1,0:T(8,128)(2,1)S(1)} %copy-done.75), channel_id=1, source_target_pairs={{0,8},{4,12},{8,0},{12,4},{16,24},{20,28},{24,16},{28,20},{1,9},{5... | collective-permute-start | bytes 1376264 | tf_op jit(solution)/shard_map/ppermute | solution.py:1121
  (141 other events, 1354.0 us)
